TPU v7x, 32 devices: a whole 2x2x4 slice. The times are simulated.
32 devices in a mesh: gz: 8 (over z, core), xy: 4 (over y, x).
Axes of the slice: x: 2, y: 2, z: 4, core: 2. Of those that a mesh axis runs over, the one named last changes fastest.
Arguments:
- density: float32 [512, 32, 512], P('xy', 'gz'), may hold values from 0.5 to 2
- momentum: float32 [3, 512, 32, 512], P(None, 'xy', 'gz'), may hold values from -3 to 3
- magnetic: float32 [3, 512, 32, 512], P(None, 'xy', 'gz'), may hold values from -3 to 3
- arm_potential: float32 [512, 512], P('xy'), may hold values from -10 to 10
- sn_cells: int32 [32, 3], P(('gz', 'xy')), may hold values from 0 to 511, as said below
- sn_counts: int32 [32], P(('gz', 'xy')), may hold values from 0 to 3
Outputs:
- new_density: float32 [512, 32, 512], P('xy', 'gz')
- new_momentum: float32 [3, 512, 32, 512], P(None, 'xy', 'gz')
- new_magnetic: float32 [3, 512, 32, 512], P(None, 'xy', 'gz')
- density_modes: float32 [2, 32, 512, 512], P(None, 'gz', 'xy')
Inputs may be any that keep to these rules, and one draw needn't show every extreme that they name: `sn_cells`: row e is the centre of an event held by device e // 1 of the joined axes gz+xy (gz slowest); its x lies among that device's 128 x rows and its z among its 4 z planes. `sn_counts`: 0 marks an empty slot.
All inputs are finite; a program needn't handle non-finite values.
Results may differ from a plain program's by a relative error of at most 0.00023.
Values sent between devices are 32-bit elements; how exact they have to be, the bound alone decides.
No kernel may reach another device: no remote copies, remote signals or barrier semaphores. Data moves between devices by JAX's collectives and lax.ppermute only.
A program may use at most 384 MiB of HBM per device.

v0:
```python
import functools
import math

import jax
import jax.numpy as jnp
import ml_dtypes
import numpy as np
from jax import lax
from jax.experimental import pallas as pl
from jax.experimental.pallas import tpu as pltpu
from jax.sharding import PartitionSpec as P

NX = 512
RADIUS = 16
IMPULSE = 2.0 / 16
TIME_STEP = 0.1
DIFFUSION = 0.05
NEAR = 8.0 * TIME_STEP / 12.0
FAR = TIME_STEP / 12.0
VMEM = 56 * 1024 * 1024
PACK_COST = MODES_COST = (1e6, 1e5)
STATE_COST = DENSITY_COST = (1e6, 4e8)
MAIN_COST = (1e12, 4e9)


def pair(ref, *index):
    return jnp.concatenate([ref[(*index[:-1], 0, index[-1])], ref[(*index[:-1], 1, index[-1])]], axis=0)


def unpair(ref, value, *index):
    ref[(*index[:-1], 0, index[-1])] = value[:4]
    ref[(*index[:-1], 1, index[-1])] = value[4:]


def slots(shape):
    sub = lax.broadcasted_iota(jnp.int32, shape, len(shape) - 2)
    return jnp.where(sub >= 4, sub - 4, sub)


def turn(value, shift, axis):
    return pltpu.roll(value, shift % value.shape[axis], axis)


def gather_planes(values, plane):
    slot = slots(values[0].shape)
    out = turn(values[-1], len(values) - 1 - plane, 0)
    for c in reversed(range(len(values) - 1)):
        out = jnp.where(slot == c, turn(values[c], c - plane, 0), out)
    return out


def shared(rho, m, b):
    inv = 1.0 / rho
    return [x * inv for x in m], rho + 0.5 * (b[0] * b[0] + b[1] * b[1] + b[2] * b[2])


def fluxes(v, total, m, b, k):
    push = [m[i] * v[k] - b[i] * b[k] + (total if i == k else 0.0) for i in range(3)]
    turned = [None if i == k else v[k] * b[i] - b[k] * v[i] for i in range(3)]
    return push + turned


def first_kernel(cell_ref, count_ref, rho_a, mom_a, mag_a, pot_a, rho_z, mom_z, mag_z, pot_z, ev_ref, first_ref, last_ref):
    shape = (1, ev_ref.shape[2])
    lane = lax.broadcasted_iota(jnp.int32, shape, 1)
    row = jnp.zeros(shape, jnp.int32)
    for e in range(count_ref.shape[0]):
        for i in range(4):
            row = jnp.where(lane == 4 * e + i, cell_ref[e, i] if i < 3 else count_ref[e], row)

    def copy(d, _):
        ev_ref[d] = row
        return 0

    lax.fori_loop(0, ev_ref.shape[0], copy, 0)
    for ref, rho, mom, mag, pot, skip in (
        (first_ref, rho_a, mom_a, mag_a, pot_a, 0), (last_ref, rho_z, mom_z, mag_z, pot_z, pot_z.shape[0] - 2),
    ):
        for j in range(2):
            ref[0, j] = rho[0, j]
            for c in range(3):
                ref[1 + c, j] = mom[c, 0, j]
                ref[4 + c, j] = mag[c, 0, j]
            ref[7, j] = jnp.broadcast_to(pot[skip + j : skip + j + 1], ref.shape[2:])


def pack_kernel(rho_ref, mz_ref, bx_ref, after_ref, up_ref, down_ref):
    half = rho_ref.shape[1]

    def body(p, _):
        rho, mz, bx = pair(rho_ref, p), pair(mz_ref, 0, p), pair(bx_ref, 0, p)
        slot = slots(rho.shape)
        up = jnp.where(slot == 2, mz, gather_planes([rho, mz, mz, bx], 3))
        down = jnp.where(slot == 2, turn(mz, 1, 0), gather_planes([rho, mz, mz, bx], 0))
        up_ref[p] = up
        down_ref[p] = down
        return 0

    lax.fori_loop(0, half, body, 0)


def write_messages(up_ref, down_ref, k, g, state):
    lasts = None
    for j in range(4):
        r = 4 * g + j
        u = state(j)
        sub = lax.broadcasted_iota(jnp.int32, u[0].shape, 0)
        near = [u[1], u[2], u[5], u[6]]
        up_ref[k, r] = gather_planes(near, 3)
        down_ref[k, r] = gather_planes(near, 0)
        f = fluxes(*shared(u[0], u[1:4], u[4:7]), u[1:4], u[4:7], 2)
        up_ref[k, 8 + r] = gather_planes(f[:4], 2)
        down_ref[k, 8 + r] = gather_planes(f[:4], 1)
        lasts = lasts or [f[4], f[4]]
        for i, plane in enumerate((2, 1)):
            for h in range(2):
                moved = turn(f[4], 2 * j + h - 4 * h - plane, 0)
                lasts[i] = jnp.where(sub == 2 * j + h, moved, lasts[i])
    up_ref[k, 16 + g] = lasts[0]
    down_ref[k, 16 + g] = lasts[1]


def state_kernel(
    ev_ref, rho_ref, mom_ref, mag_ref, pot_ref, before_ref, after_ref, rho_l, mom_l, mag_l, pot_l,
    rho_h, mom_h, mag_h, pot_h, u_out, edge_out, sb_out, sa_out, up_ref, down_ref, s_ref, sb_ref, sa_ref, *,
    depth, count, per_device,
):
    half, ny = s_ref.shape[1] - 4, s_ref.shape[3]
    step_id = pl.program_id(0)

    @pl.when(step_id == 0)
    def _():
        deposit(ev_ref, s_ref, sb_ref, sa_ref, depth, per_device)
        pieces = lambda rho, mom, mag, pot, j: (
            [rho[0, j]] + [mom[c, 0, j] for c in range(3)] + [mag[c, 0, j] for c in range(3)]
            + [jnp.broadcast_to(pot, (4, ny))]
        )
        for j in range(2):
            low = pieces(rho_l, mom_l, mag_l, pot_l[0, 6 + j : 7 + j], j)
            high = pieces(rho_h, mom_h, mag_h, pot_h[0, j : j + 1], j)
            for f in range(8):
                left = jnp.concatenate([before_ref[f, j], low[f]], axis=0)
                right = jnp.concatenate([high[f], after_ref[f, j]], axis=0)
                edge_out[f, j] = left + s_ref[f, j] if f < 4 else left
                edge_out[f, 2 + j] = right + s_ref[f, half + 2 + j] if f < 4 else right

    start = step_id * 8

    def body(g, send):
        def state(j):
            r = 4 * g + j
            q = start + r + 2
            sb_out[r] = sb_ref[q]
            sa_out[r] = sa_ref[q]
            u = [pair(rho_ref, r) + s_ref[0, q]]
            u += [pair(mom_ref, c, r) + s_ref[1 + c, q] for c in range(3)]
            u += [pair(mag_ref, c, r) for c in range(3)]
            for f in range(7):
                u_out[f, r] = u[f]
            rows = [jnp.broadcast_to(pot_ref[h, pl.ds(r, 1), :], (4, ny)) for h in range(2)]
            u_out[7, r] = jnp.concatenate(rows, axis=0)
            return u

        if send:
            write_messages(up_ref, down_ref, 0, g, state)
        else:
            for j in range(4):
                state(j)
        return 0

    @pl.when(step_id < count)
    def _():
        lax.fori_loop(0, 2, lambda g, _: body(g, True), 0)

    @pl.when(step_id >= count)
    def _():
        lax.fori_loop(0, 2, lambda g, _: body(g, False), 0)


def deposit(ev_ref, s_ref, sb_ref, sa_ref, depth, per_device):
    half, ny = s_ref.shape[1] - 4, s_ref.shape[3]
    rows, events = 2 * half, ev_ref.shape[0] * per_device
    row_start, plane_start = lax.axis_index("xy") * rows, lax.axis_index("gz") * 4
    s_ref[...] = jnp.zeros_like(s_ref)
    sb_ref[...] = jnp.zeros_like(sb_ref)
    sa_ref[...] = jnp.zeros_like(sa_ref)

    shape = (4, 8, 128)
    slot = slots(shape)
    sub = lax.broadcasted_iota(jnp.int32, shape, 1)
    step = lax.broadcasted_iota(jnp.int32, shape, 0)
    lane = lax.broadcasted_iota(jnp.int32, shape, 2)

    def wrapped(distance, size):
        distance = jnp.where(distance >= size // 2, distance - size, distance)
        return jnp.where(distance < -(size // 2), distance + size, distance)

    def event(e, _):
        device, slot_id = (e, 0) if per_device == 1 else (lax.div(e, per_device), lax.rem(e, per_device))
        row, col, plane, count = (ev_ref[device, 0, 4 * slot_id + i] for i in range(4))
        rel = wrapped(row - row_start - half, NX)
        rel = rel + half

        @pl.when((count > 0) & (rel > -2 - RADIUS) & (rel < rows + 2 + RADIUS))
        def _():
            base = plane_start - plane
            dz = wrapped(slot + base, depth).astype(jnp.float32)
            dzb = wrapped(jnp.where(slot == 2, -2, -1) + base, depth).astype(jnp.float32)
            dza = wrapped(jnp.where(slot == 2, 5, 4) + base, depth).astype(jnp.float32)
            share = lambda d: jnp.where(slot == 0, 1.0, jnp.where(slot == 3, 0.0, IMPULSE * d))
            first = jnp.bitwise_and(col - RADIUS, ny - 1) // 128
            second = jnp.bitwise_and(col + RADIUS - 1, ny - 1) // 128

            def tile(t, _):
                index = jnp.where(t == 0, first, second)
                lanes = pl.ds(pl.multiple_of(index * 128, 128), 128)
                dy = wrapped(lane + index * 128 - col, ny).astype(jnp.float32)
                dy2 = dy * dy
                for h in range(2):
                    weight = jnp.where((sub >= 4) == (h == 1), count, 0).astype(jnp.float32)
                    low = jnp.clip(rel - RADIUS + 1 - h * half + 2, 0, half + 4) // 4
                    high = (jnp.clip(rel + RADIUS - 1 - h * half + 2, -1, half + 3) + 4) // 4

                    def chunk(n, _):
                        q = pl.ds(n * 4, 4)
                        dx = (step + (n * 4 - 2 + h * half - rel)).astype(jnp.float32)
                        flat = dx * dx + dy2
                        size = lambda d: jnp.maximum(1.0 - (flat + d * d) * (1.0 / (RADIUS * RADIUS)), 0.0) * weight
                        w = size(dz)
                        s_ref[0, q, :, lanes] += w
                        w = w * IMPULSE
                        s_ref[1, q, :, lanes] += w * dx
                        s_ref[2, q, :, lanes] += w * dy
                        s_ref[3, q, :, lanes] += w * dz
                        sb_ref[q, :, lanes] += size(dzb) * share(dzb)
                        sa_ref[q, :, lanes] += size(dza) * share(dza)
                        return 0

                    lax.fori_loop(low, high, chunk, 0)
                return 0

            lax.fori_loop(0, jnp.where(first == second, 1, 2), tile, 0)

        return 0

    lax.fori_loop(0, events, event, 0)


def ends(below, above, c):
    return jnp.where(slots(below.shape) == 3, turn(above, 3 - c, 0), turn(below, -c, 0))


def along_y(f, b):
    near, far = NEAR * f, FAR * f
    return turn(b + near, 1, 1) + turn(b - near, -1, 1) + turn(far, -2, 1) - turn(far, 2, 1)


def along_z(f, b, near_f, near_u, far_f):
    slot = slots(b.shape)
    first, last = slot == 0, slot == 3
    outer = DIFFUSION * near_u
    if f is None:
        return jnp.where(first, outer, turn(b, 1, 0)) + jnp.where(last, outer, turn(b, -1, 0))
    near = NEAR * f
    outer += jnp.where(first, NEAR, -NEAR) * near_f
    out = jnp.where(first, outer, turn(b + near, 1, 0)) + jnp.where(last, outer, turn(b - near, -1, 0))
    beyond = jnp.where(slot == 1, turn(near_f, 1, 0), jnp.where(slot == 2, turn(near_f, -1, 0), far_f))
    return out + FAR * (jnp.where(slot <= 1, turn(f, -2, 0), beyond) - jnp.where(slot >= 2, turn(f, 2, 0), beyond))


def fetch(u_hbm, edge_hbm, u_ref, sem, first):
    fields, total = u_ref.shape[:2]
    half = u_hbm.shape[1]
    low, high = max(first - 2, 0), min(first + total - 2, half)
    copies = [pltpu.make_async_copy(u_hbm.at[:fields, low:high], u_ref.at[:, low - first + 2 : high - first + 2], sem.at[0])]
    if first == 0:
        copies.append(pltpu.make_async_copy(edge_hbm.at[:fields, 0:2], u_ref.at[:, 0:2], sem.at[1]))
    if first + total - 4 == half:
        copies.append(pltpu.make_async_copy(edge_hbm.at[:fields, 2:4], u_ref.at[:, total - 2 : total], sem.at[2]))
    for copy in copies:
        copy.start()
    for copy in copies:
        copy.wait()


def density_kernel(
    u_hbm, edge_hbm, below_ref, above_ref, sb_ref, sa_ref, order_ref, high_ref, low_ref, out_ref, wave_ref, *rest,
):
    *parcel, d_ref, u_ref, b_ref, sem = rest
    half = u_hbm.shape[1]
    field = None
    if parcel:
        field = pltpu.make_async_copy(u_hbm.at[4:7, half - b_ref.shape[1] :], b_ref, sem.at[3])
        field.start()
    fetch(u_hbm, edge_hbm, u_ref, sem, 0)
    half = below_ref.shape[0]
    rows = 2 * half

    def body(p, _):
        rho, my, mz = u_ref[0, p + 2], u_ref[2, p + 2], u_ref[3, p + 2]
        below, above = below_ref[p] + sb_ref[p], above_ref[p] + sa_ref[p]
        b = DIFFUSION * rho
        new = rho * (1.0 - 6.0 * DIFFUSION)
        new += DIFFUSION * (u_ref[0, p + 1] + u_ref[0, p + 3])
        new += NEAR * (u_ref[1, p + 1] - u_ref[1, p + 3]) + FAR * (u_ref[1, p + 4] - u_ref[1, p])
        new += along_y(my, b)
        new += along_z(mz, b, ends(below, above, 1), ends(below, above, 0), ends(below, above, 2))
        unpair(out_ref, new, p)
        d_ref[pl.ds(pl.multiple_of(p * 8, 8), 8), :] = new
        return 0

    lax.fori_loop(0, half, body, 0)
    d = d_ref[...]
    order = order_ref[...]
    dot = functools.partial(jnp.dot, preferred_element_type=jnp.float32)
    high = d.astype(jnp.bfloat16)
    low = (d - high.astype(jnp.float32)).astype(jnp.bfloat16)
    high = dot(order, high).astype(jnp.bfloat16)
    low = dot(order, low).astype(jnp.bfloat16)
    for part in range(2):
        c_high, c_low = high_ref[part], low_ref[part]
        wave = dot(high, c_high) + dot(high, c_low) + dot(low, c_high)
        peers, band = wave_ref.shape[0], wave_ref.shape[4]
        for j in range(peers):
            for z in range(4):
                wave_ref[j, part, z] = wave[z * rows : (z + 1) * rows, j * band : (j + 1) * band]
    if not parcel:
        return
    field.wait()
    first = half - b_ref.shape[1]

    def messages(n, _):
        r = n * 4
        state = lambda j: [u_ref[f, first + r + j + 2] for f in range(4)] + [b_ref[c, r + j] for c in range(3)]
        write_messages(*parcel, n // 2, n % 2, state)
        return 0

    lax.fori_loop(0, b_ref.shape[1] // 4, messages, 0)


def last_plane(below, above, j):
    sub = lax.broadcasted_iota(jnp.int32, below.shape, 0)
    out = turn(below, -2 * j, 0)
    out = jnp.where(sub == 3, turn(above, 3 - 2 * j, 0), out)
    out = jnp.where(sub == 4, turn(below, 3 - 2 * j, 0), out)
    return jnp.where(sub == 7, turn(above, 6 - 2 * j, 0), out)


def main_kernel(u_hbm, edge_hbm, ba_ref, aa_ref, sb_ref, sa_ref, from_below, from_above, *rest, first):
    mom_ref, mag_ref, u_ref, f_ref, sem = rest[-5:]
    chunk, total = ba_ref.shape[0], u_ref.shape[1]
    start = pl.program_id(0) * chunk
    kept = (0, 1, 2, 4, 5)

    @pl.when(pl.program_id(0) == 0)
    def _():
        fetch(u_hbm, edge_hbm, u_ref, sem, first)

        def fx(q, _):
            u = [u_ref[f, q] for f in range(7)]
            f = fluxes(*shared(u[0], u[1:4], u[4:7]), u[1:4], u[4:7], 0)
            for i, c in enumerate(kept):
                f_ref[i, q] = f[c]
            return 0

        lax.fori_loop(0, total, fx, 0)

    def row(r, g, j):
        q = start + r + 2
        u = [u_ref[f, q] for f in range(7)]
        v, pressure = shared(u[0], u[1:4], u[4:7])
        fy = fluxes(v, pressure, u[1:4], u[4:7], 1)
        fz = fluxes(v, pressure, u[1:4], u[4:7], 2)
        ba, aa = ba_ref[r] + sb_ref[r], aa_ref[r] + sa_ref[r]
        bn, an, bf, af = from_below[0, r], from_above[0, r], from_below[0, 8 + r], from_above[0, 8 + r]
        hm = [ends(bn, an, 0), ends(bn, an, 1), ends(ba, aa, 1)]
        hb = [ends(ba, aa, 3), ends(bn, an, 2), ends(bn, an, 3)]
        fh = fluxes(*shared(ends(ba, aa, 0), hm, hb), hm, hb, 2)
        halo = hm + hb
        far = [ends(bf, af, c) for c in range(4)] + [last_plane(from_below[0, 16 + g], from_above[0, 16 + g], j), None]
        for c in range(6):
            field = u[c + 1]
            new = field * (1.0 - 6.0 * DIFFUSION)
            new += DIFFUSION * (u_ref[c + 1, q - 1] + u_ref[c + 1, q + 1])
            if c in kept:
                i = kept.index(c)
                new += NEAR * (f_ref[i, q - 1] - f_ref[i, q + 1]) + FAR * (f_ref[i, q + 2] - f_ref[i, q - 2])
            b = DIFFUSION * field
            if fy[c] is None:
                new += turn(b, 1, 1) + turn(b, -1, 1)
            else:
                new += along_y(fy[c], b)
            new += along_z(fz[c], b, fh[c], halo[c], far[c])
            if c == 0:
                slope = NEAR * (u_ref[7, q - 1] - u_ref[7, q + 1]) + FAR * (u_ref[7, q + 2] - u_ref[7, q - 2])
                new += u[0] * slope
            if c == 1:
                potential = u_ref[7, q]
                slope = NEAR * (turn(potential, 1, 1) - turn(potential, -1, 1))
                new += u[0] * (slope + FAR * (turn(potential, -2, 1) - turn(potential, 2, 1)))
            if c < 3:
                unpair(mom_ref, new, c, r)
            else:
                unpair(mag_ref, new, c - 3, r)

    def body(g, _):
        for j in range(4):
            row(4 * g + j, g, j)
        return 0

    lax.fori_loop(0, chunk // 4, body, 0)


def modes_kernel(w_ref, ch_ref, cl_ref, sh_ref, sl_ref, out_ref, x_ref, *, turned):
    dot = functools.partial(jnp.dot, preferred_element_type=jnp.float32)
    planes, band, nx = out_ref.shape[1:]

    def split(part):
        if turned:
            x = jnp.concatenate([w_ref[part, z] for z in range(planes)], axis=0)
        else:
            width = w_ref.shape[3]
            for s in range(w_ref.shape[0]):
                for z in range(planes):
                    x_ref[z * band : (z + 1) * band, s * width : (s + 1) * width] = w_ref[s, part, z].T
            x = x_ref[...]
        high = x.astype(jnp.bfloat16)
        return high, (x - high.astype(jnp.float32)).astype(jnp.bfloat16)

    re, im = split(0), split(1)
    times = lambda x, h, l: dot(x[0], h[...]) + dot(x[0], l[...]) + dot(x[1], h[...])
    scale = 1.0 / math.sqrt(NX * nx)
    shape = (band, nx)
    ky = lax.broadcasted_iota(jnp.int32, shape, 0) + lax.axis_index("xy") * band
    kx = lax.broadcasted_iota(jnp.int32, shape, 1)
    keep = jnp.where((ky == 0) & (kx == 0), 0.0, scale)
    out_re = times(re, ch_ref, cl_ref) + times(im, sh_ref, sl_ref)
    out_im = times(im, ch_ref, cl_ref) - times(re, sh_ref, sl_ref)
    for z in range(planes):
        out_ref[0, z] = out_re[z * band : (z + 1) * band] * keep
        out_ref[1, z] = out_im[z * band : (z + 1) * band] * keep


def cost(flops, bytes_accessed):
    return pl.CostEstimate(flops=int(flops), bytes_accessed=int(bytes_accessed), transcendentals=0)


def tables(size):
    angle = (np.outer(np.arange(size), np.arange(size)) % size) * (2.0 * np.pi / size)
    result = []
    for table in (np.cos(angle), np.sin(angle)):
        high = table.astype(np.float32).astype(ml_dtypes.bfloat16)
        low = (table - high.astype(np.float64)).astype(np.float32).astype(ml_dtypes.bfloat16)
        result += [high, low]
    return result


def row_order(half):
    matrix = np.zeros((8 * half, 8 * half), np.float32)
    for z in range(4):
        for h in range(2):
            for p in range(half):
                matrix[(z * 2 + h) * half + p, p * 8 + h * 4 + z] = 1.0
    return matrix.astype(ml_dtypes.bfloat16)


def shift(block, axis, step):
    n = lax.axis_size(axis)
    return lax.ppermute(block, axis, [(i, (i + step) % n) for i in range(n)])


def on_device(density, momentum, magnetic, arm_potential, sn_cells, sn_counts):
    rows, planes, ny = density.shape
    half = rows // 2
    layers, across = lax.axis_size("gz"), lax.axis_size("xy")
    devices = layers * across
    tile_row, tile_plane = lax.axis_index("xy"), lax.axis_index("gz")
    field = rows * planes * ny
    f32 = jnp.float32
    shape = jax.ShapeDtypeStruct
    whole = pl.BlockSpec(memory_space=pltpu.VMEM)
    smem = pl.BlockSpec(memory_space=pltpu.SMEM)
    params = pltpu.CompilerParams(vmem_limit_bytes=VMEM)
    message = shape((2, half, planes, ny), f32)
    tile = shape((half, 8, ny), f32)
    steps = half // 8
    counts = (steps * 5 // 8, steps - steps * 5 // 8) if steps >= 2 else (steps,)

    slots_here = sn_cells.shape[0]
    rho = density.reshape(2, half, planes, ny)
    mom = momentum.reshape(3, 2, half, planes, ny)
    mag = magnetic.reshape(3, 2, half, planes, ny)

    pot = arm_potential.reshape(2, half, ny)
    edges = shape((8, 2, planes, ny), f32)
    mine = shape((devices, 1, -(-4 * slots_here // 128) * 128), jnp.int32)
    full = lambda s: pl.BlockSpec(s, lambda i: (0,) * len(s))
    mine, first_rows, last_rows = pl.pallas_call(
        first_kernel,
        grid=(1,),
        in_specs=[smem, smem] + [
            spec
            for h, k in ((0, 0), (1, half // 2 - 1))
            for spec in (
                pl.BlockSpec((1, 2, planes, ny), lambda i, h=h, k=k: (h, k, 0, 0)),
                pl.BlockSpec((3, 1, 2, planes, ny), lambda i, h=h, k=k: (0, h, k, 0, 0)),
                pl.BlockSpec((3, 1, 2, planes, ny), lambda i, h=h, k=k: (0, h, k, 0, 0)),
                pl.BlockSpec((8, ny), lambda i, h=h: (h * (rows // 8 - 1), 0)),
            )
        ],
        out_specs=[full(mine.shape)] + [full(edges.shape)] * 2,
        out_shape=[mine] + [edges] * 2,
        compiler_params=params,
        cost_estimate=cost(*PACK_COST),
        name="first",
    )(sn_cells, sn_counts, *[rho, mom, mag, arm_potential] * 2)
    events = lax.all_to_all(mine, ("gz", "xy"), split_axis=0, concat_axis=0, tiled=True)
    before, after = shift(last_rows, "xy", 1), shift(first_rows, "xy", -1)

    some = math.gcd(half, 16)
    up, down = pl.pallas_call(
        pack_kernel,
        grid=(half // some,),
        in_specs=[pl.BlockSpec((2, some, planes, ny), lambda i: (0, i, 0, 0))] + [
            pl.BlockSpec((1, 2, some, planes, ny), lambda i, f=f: (f, 0, i, 0, 0)) for f in (2, 0)
        ] + [pl.BlockSpec(memory_space=pl.ANY)],
        out_specs=[pl.BlockSpec((some, 8, ny), lambda i: (i, 0, 0))] * 2,
        out_shape=[tile] * 2,
        compiler_params=params,
        cost_estimate=cost(*PACK_COST),
        name="pack",
    )(rho, mom, mag, mine)
    below_a, above_a = shift(up, "gz", 1), shift(down, "gz", -1)

    parcels = [shape((n, 18, 8, ny), f32) for n in counts]
    side = pltpu.VMEM((half + 4, 8, ny), f32)
    begins = [sum(counts[:i]) for i in range(len(counts))]
    parcel = pl.BlockSpec((1, 18, 8, ny), lambda i: (jnp.minimum(i, counts[0] - 1), 0, 0, 0))
    eight = pl.BlockSpec((8, 8, ny), lambda i: (i, 0, 0))
    middle = [
        spec
        for h, k in ((0, steps - 1), (1, 0))
        for spec in (
            pl.BlockSpec((1, 2, planes, ny), lambda i, h=h, k=k: (h, k * 4 + 3 * (1 - h), 0, 0)),
            pl.BlockSpec((3, 1, 2, planes, ny), lambda i, h=h, k=k: (0, h, k * 4 + 3 * (1 - h), 0, 0)),
            pl.BlockSpec((3, 1, 2, planes, ny), lambda i, h=h, k=k: (0, h, k * 4 + 3 * (1 - h), 0, 0)),
            pl.BlockSpec((1, 8, ny), lambda i, h=h, k=k: (h, k, 0)),
        )
    ]
    rows_of = lambda n: pl.BlockSpec((n, 2, 8, planes, ny), lambda i: (0, 0, i, 0, 0))
    state, edge, sb, sa, up_0, down_0 = pl.pallas_call(
        functools.partial(state_kernel, depth=planes * layers, count=counts[0], per_device=slots_here),
        grid=(steps,),
        in_specs=[
            smem, pl.BlockSpec((2, 8, planes, ny), lambda i: (0, i, 0, 0)), rows_of(3), rows_of(3),
            pl.BlockSpec((2, 8, ny), lambda i: (0, i, 0)), full(edges.shape), full(edges.shape),
        ] + middle,
        out_specs=[pl.BlockSpec((8, 8, 8, ny), lambda i: (0, i, 0, 0)), full((8, 4, 8, ny)), eight, eight, parcel, parcel],
        out_shape=[shape((8, half, 8, ny), f32), shape((8, 4, 8, ny), f32), tile, tile, parcels[0], parcels[0]],
        scratch_shapes=[pltpu.VMEM((4, half + 4, 8, ny), f32), side, side],
        compiler_params=params,
        cost_estimate=cost(*STATE_COST),
        name="state",
    )(events, rho, mom, mag, pot, before, after, *[rho, mom, mag, pot] * 2)
    parcels_below, parcels_above = [shift(up_0, "gz", 1)], [shift(down_0, "gz", -1)]

    cos_high, cos_low, sin_high, sin_low = tables(ny)
    band = ny // across
    turned = band % 128 != 0 or rows % 128 != 0
    hbm = pl.BlockSpec(memory_space=pl.ANY)
    copies = pltpu.SemaphoreType.DMA((3,))
    more = parcels[1:] * 2
    new_density, wave, *messages = pl.pallas_call(
        density_kernel,
        in_specs=[hbm, hbm] + [whole] * 7,
        out_specs=[whole] * (2 + len(more)),
        out_shape=[message, shape((across, 2, planes, rows, band), f32), *more],
        scratch_shapes=[
            pltpu.VMEM((8 * half, ny), f32), pltpu.VMEM((4, half + 4, 8, ny), f32),
            pltpu.VMEM((3, counts[-1] * 8, 8, ny), f32), pltpu.SemaphoreType.DMA((4,)),
        ],
        compiler_params=params,
        cost_estimate=cost(*DENSITY_COST),
        name="density",
    )(
        state, edge, below_a, above_a, sb, sa, row_order(half),
        np.stack([cos_high, -sin_high]), np.stack([cos_low, -sin_low]),
    )

    if messages:
        parcels_below.append(shift(messages[0], "gz", 1))
        parcels_above.append(shift(messages[1], "gz", -1))
    portion = lax.all_to_all(wave, "xy", split_axis=0, concat_axis=0, tiled=True)
    if turned:
        portion = portion.transpose(1, 2, 4, 0, 3).reshape(2, planes, band, NX)
    modes = pl.pallas_call(
        functools.partial(modes_kernel, turned=turned),
        in_specs=[whole] * 5,
        out_specs=whole,
        out_shape=shape((2, planes, band, NX), f32),
        scratch_shapes=[pltpu.VMEM((planes * band, NX), f32)],
        compiler_params=params,
        cost_estimate=cost(*MODES_COST),
        name="modes",
    )(portion, *tables(NX))
    results = [shape((3, 2, half, planes, ny), f32)] * 2
    new = []
    for i, n in enumerate(counts):
        chunk, first = 8, begins[i] * 8
        here = pl.BlockSpec((chunk, 8, ny), lambda k, o=begins[i]: (o + k, 0, 0))
        parcel = pl.BlockSpec((1, 18, 8, ny), lambda k: (k, 0, 0, 0))
        three = pl.BlockSpec((3, 2, chunk, planes, ny), lambda k, o=begins[i]: (0, 0, o + k, 0, 0))
        below, above = parcels_below[i], parcels_above[i]
        extra = [*new] + [modes] * (i > 0 and i == len(counts) - 1)
        new = pl.pallas_call(
            functools.partial(main_kernel, first=first),
            grid=(n,),
            in_specs=[hbm, hbm] + [here] * 4 + [parcel] * 2 + [hbm] * len(extra),
            out_specs=[three, three],
            out_shape=results,
            scratch_shapes=[
                pltpu.VMEM((8, n * 8 + 4, 8, ny), f32), pltpu.VMEM((5, n * 8 + 4, 8, ny), f32), copies,
            ],
            input_output_aliases={8: 0, 9: 1} if new else {},
            compiler_params=pltpu.CompilerParams(vmem_limit_bytes=62 * 1024 * 1024),
            cost_estimate=cost(*MAIN_COST),
            name=f"main{i}",
        )(state, edge, below_a, above_a, sb, sa, below, above, *extra)
    new_mom, new_mag = new

    return (
        new_density.reshape(rows, planes, ny),
        new_mom.reshape(3, rows, planes, ny),
        new_mag.reshape(3, rows, planes, ny),
        modes,
    )


def solution(mesh):
    in_specs = (
        P("xy", "gz", None),
        P(None, "xy", "gz", None),
        P(None, "xy", "gz", None),
        P("xy", None),
        P(("gz", "xy"), None),
        P(("gz", "xy")),
    )
    out_specs = (
        P("xy", "gz", None),
        P(None, "xy", "gz", None),
        P(None, "xy", "gz", None),
        P(None, "gz", "xy", None),
    )
    return jax.shard_map(
        on_device, mesh=mesh, in_specs=in_specs, out_specs=out_specs, check_vma=False
    )
```

profile of v0, /device:TPU:0, one launch (start us, length us, event | category | flops | bytes accessed | tf_op | source)
XLA Modules:
  0.0 156.7 jit_solution(11716568928711741525)
XLA Ops:
  1.3 1.8 %first.1 = (s32[32,1,128]{2,1,0:T(1,128)}, f32[8,2,4,512]{3,2,1,0:T(4,128)}, f32[8,2,4,512]{3,2,1,0:T(4,128)}) custom-call(s32[1,3]{1,0:T(1,128)} %cell_ref.1, s32[1]{0:T(128)S(6)} %copy.21.count_ref, f32[2,64,4,512]{3,2,1,0:T(4,128)} %bitcast.19, f32[3,2,64,4,512]{4,3,2,1,0:T(4,128)} %bitcast.7, f32[3,2,64,4,512]{4,3,2,1,0:T(4,128)} %bitcast.13, ...), custom_call_target="tpu_custom_call" | custom-call | flops 1000000 | bytes 100000 | tf_op jit(solution)/shard_map/first/pallas_call | solution.py:498
  3.1 2.9 %collective-permute-start = (f32[8,2,4,512]{3,2,1,0:T(4,128)}, f32[8,2,4,512]{3,2,1,0:T(4,128)S(1)}, u32[]{:S(2)}, u32[]{:S(2)}) collective-permute-start(f32[8,2,4,512]{3,2,1,0:T(4,128)} %get-tuple-element.24), channel_id=1, source_target_pairs={{0,1},{1,2},{2,3},{3,0},{4,5},{5,6},{6,7},{7,4},{8,9},{9,10},{10,1... | collective-permute-start | bytes 393224 | tf_op jit(solution)/shard_map/ppermute | solution.py:469
  6.1 1.0 collective-permute-start.1
  7.0 12.7 %all_to_all.10.ev_ref = s32[32,1,128]{2,1,0:T(1,128)} all-to-all(s32[32,1,128]{2,1,0:T(1,128)} %get-tuple-element.23.after_ref), channel_id=1, replica_groups=mesh['gz'=8,'xy'=4] {'gz','xy'}, dimensions={0} | all-to-all | bytes 32768 | tf_op jit(solution)/shard_map/all_to_all | solution.py:517
  19.7 0.0 collective-permute-done.before_ref
  19.7 0.0 copy-start.2
  19.7 0.0 collective-permute-done.1.after_ref
  19.7 0.0 copy-start.3
  19.8 0.6 copy-done.2
  20.4 0.0 copy-done.3
  20.4 14.0 %state.1 = (f32[8,64,8,512]{3,2,1,0:T(8,128)}, f32[8,4,8,512]{3,2,1,0:T(8,128)}, f32[64,8,512]{2,1,0:T(8,128)}, f32[64,8,512]{2,1,0:T(8,128)}, f32[5,18,8,512]{3,2,1,0:T(8,128)}, /*index=5*/f32[5,18,8,512]{3,2,1,0:T(8,128)}) custom-call(s32[32,1,128]{2,1,0:T(1,128)} %all_to_all.10.ev_ref, f32[2,64,4,512]{3,2,1,0:T(4,128)} %bitcast.21, ...), custom_call_target="tpu_custom_call" | custom-call | flops 1000000 | bytes 400000000 | tf_op jit(solution)/shard_map/state/pallas_call | solution.py:551
  34.5 0.1 collective-permute-start.6
  34.5 3.5 %collective-permute-start.7 = (f32[5,18,8,512]{3,2,1,0:T(8,128)}, f32[5,18,8,512]{3,2,1,0:T(8,128)}, u32[]{:S(2)}, u32[]{:S(2)}) collective-permute-start(f32[5,18,8,512]{3,2,1,0:T(8,128)} %get-tuple-element.36), channel_id=1, source_target_pairs={{0,28},{4,0},{8,4},{12,8},{16,12},{20,16},{24,20},{28,24},{1,29},{... | collective-permute-start | bytes 4423688 | tf_op jit(solution)/shard_map/ppermute | solution.py:469
  38.1 4.3 %pack.1 = (f32[64,8,512]{2,1,0:T(8,128)}, f32[64,8,512]{2,1,0:T(8,128)}) custom-call(f32[2,64,4,512]{3,2,1,0:T(4,128)} %bitcast.24, f32[3,2,64,4,512]{4,3,2,1,0:T(4,128)} %bitcast.12, f32[3,2,64,4,512]{4,3,2,1,0:T(4,128)} %bitcast.18, s32[32,1,128]{2,1,0:T(1,128)} %get-tuple-element.23.after_ref), custom_call_target="tpu_custom_call" | custom-call | flops 1000000 | bytes 100000 | tf_op jit(solution)/shard_map/pack/pallas_call | solution.py:521
  42.4 0.0 collective-permute-start.2
  42.4 3.5 %collective-permute-start.3 = (f32[64,8,512]{2,1,0:T(8,128)}, f32[64,8,512]{2,1,0:T(8,128)S(1)}, u32[]{:S(2)}, u32[]{:S(2)}) collective-permute-start(f32[64,8,512]{2,1,0:T(8,128)} %get-tuple-element.29), channel_id=1, source_target_pairs={{0,28},{4,0},{8,4},{12,8},{16,12},{20,16},{24,20},{28,24},{1,29},{... | collective-permute-start | bytes 3145736 | tf_op jit(solution)/shard_map/ppermute | solution.py:469
  46.0 46.7 %collective-permute-done.2.below_ref.ba_ref = f32[64,8,512]{2,1,0:T(8,128)S(1)} collective-permute-done((f32[64,8,512]{2,1,0:T(8,128)}, f32[64,8,512]{2,1,0:T(8,128)S(1)}, u32[]{:S(2)}, u32[]{:S(2)}) %collective-permute-start.2) | collective-permute-done | bytes 1048608 | tf_op jit(solution)/shard_map/ppermute | solution.py:469
  92.7 0.0 collective-permute-done.3.above_ref.aa_ref
  92.7 1.0 copy-done
  93.6 0.3 copy-done.1
  94.0 16.7 %density.1 = (f32[2,64,4,512]{3,2,1,0:T(4,128)}, f32[4,2,4,128,128]{4,3,2,1,0:T(8,128)}, f32[3,18,8,512]{3,2,1,0:T(8,128)}, f32[3,18,8,512]{3,2,1,0:T(8,128)}) custom-call(f32[8,64,8,512]{3,2,1,0:T(8,128)} %get-tuple-element.26.u_hbm, f32[8,4,8,512]{3,2,1,0:T(8,128)} %get-tuple-element.27.edge_hbm, f32[64,8,512]{2,1,0:T(8,128)} %copy-done, ...), custom_call_target="tpu_custom_call" | custom-call | flops 1000000 | bytes 400000000 | tf_op jit(solution)/shard_map/density/pallas_call | solution.py:573
  110.7 4.5 %all-to-all-start.1 = ((f32[4,2,4,128,128]{4,3,2,1,0:T(8,128)}), f32[4,2,4,128,128]{4,3,2,1,0:T(8,128)}, u32[]{:S(2)}, u32[]{:S(2)}) async-start(f32[4,2,4,128,128]{4,3,2,1,0:T(8,128)} %get-tuple-element.39), calls=%async_computation.1 | async-start | bytes 4194304 | tf_op jit(solution)/shard_map/all_to_all | solution.py:593
  115.2 0.1 collective-permute-start.4
  115.2 3.5 %collective-permute-start.5 = (f32[3,18,8,512]{3,2,1,0:T(8,128)}, f32[3,18,8,512]{3,2,1,0:T(8,128)}, u32[]{:S(2)}, u32[]{:S(2)}) collective-permute-start(f32[3,18,8,512]{3,2,1,0:T(8,128)} %get-tuple-element.34), channel_id=1, source_target_pairs={{0,28},{4,0},{8,4},{12,8},{16,12},{20,16},{24,20},{28,24},{1,29},{... | collective-permute-start | bytes 2654216 | tf_op jit(solution)/shard_map/ppermute | solution.py:469
  118.8 0.0 collective-permute-done.6.from_below
  118.8 0.0 collective-permute-done.7.from_above
  118.8 14.3 %main0.1 = (f32[3,2,64,4,512]{4,3,2,1,0:T(4,128)}, f32[3,2,64,4,512]{4,3,2,1,0:T(4,128)}) custom-call(f32[8,64,8,512]{3,2,1,0:T(8,128)} %get-tuple-element.26.u_hbm, f32[8,4,8,512]{3,2,1,0:T(8,128)} %get-tuple-element.27.edge_hbm, f32[64,8,512]{2,1,0:T(8,128)} %copy-done, f32[64,8,512]{2,1,0:T(8,128)} %copy-done.1, f32[64,8,512]{2,1,0:T(8,128)} %get-tuple-element.30.sb_ref, ...), custom_call_target="tpu_custom_call" | custom-call | flops 999999995904 | bytes 4000000000 | tf_op jit(solution)/shard_map/main0/pallas_call | solution.py:615
  133.1 6.6 %all-to-all-done.1.w_ref = f32[4,2,4,128,128]{4,3,2,1,0:T(8,128)} async-done(((f32[4,2,4,128,128]{4,3,2,1,0:T(8,128)}), f32[4,2,4,128,128]{4,3,2,1,0:T(8,128)}, u32[]{:S(2)}, u32[]{:S(2)}) %all-to-all-start.1) | async-done | bytes 2097184 | tf_op jit(solution)/shard_map/all_to_all | solution.py:593
  139.7 7.0 %modes.1.rest_2_ = f32[2,4,128,512]{3,2,1,0:T(8,128)} custom-call(f32[4,2,4,128,128]{4,3,2,1,0:T(8,128)} %all-to-all-done.1.w_ref, bf16[512,512]{1,0:T(8,128)(2,1)} %constant.17.clone.ch_ref, bf16[512,512]{1,0:T(8,128)(2,1)} %constant.18.clone.cl_ref, bf16[512,512]{1,0:T(8,128)(2,1)} %constant.19.clone.sh_ref, bf16[512,512]{1,0:T(8,128)(2,1)} %constant.20.clone.sl_ref), custom_call_target="tpu_custom_call" | custom-call | flops 1000000 | bytes 100000 | tf_op jit(solution)/shard_map/modes/pallas_call | solution.py:596
  146.7 0.0 collective-permute-done.4.from_below
  146.7 0.0 collective-permute-done.5.from_above
  146.7 10.0 %main1.1 = (f32[3,2,64,4,512]{4,3,2,1,0:T(4,128)}, f32[3,2,64,4,512]{4,3,2,1,0:T(4,128)}) custom-call(f32[8,64,8,512]{3,2,1,0:T(8,128)} %get-tuple-element.26.u_hbm, f32[8,4,8,512]{3,2,1,0:T(8,128)} %get-tuple-element.27.edge_hbm, f32[64,8,512]{2,1,0:T(8,128)} %copy-done, f32[64,8,512]{2,1,0:T(8,128)} %copy-done.1, ...), custom_call_target="tpu_custom_call", output_to_operand_aliasing={{0}: (8, {}), {1}: (9, {})} | custom-call | flops 999999995904 | bytes 4000000000 | tf_op jit(solution)/shard_map/main1/pallas_call | solution.py:615
  (2 shorter events, 0.0 us)
Async XLA Ops:
  3.1 16.6 %collective-permute-start = (f32[8,2,4,512]{3,2,1,0:T(4,128)}, f32[8,2,4,512]{3,2,1,0:T(4,128)S(1)}, u32[]{:S(2)}, u32[]{:S(2)}) collective-permute-start(f32[8,2,4,512]{3,2,1,0:T(4,128)} %get-tuple-element.24), channel_id=1, source_target_pairs={{0,1},{1,2},{2,3},{3,0},{4,5},{5,6},{6,7},{7,4},{8,9},{9,10},{10,1... | collective-permute-start | bytes 393224 | tf_op jit(solution)/shard_map/ppermute | solution.py:469
  6.1 13.7 %collective-permute-start.1 = (f32[8,2,4,512]{3,2,1,0:T(4,128)}, f32[8,2,4,512]{3,2,1,0:T(4,128)S(1)}, u32[]{:S(2)}, u32[]{:S(2)}) collective-permute-start(f32[8,2,4,512]{3,2,1,0:T(4,128)} %get-tuple-element.25), channel_id=1, source_target_pairs={{0,3},{1,0},{2,1},{3,2},{4,7},{5,4},{6,5},{7,6},{8,11},{9,8},{10,9... | collective-permute-start | bytes 393224 | tf_op jit(solution)/shard_map/ppermute | solution.py:469
  19.7 0.7 copy-start.2
  19.7 0.7 copy-start.3
  34.5 84.3 %collective-permute-start.6 = (f32[5,18,8,512]{3,2,1,0:T(8,128)}, f32[5,18,8,512]{3,2,1,0:T(8,128)}, u32[]{:S(2)}, u32[]{:S(2)}) collective-permute-start(f32[5,18,8,512]{3,2,1,0:T(8,128)} %get-tuple-element.35), channel_id=1, source_target_pairs={{0,4},{4,8},{8,12},{12,16},{16,20},{20,24},{24,28},{28,0},{1,5},{5... | collective-permute-start | bytes 4423688 | tf_op jit(solution)/shard_map/ppermute | solution.py:469
  34.5 84.2 %collective-permute-start.7 = (f32[5,18,8,512]{3,2,1,0:T(8,128)}, f32[5,18,8,512]{3,2,1,0:T(8,128)}, u32[]{:S(2)}, u32[]{:S(2)}) collective-permute-start(f32[5,18,8,512]{3,2,1,0:T(8,128)} %get-tuple-element.36), channel_id=1, source_target_pairs={{0,28},{4,0},{8,4},{12,8},{16,12},{20,16},{24,20},{28,24},{1,29},{... | collective-permute-start | bytes 4423688 | tf_op jit(solution)/shard_map/ppermute | solution.py:469
  42.4 50.3 %collective-permute-start.2 = (f32[64,8,512]{2,1,0:T(8,128)}, f32[64,8,512]{2,1,0:T(8,128)S(1)}, u32[]{:S(2)}, u32[]{:S(2)}) collective-permute-start(f32[64,8,512]{2,1,0:T(8,128)} %get-tuple-element.28), channel_id=1, source_target_pairs={{0,4},{4,8},{8,12},{12,16},{16,20},{20,24},{24,28},{28,0},{1,5},{5... | collective-permute-start | bytes 3145736 | tf_op jit(solution)/shard_map/ppermute | solution.py:469
  42.4 50.3 %collective-permute-start.3 = (f32[64,8,512]{2,1,0:T(8,128)}, f32[64,8,512]{2,1,0:T(8,128)S(1)}, u32[]{:S(2)}, u32[]{:S(2)}) collective-permute-start(f32[64,8,512]{2,1,0:T(8,128)} %get-tuple-element.29), channel_id=1, source_target_pairs={{0,28},{4,0},{8,4},{12,8},{16,12},{20,16},{24,20},{28,24},{1,29},{... | collective-permute-start | bytes 3145736 | tf_op jit(solution)/shard_map/ppermute | solution.py:469
  92.7 1.0 copy-start
  92.7 1.3 copy-start.1
  110.7 29.0 %all-to-all-start.1 = ((f32[4,2,4,128,128]{4,3,2,1,0:T(8,128)}), f32[4,2,4,128,128]{4,3,2,1,0:T(8,128)}, u32[]{:S(2)}, u32[]{:S(2)}) async-start(f32[4,2,4,128,128]{4,3,2,1,0:T(8,128)} %get-tuple-element.39), calls=%async_computation.1 | async-start | bytes 4194304 | tf_op jit(solution)/shard_map/all_to_all | solution.py:593
  115.2 31.5 %collective-permute-start.4 = (f32[3,18,8,512]{3,2,1,0:T(8,128)}, f32[3,18,8,512]{3,2,1,0:T(8,128)}, u32[]{:S(2)}, u32[]{:S(2)}) collective-permute-start(f32[3,18,8,512]{3,2,1,0:T(8,128)} %get-tuple-element.33), channel_id=1, source_target_pairs={{0,4},{4,8},{8,12},{12,16},{16,20},{20,24},{24,28},{28,0},{1,5},{5... | collective-permute-start | bytes 2654216 | tf_op jit(solution)/shard_map/ppermute | solution.py:469
  115.2 31.4 %collective-permute-start.5 = (f32[3,18,8,512]{3,2,1,0:T(8,128)}, f32[3,18,8,512]{3,2,1,0:T(8,128)}, u32[]{:S(2)}, u32[]{:S(2)}) collective-permute-start(f32[3,18,8,512]{3,2,1,0:T(8,128)} %get-tuple-element.34), channel_id=1, source_target_pairs={{0,28},{4,0},{8,4},{12,8},{16,12},{20,16},{24,20},{28,24},{1,29},{... | collective-permute-start | bytes 2654216 | tf_op jit(solution)/shard_map/ppermute | solution.py:469
where the time goes:
time: 157 us
  Pallas kernels  68.2 us (43%)
  waiting for transfers between devices  53.3 us (34%)
  starting transfers between devices  19.1 us (12%)
  blocking collectives  12.7 us (8%)
  local copies, waits for them, and re-layouts  1.97 us (1%)
    ppermute x8, waiting for transfers between devices, shift(): return lax.ppermute(block, axis, [(i, (i + step) % n) for i in range(n)])  46.7 us
    pallas_call x2, Pallas kernels, on_device(): pl.pallas_call(functools.partial(main_kernel, first=first), grid=(n,), in...  24.3 us
    pallas_call x1, Pallas kernels, on_device(): pl.pallas_call(density_kernel, in_specs=[hbm, hbm] + [whole] * 7, out_spe...  16.7 us
    ppermute x8, starting transfers between devices, shift(): return lax.ppermute(block, axis, [(i, (i + step) % n) for i in range(n)])  14.6 us
    pallas_call x1, Pallas kernels, on_device(): pl.pallas_call(functools.partial(state_kernel, depth=planes * layers, cou...  14 us
    all_to_all x1, blocking collectives, on_device(): lax.all_to_all(mine, ('gz', 'xy'), split_axis=0, concat_axis=0, tiled=True)  12.7 us
    pallas_call x1, Pallas kernels, on_device(): pl.pallas_call(functools.partial(modes_kernel, turned=turned), in_specs=[...  6.98 us
    all_to_all x1, waiting for transfers between devices, on_device(): lax.all_to_all(wave, 'xy', split_axis=0, concat_axis=0, tiled=True)  6.62 us
  transfers between devices with their start and end apart: 9, of which 2 were waited for; matrix products, arithmetic and copies ran while one was open for 0% of the time, Pallas kernels for 27%

commit v1 on v0

--- a/solution.py
+++ b/solution.py
@@ -19,7 +19,7 @@
 FAR = TIME_STEP / 12.0
 VMEM = 56 * 1024 * 1024
 PACK_COST = MODES_COST = (1e6, 1e5)
-STATE_COST = DENSITY_COST = (1e6, 4e8)
+STATE_COST = DENSITY_COST = (1e12, 4e9)
 MAIN_COST = (1e12, 4e9)
 
 

time: 157 us -> 110 us (0.70); the launches traced: 157 us -> 108 us
  waiting for transfers between devices: 53.3 us -> 11.5 us
  blocking collectives: 12.7 us -> 0 us
  starting transfers between devices: 19.1 us -> 24.8 us
    ppermute x8, waiting for transfers between devices: 46.7 us -> 10.9 us  [shift(): return lax.ppermute(block, axis, [(i, (i + step) % n) for i in range(n)])]
    all_to_all x1 -> x0, blocking collectives: 12.7 us -> none  [on_device(): lax.all_to_all(mine, ('gz', 'xy'), split_axis=0, concat_axis=0, tiled=True)]
    all_to_all x1, waiting for transfers between devices: 6.62 us -> 0.58 us  [on_device(): lax.all_to_all(wave, 'xy', split_axis=0, concat_axis=0, tiled=True)]
    all_to_all x0 -> x1, starting transfers between devices: none -> 5.43 us  [on_device(): lax.all_to_all(mine, ('gz', 'xy'), split_axis=0, concat_axis=0, tiled=True)]
  transfers between devices with their start and end apart: 9 -> 10, of which waited for: 2 -> 5; matrix products, arithmetic and copies ran while one was open for 0% -> 0% of each run, Pallas kernels for 27% -> 53%
where the time goes in v1:
time: 110 us; the launch traced here: 108 us
  Pallas kernels  69.4 us (63%)
  starting transfers between devices  24.8 us (23%)
  waiting for transfers between devices  11.5 us (10%)
  between operations  1.36 us (1%)
    pallas_call x2, Pallas kernels, on_device(): pl.pallas_call(functools.partial(main_kernel, first=first), grid=(n,), in...  24.3 us
    pallas_call x1, Pallas kernels, on_device(): pl.pallas_call(density_kernel, in_specs=[hbm, hbm] + [whole] * 7, out_spe...  16.7 us
    pallas_call x1, Pallas kernels, on_device(): pl.pallas_call(functools.partial(state_kernel, depth=planes * layers, cou...  15.2 us
    ppermute x8, starting transfers between devices, shift(): return lax.ppermute(block, axis, [(i, (i + step) % n) for i in range(n)])  14.9 us
    ppermute x8, waiting for transfers between devices, shift(): return lax.ppermute(block, axis, [(i, (i + step) % n) for i in range(n)])  10.9 us
    pallas_call x1, Pallas kernels, on_device(): pl.pallas_call(functools.partial(modes_kernel, turned=turned), in_specs=[...  6.98 us
    all_to_all x1, starting transfers between devices, on_device(): lax.all_to_all(mine, ('gz', 'xy'), split_axis=0, concat_axis=0, tiled=True)  5.43 us
    all_to_all x1, starting transfers between devices, on_device(): lax.all_to_all(wave, 'xy', split_axis=0, concat_axis=0, tiled=True)  4.52 us
  transfers between devices with their start and end apart: 10, of which 5 were waited for; matrix products, arithmetic and copies ran while one was open for 0% of the time, Pallas kernels for 53%

profile of v1, /device:TPU:0, one launch (start us, length us, event | category | flops | bytes accessed | tf_op | source)
XLA Modules:
  0.0 107.7 jit_solution(13148404483292680685)
XLA Ops:
  1.3 1.8 %first.1 = (s32[32,1,128]{2,1,0:T(1,128)}, f32[8,2,4,512]{3,2,1,0:T(4,128)}, f32[8,2,4,512]{3,2,1,0:T(4,128)}) custom-call(s32[1,3]{1,0:T(1,128)} %cell_ref.1, s32[1]{0:T(128)S(6)} %copy.21.count_ref, f32[2,64,4,512]{3,2,1,0:T(4,128)} %bitcast.19, f32[3,2,64,4,512]{4,3,2,1,0:T(4,128)} %bitcast.7, f32[3,2,64,4,512]{4,3,2,1,0:T(4,128)} %bitcast.13, ...), custom_call_target="tpu_custom_call" | custom-call | flops 1000000 | bytes 100000 | tf_op jit(solution)/shard_map/first/pallas_call | solution.py:498
  3.1 2.9 %collective-permute-start = (f32[8,2,4,512]{3,2,1,0:T(4,128)}, f32[8,2,4,512]{3,2,1,0:T(4,128)S(1)}, u32[]{:S(2)}, u32[]{:S(2)}) collective-permute-start(f32[8,2,4,512]{3,2,1,0:T(4,128)} %get-tuple-element.24), channel_id=1, source_target_pairs={{0,1},{1,2},{2,3},{3,0},{4,5},{5,6},{6,7},{7,4},{8,9},{9,10},{10,1... | collective-permute-start | bytes 393224 | tf_op jit(solution)/shard_map/ppermute | solution.py:469
  6.1 1.0 collective-permute-start.1
  7.0 5.4 %all-to-all-start = ((s32[32,1,128]{2,1,0:T(1,128)}), s32[32,1,128]{2,1,0:T(1,128)S(1)}, u32[]{:S(2)}, u32[]{:S(2)}) async-start(s32[32,1,128]{2,1,0:T(1,128)} %get-tuple-element.23.after_ref), calls=%async_computation | async-start | bytes 32768 | tf_op jit(solution)/shard_map/all_to_all | solution.py:517
  12.5 4.4 %pack.1 = (f32[64,8,512]{2,1,0:T(8,128)}, f32[64,8,512]{2,1,0:T(8,128)}) custom-call(f32[2,64,4,512]{3,2,1,0:T(4,128)} %bitcast.21, f32[3,2,64,4,512]{4,3,2,1,0:T(4,128)} %bitcast.9, f32[3,2,64,4,512]{4,3,2,1,0:T(4,128)} %bitcast.15, s32[32,1,128]{2,1,0:T(1,128)} %get-tuple-element.23.after_ref), custom_call_target="tpu_custom_call" | custom-call | flops 1000000 | bytes 100000 | tf_op jit(solution)/shard_map/pack/pallas_call | solution.py:521
  16.8 0.3 collective-permute-start.2
  17.1 3.3 %collective-permute-start.3 = (f32[64,8,512]{2,1,0:T(8,128)}, f32[64,8,512]{2,1,0:T(8,128)}, u32[]{:S(2)}, u32[]{:S(2)}) collective-permute-start(f32[64,8,512]{2,1,0:T(8,128)} %get-tuple-element.29), channel_id=1, source_target_pairs={{0,28},{4,0},{8,4},{12,8},{16,12},{20,16},{24,20},{28,24},{1,29},{... | collective-permute-start | bytes 3145736 | tf_op jit(solution)/shard_map/ppermute | solution.py:469
  20.4 0.0 all-to-all-done.ev_ref
  20.4 0.0 collective-permute-done.before_ref
  20.4 0.0 copy-start.1
  20.4 0.0 collective-permute-done.1.after_ref
  20.4 0.0 copy-start.2
  20.4 0.6 copy-done
  21.0 0.1 copy-done.1
  21.0 0.0 copy-done.2
  21.1 15.2 %state.1 = (f32[8,64,8,512]{3,2,1,0:T(8,128)}, f32[8,4,8,512]{3,2,1,0:T(8,128)}, f32[64,8,512]{2,1,0:T(8,128)}, f32[64,8,512]{2,1,0:T(8,128)}, f32[5,18,8,512]{3,2,1,0:T(8,128)}, /*index=5*/f32[5,18,8,512]{3,2,1,0:T(8,128)}) custom-call(s32[32,1,128]{2,1,0:T(1,128)} %copy-done, f32[2,64,4,512]{3,2,1,0:T(4,128)} %bitcast.22, f32[3,2,64,4,512]{4,3,2,1,0:T(4,128)} %bitcast.10, ...), custom_call_target="tpu_custom_call" | custom-call | flops 999999995904 | bytes 4000000000 | tf_op jit(solution)/shard_map/state/pallas_call | solution.py:551
  36.3 0.1 collective-permute-start.6
  36.4 3.5 %collective-permute-start.7 = (f32[5,18,8,512]{3,2,1,0:T(8,128)}, f32[5,18,8,512]{3,2,1,0:T(8,128)}, u32[]{:S(2)}, u32[]{:S(2)}) collective-permute-start(f32[5,18,8,512]{3,2,1,0:T(8,128)} %get-tuple-element.36), channel_id=1, source_target_pairs={{0,28},{4,0},{8,4},{12,8},{16,12},{20,16},{24,20},{28,24},{1,29},{... | collective-permute-start | bytes 4423688 | tf_op jit(solution)/shard_map/ppermute | solution.py:469
  39.9 2.3 %collective-permute-done.2.below_ref.ba_ref = f32[64,8,512]{2,1,0:T(8,128)} collective-permute-done((f32[64,8,512]{2,1,0:T(8,128)}, f32[64,8,512]{2,1,0:T(8,128)}, u32[]{:S(2)}, u32[]{:S(2)}) %collective-permute-start.2) | collective-permute-done | bytes 1048608 | tf_op jit(solution)/shard_map/ppermute | solution.py:469
  42.2 2.1 %collective-permute-done.3.above_ref.aa_ref = f32[64,8,512]{2,1,0:T(8,128)} collective-permute-done((f32[64,8,512]{2,1,0:T(8,128)}, f32[64,8,512]{2,1,0:T(8,128)}, u32[]{:S(2)}, u32[]{:S(2)}) %collective-permute-start.3) | collective-permute-done | bytes 1048608 | tf_op jit(solution)/shard_map/ppermute | solution.py:469
  44.3 16.7 %density.1 = (f32[2,64,4,512]{3,2,1,0:T(4,128)}, f32[4,2,4,128,128]{4,3,2,1,0:T(8,128)}, f32[3,18,8,512]{3,2,1,0:T(8,128)}, f32[3,18,8,512]{3,2,1,0:T(8,128)}) custom-call(f32[8,64,8,512]{3,2,1,0:T(8,128)} %get-tuple-element.26.u_hbm, f32[8,4,8,512]{3,2,1,0:T(8,128)} %get-tuple-element.27.edge_hbm, f32[64,8,512]{2,1,0:T(8,128)} %collective-permute-done.2.below_ref.ba_ref, ...), custom_call_target="tpu_custom_call" | custom-call | flops 999999995904 | bytes 4000000000 | tf_op jit(solution)/shard_map/density/pallas_call | solution.py:573
  61.0 4.5 %all-to-all-start.1 = ((f32[4,2,4,128,128]{4,3,2,1,0:T(8,128)}), f32[4,2,4,128,128]{4,3,2,1,0:T(8,128)}, u32[]{:S(2)}, u32[]{:S(2)}) async-start(f32[4,2,4,128,128]{4,3,2,1,0:T(8,128)} %get-tuple-element.39), calls=%async_computation.1 | async-start | bytes 4194304 | tf_op jit(solution)/shard_map/all_to_all | solution.py:593
  65.5 2.4 %collective-permute-start.4 = (f32[3,18,8,512]{3,2,1,0:T(8,128)}, f32[3,18,8,512]{3,2,1,0:T(8,128)}, u32[]{:S(2)}, u32[]{:S(2)}) collective-permute-start(f32[3,18,8,512]{3,2,1,0:T(8,128)} %get-tuple-element.33), channel_id=1, source_target_pairs={{0,4},{4,8},{8,12},{12,16},{16,20},{20,24},{24,28},{28,0},{1,5},{5... | collective-permute-start | bytes 2654216 | tf_op jit(solution)/shard_map/ppermute | solution.py:469
  68.0 1.4 %collective-permute-start.5 = (f32[3,18,8,512]{3,2,1,0:T(8,128)}, f32[3,18,8,512]{3,2,1,0:T(8,128)}, u32[]{:S(2)}, u32[]{:S(2)}) collective-permute-start(f32[3,18,8,512]{3,2,1,0:T(8,128)} %get-tuple-element.34), channel_id=1, source_target_pairs={{0,28},{4,0},{8,4},{12,8},{16,12},{20,16},{24,20},{28,24},{1,29},{... | collective-permute-start | bytes 2654216 | tf_op jit(solution)/shard_map/ppermute | solution.py:469
  69.4 4.4 %collective-permute-done.6.from_below = f32[5,18,8,512]{3,2,1,0:T(8,128)} collective-permute-done((f32[5,18,8,512]{3,2,1,0:T(8,128)}, f32[5,18,8,512]{3,2,1,0:T(8,128)}, u32[]{:S(2)}, u32[]{:S(2)}) %collective-permute-start.6) | collective-permute-done | bytes 1474592 | tf_op jit(solution)/shard_map/ppermute | solution.py:469
  73.8 2.1 %collective-permute-done.7.from_above = f32[5,18,8,512]{3,2,1,0:T(8,128)} collective-permute-done((f32[5,18,8,512]{3,2,1,0:T(8,128)}, f32[5,18,8,512]{3,2,1,0:T(8,128)}, u32[]{:S(2)}, u32[]{:S(2)}) %collective-permute-start.7) | collective-permute-done | bytes 1474592 | tf_op jit(solution)/shard_map/ppermute | solution.py:469
  75.9 14.3 %main0.1 = (f32[3,2,64,4,512]{4,3,2,1,0:T(4,128)}, f32[3,2,64,4,512]{4,3,2,1,0:T(4,128)}) custom-call(f32[8,64,8,512]{3,2,1,0:T(8,128)} %get-tuple-element.26.u_hbm, f32[8,4,8,512]{3,2,1,0:T(8,128)} %get-tuple-element.27.edge_hbm, f32[64,8,512]{2,1,0:T(8,128)} %collective-permute-done.2.below_ref.ba_ref, ...), custom_call_target="tpu_custom_call" | custom-call | flops 999999995904 | bytes 4000000000 | tf_op jit(solution)/shard_map/main0/pallas_call | solution.py:615
  90.2 0.6 all-to-all-done.1.w_ref
  90.8 7.0 %modes.1.rest_2_ = f32[2,4,128,512]{3,2,1,0:T(8,128)} custom-call(f32[4,2,4,128,128]{4,3,2,1,0:T(8,128)} %all-to-all-done.1.w_ref, bf16[512,512]{1,0:T(8,128)(2,1)} %constant.17.clone.ch_ref, bf16[512,512]{1,0:T(8,128)(2,1)} %constant.18.clone.cl_ref, bf16[512,512]{1,0:T(8,128)(2,1)} %constant.19.clone.sh_ref, bf16[512,512]{1,0:T(8,128)(2,1)} %constant.20.clone.sl_ref), custom_call_target="tpu_custom_call" | custom-call | flops 1000000 | bytes 100000 | tf_op jit(solution)/shard_map/modes/pallas_call | solution.py:596
  97.8 0.0 collective-permute-done.4.from_below
  97.8 0.0 collective-permute-done.5.from_above
  97.8 10.0 %main1.1 = (f32[3,2,64,4,512]{4,3,2,1,0:T(4,128)}, f32[3,2,64,4,512]{4,3,2,1,0:T(4,128)}) custom-call(f32[8,64,8,512]{3,2,1,0:T(8,128)} %get-tuple-element.26.u_hbm, f32[8,4,8,512]{3,2,1,0:T(8,128)} %get-tuple-element.27.edge_hbm, f32[64,8,512]{2,1,0:T(8,128)} %collective-permute-done.2.below_ref.ba_ref, ...), custom_call_target="tpu_custom_call", output_to_operand_aliasing={{0}: (8, {}), {1}: (9, {})} | custom-call | flops 999999995904 | bytes 4000000000 | tf_op jit(solution)/shard_map/main1/pallas_call | solution.py:615
  (1 shorter events, 0.0 us)
Async XLA Ops:
  3.1 17.3 %collective-permute-start = (f32[8,2,4,512]{3,2,1,0:T(4,128)}, f32[8,2,4,512]{3,2,1,0:T(4,128)S(1)}, u32[]{:S(2)}, u32[]{:S(2)}) collective-permute-start(f32[8,2,4,512]{3,2,1,0:T(4,128)} %get-tuple-element.24), channel_id=1, source_target_pairs={{0,1},{1,2},{2,3},{3,0},{4,5},{5,6},{6,7},{7,4},{8,9},{9,10},{10,1... | collective-permute-start | bytes 393224 | tf_op jit(solution)/shard_map/ppermute | solution.py:469
  6.1 14.3 %collective-permute-start.1 = (f32[8,2,4,512]{3,2,1,0:T(4,128)}, f32[8,2,4,512]{3,2,1,0:T(4,128)S(1)}, u32[]{:S(2)}, u32[]{:S(2)}) collective-permute-start(f32[8,2,4,512]{3,2,1,0:T(4,128)} %get-tuple-element.25), channel_id=1, source_target_pairs={{0,3},{1,0},{2,1},{3,2},{4,7},{5,4},{6,5},{7,6},{8,11},{9,8},{10,9... | collective-permute-start | bytes 393224 | tf_op jit(solution)/shard_map/ppermute | solution.py:469
  7.0 13.3 %all-to-all-start = ((s32[32,1,128]{2,1,0:T(1,128)}), s32[32,1,128]{2,1,0:T(1,128)S(1)}, u32[]{:S(2)}, u32[]{:S(2)}) async-start(s32[32,1,128]{2,1,0:T(1,128)} %get-tuple-element.23.after_ref), calls=%async_computation | async-start | bytes 32768 | tf_op jit(solution)/shard_map/all_to_all | solution.py:517
  16.8 25.4 %collective-permute-start.2 = (f32[64,8,512]{2,1,0:T(8,128)}, f32[64,8,512]{2,1,0:T(8,128)}, u32[]{:S(2)}, u32[]{:S(2)}) collective-permute-start(f32[64,8,512]{2,1,0:T(8,128)} %get-tuple-element.28), channel_id=1, source_target_pairs={{0,4},{4,8},{8,12},{12,16},{16,20},{20,24},{24,28},{28,0},{1,5},{5... | collective-permute-start | bytes 3145736 | tf_op jit(solution)/shard_map/ppermute | solution.py:469
  17.1 27.2 %collective-permute-start.3 = (f32[64,8,512]{2,1,0:T(8,128)}, f32[64,8,512]{2,1,0:T(8,128)}, u32[]{:S(2)}, u32[]{:S(2)}) collective-permute-start(f32[64,8,512]{2,1,0:T(8,128)} %get-tuple-element.29), channel_id=1, source_target_pairs={{0,28},{4,0},{8,4},{12,8},{16,12},{20,16},{24,20},{28,24},{1,29},{... | collective-permute-start | bytes 3145736 | tf_op jit(solution)/shard_map/ppermute | solution.py:469
  20.4 0.6 copy-start
  20.4 0.7 copy-start.1
  20.4 0.7 copy-start.2
  36.3 37.5 %collective-permute-start.6 = (f32[5,18,8,512]{3,2,1,0:T(8,128)}, f32[5,18,8,512]{3,2,1,0:T(8,128)}, u32[]{:S(2)}, u32[]{:S(2)}) collective-permute-start(f32[5,18,8,512]{3,2,1,0:T(8,128)} %get-tuple-element.35), channel_id=1, source_target_pairs={{0,4},{4,8},{8,12},{12,16},{16,20},{20,24},{24,28},{28,0},{1,5},{5... | collective-permute-start | bytes 4423688 | tf_op jit(solution)/shard_map/ppermute | solution.py:469
  36.4 39.5 %collective-permute-start.7 = (f32[5,18,8,512]{3,2,1,0:T(8,128)}, f32[5,18,8,512]{3,2,1,0:T(8,128)}, u32[]{:S(2)}, u32[]{:S(2)}) collective-permute-start(f32[5,18,8,512]{3,2,1,0:T(8,128)} %get-tuple-element.36), channel_id=1, source_target_pairs={{0,28},{4,0},{8,4},{12,8},{16,12},{20,16},{24,20},{28,24},{1,29},{... | collective-permute-start | bytes 4423688 | tf_op jit(solution)/shard_map/ppermute | solution.py:469
  61.0 29.8 %all-to-all-start.1 = ((f32[4,2,4,128,128]{4,3,2,1,0:T(8,128)}), f32[4,2,4,128,128]{4,3,2,1,0:T(8,128)}, u32[]{:S(2)}, u32[]{:S(2)}) async-start(f32[4,2,4,128,128]{4,3,2,1,0:T(8,128)} %get-tuple-element.39), calls=%async_computation.1 | async-start | bytes 4194304 | tf_op jit(solution)/shard_map/all_to_all | solution.py:593
  65.5 32.2 %collective-permute-start.4 = (f32[3,18,8,512]{3,2,1,0:T(8,128)}, f32[3,18,8,512]{3,2,1,0:T(8,128)}, u32[]{:S(2)}, u32[]{:S(2)}) collective-permute-start(f32[3,18,8,512]{3,2,1,0:T(8,128)} %get-tuple-element.33), channel_id=1, source_target_pairs={{0,4},{4,8},{8,12},{12,16},{16,20},{20,24},{24,28},{28,0},{1,5},{5... | collective-permute-start | bytes 2654216 | tf_op jit(solution)/shard_map/ppermute | solution.py:469
  68.0 29.8 %collective-permute-start.5 = (f32[3,18,8,512]{3,2,1,0:T(8,128)}, f32[3,18,8,512]{3,2,1,0:T(8,128)}, u32[]{:S(2)}, u32[]{:S(2)}) collective-permute-start(f32[3,18,8,512]{3,2,1,0:T(8,128)} %get-tuple-element.34), channel_id=1, source_target_pairs={{0,28},{4,0},{8,4},{12,8},{16,12},{20,16},{24,20},{28,24},{1,29},{... | collective-permute-start | bytes 2654216 | tf_op jit(solution)/shard_map/ppermute | solution.py:469

commit v2 on v1

--- a/solution.py
+++ b/solution.py
@@ -49,6 +49,15 @@
     return out
 
 
+def collect(values, plane):
+    sub = lax.broadcasted_iota(jnp.int32, values[0].shape, 0)
+    out = turn(values[0], -plane, 0)
+    for n in range(1, 8):
+        j, h = n // 2, n % 2
+        out = jnp.where(sub == n, turn(values[j], n - 4 * h - plane, 0), out)
+    return out
+
+
 def shared(rho, m, b):
     inv = 1.0 / rho
     return [x * inv for x in m], rho + 0.5 * (b[0] * b[0] + b[1] * b[1] + b[2] * b[2])
@@ -84,40 +93,35 @@
             ref[7, j] = jnp.broadcast_to(pot[skip + j : skip + j + 1], ref.shape[2:])
 
 
-def pack_kernel(rho_ref, mz_ref, bx_ref, after_ref, up_ref, down_ref):
-    half = rho_ref.shape[1]
-
-    def body(p, _):
-        rho, mz, bx = pair(rho_ref, p), pair(mz_ref, 0, p), pair(bx_ref, 0, p)
-        slot = slots(rho.shape)
-        up = jnp.where(slot == 2, mz, gather_planes([rho, mz, mz, bx], 3))
-        down = jnp.where(slot == 2, turn(mz, 1, 0), gather_planes([rho, mz, mz, bx], 0))
-        up_ref[p] = up
-        down_ref[p] = down
-        return 0
-
-    lax.fori_loop(0, half, body, 0)
+def pack_kernel(rho_ref, mz_ref, after_ref, up_ref, down_ref):
+    def body(g, _):
+        rho = [pair(rho_ref, 4 * g + j) for j in range(4)]
+        mz = [pair(mz_ref, 0, 4 * g + j) for j in range(4)]
+        for i, (values, up, down) in enumerate(((rho, 3, 0), (mz, 3, 0), (mz, 2, 1))):
+            up_ref[g, i] = collect(values, up)
+            down_ref[g, i] = collect(values, down)
+        return 0
+
+    lax.fori_loop(0, rho_ref.shape[1] // 4, body, 0)
 
 
 def write_messages(up_ref, down_ref, k, g, state):
-    lasts = None
+    fluxes_by, bx = [], []
     for j in range(4):
         r = 4 * g + j
         u = state(j)
-        sub = lax.broadcasted_iota(jnp.int32, u[0].shape, 0)
         near = [u[1], u[2], u[5], u[6]]
         up_ref[k, r] = gather_planes(near, 3)
         down_ref[k, r] = gather_planes(near, 0)
         f = fluxes(*shared(u[0], u[1:4], u[4:7]), u[1:4], u[4:7], 2)
         up_ref[k, 8 + r] = gather_planes(f[:4], 2)
         down_ref[k, 8 + r] = gather_planes(f[:4], 1)
-        lasts = lasts or [f[4], f[4]]
-        for i, plane in enumerate((2, 1)):
-            for h in range(2):
-                moved = turn(f[4], 2 * j + h - 4 * h - plane, 0)
-                lasts[i] = jnp.where(sub == 2 * j + h, moved, lasts[i])
-    up_ref[k, 16 + g] = lasts[0]
-    down_ref[k, 16 + g] = lasts[1]
+        fluxes_by.append(f[4])
+        bx.append(u[4])
+    up_ref[k, 16 + g] = collect(fluxes_by, 2)
+    down_ref[k, 16 + g] = collect(fluxes_by, 1)
+    up_ref[k, 18 + g] = collect(bx, 3)
+    down_ref[k, 18 + g] = collect(bx, 0)
 
 
 def state_kernel(
@@ -284,7 +288,8 @@
 
 
 def density_kernel(
-    u_hbm, edge_hbm, below_ref, above_ref, sb_ref, sa_ref, order_ref, high_ref, low_ref, out_ref, wave_ref, *rest,
+    u_hbm, edge_hbm, below_ref, above_ref, sb_ref, sa_ref, order_ref, high_ref, low_ref, out_ref, wave_ref,
+    rho_out, mz_out, *rest,
 ):
     *parcel, d_ref, u_ref, b_ref, sem = rest
     half = u_hbm.shape[1]
@@ -293,23 +298,28 @@
         field = pltpu.make_async_copy(u_hbm.at[4:7, half - b_ref.shape[1] :], b_ref, sem.at[3])
         field.start()
     fetch(u_hbm, edge_hbm, u_ref, sem, 0)
-    half = below_ref.shape[0]
     rows = 2 * half
 
-    def body(p, _):
+    def row(p, g, j):
         rho, my, mz = u_ref[0, p + 2], u_ref[2, p + 2], u_ref[3, p + 2]
-        below, above = below_ref[p] + sb_ref[p], above_ref[p] + sa_ref[p]
+        sb, sa = sb_ref[p], sa_ref[p]
+        halo = [last_plane(below_ref[g, i], above_ref[g, i], j) + ends(sb, sa, i) for i in range(3)]
+        rho_out[p], mz_out[p] = halo[:2]
         b = DIFFUSION * rho
         new = rho * (1.0 - 6.0 * DIFFUSION)
         new += DIFFUSION * (u_ref[0, p + 1] + u_ref[0, p + 3])
         new += NEAR * (u_ref[1, p + 1] - u_ref[1, p + 3]) + FAR * (u_ref[1, p + 4] - u_ref[1, p])
         new += along_y(my, b)
-        new += along_z(mz, b, ends(below, above, 1), ends(below, above, 0), ends(below, above, 2))
+        new += along_z(mz, b, halo[1], halo[0], halo[2])
         unpair(out_ref, new, p)
         d_ref[pl.ds(pl.multiple_of(p * 8, 8), 8), :] = new
-        return 0
-
-    lax.fori_loop(0, half, body, 0)
+
+    def body(g, _):
+        for j in range(4):
+            row(4 * g + j, g, j)
+        return 0
+
+    lax.fori_loop(0, half // 4, body, 0)
     d = d_ref[...]
     order = order_ref[...]
     dot = functools.partial(jnp.dot, preferred_element_type=jnp.float32)
@@ -346,24 +356,46 @@
     return jnp.where(sub == 7, turn(above, 6 - 2 * j, 0), out)
 
 
-def main_kernel(u_hbm, edge_hbm, ba_ref, aa_ref, sb_ref, sa_ref, from_below, from_above, *rest, first):
+def main_kernel(u_hbm, edge_hbm, rho_ref, mz_ref, from_below, from_above, *rest, first):
     mom_ref, mag_ref, u_ref, f_ref, sem = rest[-5:]
-    chunk, total = ba_ref.shape[0], u_ref.shape[1]
-    start = pl.program_id(0) * chunk
+    chunk, total, half = rho_ref.shape[0], u_ref.shape[1], u_hbm.shape[1]
+    step_id = pl.program_id(0)
+    start = step_id * chunk
     kept = (0, 1, 2, 4, 5)
 
-    @pl.when(pl.program_id(0) == 0)
+    def copies(i):
+        low = 0 if i == 0 else chunk * i + 4
+        high = chunk * (i + 1) + 4
+        a, b = max(first - 2 + low, 0), min(first - 2 + high, half)
+        at = a - first + 2
+        result = [(u_hbm.at[:, a:b], u_ref.at[:, at : at + b - a], sem.at[i])]
+        if first - 2 + low < 0:
+            result.append((edge_hbm.at[:, 0:2], u_ref.at[:, 0:2], sem.at[total // chunk]))
+        if first - 2 + high > half:
+            result.append((edge_hbm.at[:, 2:4], u_ref.at[:, total - 2 : total], sem.at[total // chunk + 1]))
+        return [pltpu.make_async_copy(*c) for c in result]
+
+    @pl.when(step_id == 0)
     def _():
-        fetch(u_hbm, edge_hbm, u_ref, sem, first)
-
-        def fx(q, _):
-            u = [u_ref[f, q] for f in range(7)]
-            f = fluxes(*shared(u[0], u[1:4], u[4:7]), u[1:4], u[4:7], 0)
-            for i, c in enumerate(kept):
-                f_ref[i, q] = f[c]
-            return 0
-
-        lax.fori_loop(0, total, fx, 0)
+        for i in range(total // chunk):
+            for copy in copies(i):
+                copy.start()
+
+    for i in range(total // chunk):
+
+        @pl.when(step_id == i)
+        def _(i=i):
+            for copy in copies(i):
+                copy.wait()
+
+    def fx(q, _):
+        u = [u_ref[f, q] for f in range(7)]
+        f = fluxes(*shared(u[0], u[1:4], u[4:7]), u[1:4], u[4:7], 0)
+        for i, c in enumerate(kept):
+            f_ref[i, q] = f[c]
+        return 0
+
+    lax.fori_loop(jnp.where(step_id == 0, 0, start + 4), start + chunk + 4, fx, 0)
 
     def row(r, g, j):
         q = start + r + 2
@@ -371,11 +403,10 @@
         v, pressure = shared(u[0], u[1:4], u[4:7])
         fy = fluxes(v, pressure, u[1:4], u[4:7], 1)
         fz = fluxes(v, pressure, u[1:4], u[4:7], 2)
-        ba, aa = ba_ref[r] + sb_ref[r], aa_ref[r] + sa_ref[r]
         bn, an, bf, af = from_below[0, r], from_above[0, r], from_below[0, 8 + r], from_above[0, 8 + r]
-        hm = [ends(bn, an, 0), ends(bn, an, 1), ends(ba, aa, 1)]
-        hb = [ends(ba, aa, 3), ends(bn, an, 2), ends(bn, an, 3)]
-        fh = fluxes(*shared(ends(ba, aa, 0), hm, hb), hm, hb, 2)
+        hm = [ends(bn, an, 0), ends(bn, an, 1), mz_ref[r]]
+        hb = [last_plane(from_below[0, 18 + g], from_above[0, 18 + g], j), ends(bn, an, 2), ends(bn, an, 3)]
+        fh = fluxes(*shared(rho_ref[r], hm, hb), hm, hb, 2)
         halo = hm + hb
         far = [ends(bf, af, c) for c in range(4)] + [last_plane(from_below[0, 16 + g], from_above[0, 16 + g], j), None]
         for c in range(6):
@@ -522,20 +553,20 @@
         pack_kernel,
         grid=(half // some,),
         in_specs=[pl.BlockSpec((2, some, planes, ny), lambda i: (0, i, 0, 0))] + [
-            pl.BlockSpec((1, 2, some, planes, ny), lambda i, f=f: (f, 0, i, 0, 0)) for f in (2, 0)
+            pl.BlockSpec((1, 2, some, planes, ny), lambda i, f=f: (f, 0, i, 0, 0)) for f in (2,)
         ] + [pl.BlockSpec(memory_space=pl.ANY)],
-        out_specs=[pl.BlockSpec((some, 8, ny), lambda i: (i, 0, 0))] * 2,
-        out_shape=[tile] * 2,
+        out_specs=[pl.BlockSpec((some // 4, 3, 8, ny), lambda i: (i, 0, 0, 0))] * 2,
+        out_shape=[shape((half // 4, 3, 8, ny), f32)] * 2,
         compiler_params=params,
         cost_estimate=cost(*PACK_COST),
         name="pack",
-    )(rho, mom, mag, mine)
+    )(rho, mom, mine)
     below_a, above_a = shift(up, "gz", 1), shift(down, "gz", -1)
 
-    parcels = [shape((n, 18, 8, ny), f32) for n in counts]
+    parcels = [shape((n, 20, 8, ny), f32) for n in counts]
     side = pltpu.VMEM((half + 4, 8, ny), f32)
     begins = [sum(counts[:i]) for i in range(len(counts))]
-    parcel = pl.BlockSpec((1, 18, 8, ny), lambda i: (jnp.minimum(i, counts[0] - 1), 0, 0, 0))
+    parcel = pl.BlockSpec((1, 20, 8, ny), lambda i: (jnp.minimum(i, counts[0] - 1), 0, 0, 0))
     eight = pl.BlockSpec((8, 8, ny), lambda i: (i, 0, 0))
     middle = [
         spec
@@ -568,13 +599,12 @@
     band = ny // across
     turned = band % 128 != 0 or rows % 128 != 0
     hbm = pl.BlockSpec(memory_space=pl.ANY)
-    copies = pltpu.SemaphoreType.DMA((3,))
     more = parcels[1:] * 2
-    new_density, wave, *messages = pl.pallas_call(
+    new_density, wave, rho_halo, mz_halo, *messages = pl.pallas_call(
         density_kernel,
         in_specs=[hbm, hbm] + [whole] * 7,
-        out_specs=[whole] * (2 + len(more)),
-        out_shape=[message, shape((across, 2, planes, rows, band), f32), *more],
+        out_specs=[whole] * (4 + len(more)),
+        out_shape=[message, shape((across, 2, planes, rows, band), f32), tile, tile, *more],
         scratch_shapes=[
             pltpu.VMEM((8 * half, ny), f32), pltpu.VMEM((4, half + 4, 8, ny), f32),
             pltpu.VMEM((3, counts[-1] * 8, 8, ny), f32), pltpu.SemaphoreType.DMA((4,)),
@@ -608,24 +638,24 @@
     for i, n in enumerate(counts):
         chunk, first = 8, begins[i] * 8
         here = pl.BlockSpec((chunk, 8, ny), lambda k, o=begins[i]: (o + k, 0, 0))
-        parcel = pl.BlockSpec((1, 18, 8, ny), lambda k: (k, 0, 0, 0))
+        parcel = pl.BlockSpec((1, 20, 8, ny), lambda k: (k, 0, 0, 0))
         three = pl.BlockSpec((3, 2, chunk, planes, ny), lambda k, o=begins[i]: (0, 0, o + k, 0, 0))
         below, above = parcels_below[i], parcels_above[i]
         extra = [*new] + [modes] * (i > 0 and i == len(counts) - 1)
         new = pl.pallas_call(
             functools.partial(main_kernel, first=first),
             grid=(n,),
-            in_specs=[hbm, hbm] + [here] * 4 + [parcel] * 2 + [hbm] * len(extra),
+            in_specs=[hbm, hbm] + [here] * 2 + [parcel] * 2 + [hbm] * len(extra),
             out_specs=[three, three],
             out_shape=results,
             scratch_shapes=[
-                pltpu.VMEM((8, n * 8 + 4, 8, ny), f32), pltpu.VMEM((5, n * 8 + 4, 8, ny), f32), copies,
+                pltpu.VMEM((8, n * 8 + 4, 8, ny), f32), pltpu.VMEM((5, n * 8 + 4, 8, ny), f32), pltpu.SemaphoreType.DMA((n + 2,)),
             ],
-            input_output_aliases={8: 0, 9: 1} if new else {},
+            input_output_aliases={6: 0, 7: 1} if new else {},
             compiler_params=pltpu.CompilerParams(vmem_limit_bytes=62 * 1024 * 1024),
             cost_estimate=cost(*MAIN_COST),
             name=f"main{i}",
-        )(state, edge, below_a, above_a, sb, sa, below, above, *extra)
+        )(state, edge, rho_halo, mz_halo, below, above, *extra)
     new_mom, new_mag = new
 
     return (

time: 110 us -> 106 us (0.964); the launches traced: 108 us -> 105 us
  Pallas kernels: 69.4 us -> 63.5 us
  waiting for transfers between devices: 11.5 us -> 15.1 us
    ppermute x8, waiting for transfers between devices: 10.9 us -> 15.1 us  [shift(): return lax.ppermute(block, axis, [(i, (i + step) % n) for i in range(n)])]
    pallas_call x1, Pallas kernels: 16.7 us -> 14.3 us  [on_device(): pl.pallas_call(density_kernel, in_specs=[hbm, hbm] + [whole] * 7, out_spe...]
    pallas_call x2, Pallas kernels: 24.3 us -> 22.2 us  [on_device(): pl.pallas_call(functools.partial(main_kernel, first=first), grid=(n,), in...]
  transfers between devices with their start and end apart: 10 -> 10, of which waited for: 5 -> 3; matrix products, arithmetic and copies ran while one was open for 0% -> 0% of each run, Pallas kernels for 53% -> 50%
where the time goes in v2:
time: 106 us; the launch traced here: 105 us
  Pallas kernels  63.5 us (60%)
  starting transfers between devices  24.6 us (23%)
  waiting for transfers between devices  15.1 us (14%)
  between operations  1.37 us (1%)
    pallas_call x2, Pallas kernels, on_device(): pl.pallas_call(functools.partial(main_kernel, first=first), grid=(n,), in...  22.2 us
    ppermute x8, waiting for transfers between devices, shift(): return lax.ppermute(block, axis, [(i, (i + step) % n) for i in range(n)])  15.1 us
    ppermute x8, starting transfers between devices, shift(): return lax.ppermute(block, axis, [(i, (i + step) % n) for i in range(n)])  14.6 us
    pallas_call x1, Pallas kernels, on_device(): pl.pallas_call(density_kernel, in_specs=[hbm, hbm] + [whole] * 7, out_spe...  14.3 us
    pallas_call x1, Pallas kernels, on_device(): pl.pallas_call(functools.partial(state_kernel, depth=planes * layers, cou...  14.2 us
    pallas_call x1, Pallas kernels, on_device(): pl.pallas_call(functools.partial(modes_kernel, turned=turned), in_specs=[...  6.93 us
    all_to_all x1, starting transfers between devices, on_device(): lax.all_to_all(mine, ('gz', 'xy'), split_axis=0, concat_axis=0, tiled=True)  5.43 us
    all_to_all x1, starting transfers between devices, on_device(): lax.all_to_all(wave, 'xy', split_axis=0, concat_axis=0, tiled=True)  4.52 us
  transfers between devices with their start and end apart: 10, of which 3 were waited for; matrix products, arithmetic and copies ran while one was open for 0% of the time, Pallas kernels for 50%

profile of v2, /device:TPU:0, one launch (start us, length us, event | category | flops | bytes accessed | tf_op | source)
XLA Modules:
  0.0 105.2 jit_solution(3896696144050008804)
XLA Ops:
  1.3 1.8 %first.1 = (s32[32,1,128]{2,1,0:T(1,128)}, f32[8,2,4,512]{3,2,1,0:T(4,128)}, f32[8,2,4,512]{3,2,1,0:T(4,128)}) custom-call(s32[1,3]{1,0:T(1,128)} %cell_ref.1, s32[1]{0:T(128)S(6)} %copy.21.count_ref, f32[2,64,4,512]{3,2,1,0:T(4,128)} %bitcast.18, f32[3,2,64,4,512]{4,3,2,1,0:T(4,128)} %bitcast.7, f32[3,2,64,4,512]{4,3,2,1,0:T(4,128)} %bitcast.13, ...), custom_call_target="tpu_custom_call" | custom-call | flops 1000000 | bytes 100000 | tf_op jit(solution)/shard_map/first/pallas_call | solution.py:529
  3.1 2.9 %collective-permute-start = (f32[8,2,4,512]{3,2,1,0:T(4,128)}, f32[8,2,4,512]{3,2,1,0:T(4,128)S(1)}, u32[]{:S(2)}, u32[]{:S(2)}) collective-permute-start(f32[8,2,4,512]{3,2,1,0:T(4,128)} %get-tuple-element.26), channel_id=1, source_target_pairs={{0,1},{1,2},{2,3},{3,0},{4,5},{5,6},{6,7},{7,4},{8,9},{9,10},{10,1... | collective-permute-start | bytes 393224 | tf_op jit(solution)/shard_map/ppermute | solution.py:500
  6.1 1.0 collective-permute-start.1
  7.0 5.4 %all-to-all-start = ((s32[32,1,128]{2,1,0:T(1,128)}), s32[32,1,128]{2,1,0:T(1,128)S(1)}, u32[]{:S(2)}, u32[]{:S(2)}) async-start(s32[32,1,128]{2,1,0:T(1,128)} %get-tuple-element.25.after_ref), calls=%async_computation | async-start | bytes 32768 | tf_op jit(solution)/shard_map/all_to_all | solution.py:548
  12.5 4.0 %pack.1 = (f32[16,3,8,512]{3,2,1,0:T(8,128)}, f32[16,3,8,512]{3,2,1,0:T(8,128)}) custom-call(f32[2,64,4,512]{3,2,1,0:T(4,128)} %bitcast.20, f32[3,2,64,4,512]{4,3,2,1,0:T(4,128)} %bitcast.9, s32[32,1,128]{2,1,0:T(1,128)} %get-tuple-element.25.after_ref), custom_call_target="tpu_custom_call" | custom-call | flops 1000000 | bytes 100000 | tf_op jit(solution)/shard_map/pack/pallas_call | solution.py:552
  16.5 0.3 collective-permute-start.2
  16.7 3.3 %collective-permute-start.3 = (f32[16,3,8,512]{3,2,1,0:T(8,128)}, f32[16,3,8,512]{3,2,1,0:T(8,128)}, u32[]{:S(2)}, u32[]{:S(2)}) collective-permute-start(f32[16,3,8,512]{3,2,1,0:T(8,128)} %get-tuple-element.31), channel_id=1, source_target_pairs={{0,28},{4,0},{8,4},{12,8},{16,12},{20,16},{24,20},{28,24},{1,29},{... | collective-permute-start | bytes 2359304 | tf_op jit(solution)/shard_map/ppermute | solution.py:500
  20.0 0.0 all-to-all-done.ev_ref
  20.0 0.0 collective-permute-done.before_ref
  20.0 0.0 copy-start.1
  20.1 0.0 collective-permute-done.1.after_ref
  20.1 0.0 copy-start.2
  20.1 0.6 copy-done
  20.6 0.1 copy-done.1
  20.7 0.1 copy-done.2
  20.8 14.2 %state.1 = (f32[8,64,8,512]{3,2,1,0:T(8,128)}, f32[8,4,8,512]{3,2,1,0:T(8,128)}, f32[64,8,512]{2,1,0:T(8,128)}, f32[64,8,512]{2,1,0:T(8,128)}, f32[5,20,8,512]{3,2,1,0:T(8,128)}, /*index=5*/f32[5,20,8,512]{3,2,1,0:T(8,128)}) custom-call(s32[32,1,128]{2,1,0:T(1,128)} %copy-done, f32[2,64,4,512]{3,2,1,0:T(4,128)} %bitcast.21, f32[3,2,64,4,512]{4,3,2,1,0:T(4,128)} %bitcast.10, ...), custom_call_target="tpu_custom_call" | custom-call | flops 999999995904 | bytes 4000000000 | tf_op jit(solution)/shard_map/state/pallas_call | solution.py:582
  34.9 0.1 collective-permute-start.6
  35.0 3.5 %collective-permute-start.7 = (f32[5,20,8,512]{3,2,1,0:T(8,128)}, f32[5,20,8,512]{3,2,1,0:T(8,128)}, u32[]{:S(2)}, u32[]{:S(2)}) collective-permute-start(f32[5,20,8,512]{3,2,1,0:T(8,128)} %get-tuple-element.40), channel_id=1, source_target_pairs={{0,28},{4,0},{8,4},{12,8},{16,12},{20,16},{24,20},{28,24},{1,29},{... | collective-permute-start | bytes 4915208 | tf_op jit(solution)/shard_map/ppermute | solution.py:500
  38.5 0.0 collective-permute-done.2.below_ref
  38.5 0.0 collective-permute-done.3.above_ref
  38.5 14.3 %density.1 = (f32[2,64,4,512]{3,2,1,0:T(4,128)}, f32[4,2,4,128,128]{4,3,2,1,0:T(8,128)}, f32[64,8,512]{2,1,0:T(8,128)}, f32[64,8,512]{2,1,0:T(8,128)}, f32[3,20,...) custom-call(f32[8,64,8,512]{3,2,1,0:T(8,128)} %get-tuple-element.28.u_hbm, f32[8,4,8,512]{3,2,1,0:T(8,128)} %get-tuple-element.29.edge_hbm, ...), custom_call_target="tpu_custom_call" | custom-call | flops 999999995904 | bytes 4000000000 | tf_op jit(solution)/shard_map/density/pallas_call | solution.py:603
  52.8 4.5 %all-to-all-start.1 = ((f32[4,2,4,128,128]{4,3,2,1,0:T(8,128)}), f32[4,2,4,128,128]{4,3,2,1,0:T(8,128)}, u32[]{:S(2)}, u32[]{:S(2)}) async-start(f32[4,2,4,128,128]{4,3,2,1,0:T(8,128)} %get-tuple-element.43), calls=%async_computation.1 | async-start | bytes 4194304 | tf_op jit(solution)/shard_map/all_to_all | solution.py:623
  57.4 0.1 collective-permute-start.4
  57.4 3.5 %collective-permute-start.5 = (f32[3,20,8,512]{3,2,1,0:T(8,128)}, f32[3,20,8,512]{3,2,1,0:T(8,128)}, u32[]{:S(2)}, u32[]{:S(2)}) collective-permute-start(f32[3,20,8,512]{3,2,1,0:T(8,128)} %get-tuple-element.38), channel_id=1, source_target_pairs={{0,28},{4,0},{8,4},{12,8},{16,12},{20,16},{24,20},{28,24},{1,29},{... | collective-permute-start | bytes 2949128 | tf_op jit(solution)/shard_map/ppermute | solution.py:500
  61.0 13.9 %collective-permute-done.6.from_below = f32[5,20,8,512]{3,2,1,0:T(8,128)} collective-permute-done((f32[5,20,8,512]{3,2,1,0:T(8,128)}, f32[5,20,8,512]{3,2,1,0:T(8,128)}, u32[]{:S(2)}, u32[]{:S(2)}) %collective-permute-start.6) | collective-permute-done | bytes 1638432 | tf_op jit(solution)/shard_map/ppermute | solution.py:500
  74.9 0.2 collective-permute-done.7.from_above
  75.1 13.0 %main0.1 = (f32[3,2,64,4,512]{4,3,2,1,0:T(4,128)}, f32[3,2,64,4,512]{4,3,2,1,0:T(4,128)}) custom-call(f32[8,64,8,512]{3,2,1,0:T(8,128)} %get-tuple-element.28.u_hbm, f32[8,4,8,512]{3,2,1,0:T(8,128)} %get-tuple-element.29.edge_hbm, f32[64,8,512]{2,1,0:T(8,128)} %get-tuple-element.35.rho_ref, f32[64,8,512]{2,1,0:T(8,128)} %get-tuple-element.36.mz_ref, ...), custom_call_target="tpu_custom_call" | custom-call | flops 999999995904 | bytes 4000000000 | tf_op jit(solution)/shard_map/main0/pallas_call | solution.py:645
  88.1 0.0 all-to-all-done.1.w_ref
  88.1 6.9 %modes.1.rest_2_ = f32[2,4,128,512]{3,2,1,0:T(8,128)} custom-call(f32[4,2,4,128,128]{4,3,2,1,0:T(8,128)} %all-to-all-done.1.w_ref, bf16[512,512]{1,0:T(8,128)(2,1)} %constant.17.clone.ch_ref, bf16[512,512]{1,0:T(8,128)(2,1)} %constant.18.clone.cl_ref, bf16[512,512]{1,0:T(8,128)(2,1)} %constant.19.clone.sh_ref, bf16[512,512]{1,0:T(8,128)(2,1)} %constant.20.clone.sl_ref), custom_call_target="tpu_custom_call" | custom-call | flops 1000000 | bytes 100000 | tf_op jit(solution)/shard_map/modes/pallas_call | solution.py:626
  95.0 0.9 collective-permute-done.4.from_below
  95.9 0.0 collective-permute-done.5.from_above
  95.9 9.3 %main1.1 = (f32[3,2,64,4,512]{4,3,2,1,0:T(4,128)}, f32[3,2,64,4,512]{4,3,2,1,0:T(4,128)}) custom-call(f32[8,64,8,512]{3,2,1,0:T(8,128)} %get-tuple-element.28.u_hbm, f32[8,4,8,512]{3,2,1,0:T(8,128)} %get-tuple-element.29.edge_hbm, f32[64,8,512]{2,1,0:T(8,128)} %get-tuple-element.35.rho_ref, ...), custom_call_target="tpu_custom_call", output_to_operand_aliasing={{0}: (6, {}), {1}: (7, {})} | custom-call | flops 999999995904 | bytes 4000000000 | tf_op jit(solution)/shard_map/main1/pallas_call | solution.py:645
  (1 shorter events, 0.0 us)
Async XLA Ops:
  3.1 16.9 %collective-permute-start = (f32[8,2,4,512]{3,2,1,0:T(4,128)}, f32[8,2,4,512]{3,2,1,0:T(4,128)S(1)}, u32[]{:S(2)}, u32[]{:S(2)}) collective-permute-start(f32[8,2,4,512]{3,2,1,0:T(4,128)} %get-tuple-element.26), channel_id=1, source_target_pairs={{0,1},{1,2},{2,3},{3,0},{4,5},{5,6},{6,7},{7,4},{8,9},{9,10},{10,1... | collective-permute-start | bytes 393224 | tf_op jit(solution)/shard_map/ppermute | solution.py:500
  6.1 14.0 %collective-permute-start.1 = (f32[8,2,4,512]{3,2,1,0:T(4,128)}, f32[8,2,4,512]{3,2,1,0:T(4,128)S(1)}, u32[]{:S(2)}, u32[]{:S(2)}) collective-permute-start(f32[8,2,4,512]{3,2,1,0:T(4,128)} %get-tuple-element.27), channel_id=1, source_target_pairs={{0,3},{1,0},{2,1},{3,2},{4,7},{5,4},{6,5},{7,6},{8,11},{9,8},{10,9... | collective-permute-start | bytes 393224 | tf_op jit(solution)/shard_map/ppermute | solution.py:500
  7.0 13.0 %all-to-all-start = ((s32[32,1,128]{2,1,0:T(1,128)}), s32[32,1,128]{2,1,0:T(1,128)S(1)}, u32[]{:S(2)}, u32[]{:S(2)}) async-start(s32[32,1,128]{2,1,0:T(1,128)} %get-tuple-element.25.after_ref), calls=%async_computation | async-start | bytes 32768 | tf_op jit(solution)/shard_map/all_to_all | solution.py:548
  16.5 22.0 %collective-permute-start.2 = (f32[16,3,8,512]{3,2,1,0:T(8,128)}, f32[16,3,8,512]{3,2,1,0:T(8,128)}, u32[]{:S(2)}, u32[]{:S(2)}) collective-permute-start(f32[16,3,8,512]{3,2,1,0:T(8,128)} %get-tuple-element.30), channel_id=1, source_target_pairs={{0,4},{4,8},{8,12},{12,16},{16,20},{20,24},{24,28},{28,0},{1,5},{5... | collective-permute-start | bytes 2359304 | tf_op jit(solution)/shard_map/ppermute | solution.py:500
  16.7 21.8 %collective-permute-start.3 = (f32[16,3,8,512]{3,2,1,0:T(8,128)}, f32[16,3,8,512]{3,2,1,0:T(8,128)}, u32[]{:S(2)}, u32[]{:S(2)}) collective-permute-start(f32[16,3,8,512]{3,2,1,0:T(8,128)} %get-tuple-element.31), channel_id=1, source_target_pairs={{0,28},{4,0},{8,4},{12,8},{16,12},{20,16},{24,20},{28,24},{1,29},{... | collective-permute-start | bytes 2359304 | tf_op jit(solution)/shard_map/ppermute | solution.py:500
  20.0 0.6 copy-start
  20.0 0.7 copy-start.1
  20.1 0.7 copy-start.2
  34.9 40.0 %collective-permute-start.6 = (f32[5,20,8,512]{3,2,1,0:T(8,128)}, f32[5,20,8,512]{3,2,1,0:T(8,128)}, u32[]{:S(2)}, u32[]{:S(2)}) collective-permute-start(f32[5,20,8,512]{3,2,1,0:T(8,128)} %get-tuple-element.39), channel_id=1, source_target_pairs={{0,4},{4,8},{8,12},{12,16},{16,20},{20,24},{24,28},{28,0},{1,5},{5... | collective-permute-start | bytes 4915208 | tf_op jit(solution)/shard_map/ppermute | solution.py:500
  35.0 40.1 %collective-permute-start.7 = (f32[5,20,8,512]{3,2,1,0:T(8,128)}, f32[5,20,8,512]{3,2,1,0:T(8,128)}, u32[]{:S(2)}, u32[]{:S(2)}) collective-permute-start(f32[5,20,8,512]{3,2,1,0:T(8,128)} %get-tuple-element.40), channel_id=1, source_target_pairs={{0,28},{4,0},{8,4},{12,8},{16,12},{20,16},{24,20},{28,24},{1,29},{... | collective-permute-start | bytes 4915208 | tf_op jit(solution)/shard_map/ppermute | solution.py:500
  52.8 35.2 %all-to-all-start.1 = ((f32[4,2,4,128,128]{4,3,2,1,0:T(8,128)}), f32[4,2,4,128,128]{4,3,2,1,0:T(8,128)}, u32[]{:S(2)}, u32[]{:S(2)}) async-start(f32[4,2,4,128,128]{4,3,2,1,0:T(8,128)} %get-tuple-element.43), calls=%async_computation.1 | async-start | bytes 4194304 | tf_op jit(solution)/shard_map/all_to_all | solution.py:623
  57.4 38.6 %collective-permute-start.4 = (f32[3,20,8,512]{3,2,1,0:T(8,128)}, f32[3,20,8,512]{3,2,1,0:T(8,128)}, u32[]{:S(2)}, u32[]{:S(2)}) collective-permute-start(f32[3,20,8,512]{3,2,1,0:T(8,128)} %get-tuple-element.37), channel_id=1, source_target_pairs={{0,4},{4,8},{8,12},{12,16},{16,20},{20,24},{24,28},{28,0},{1,5},{5... | collective-permute-start | bytes 2949128 | tf_op jit(solution)/shard_map/ppermute | solution.py:500
  57.4 38.5 %collective-permute-start.5 = (f32[3,20,8,512]{3,2,1,0:T(8,128)}, f32[3,20,8,512]{3,2,1,0:T(8,128)}, u32[]{:S(2)}, u32[]{:S(2)}) collective-permute-start(f32[3,20,8,512]{3,2,1,0:T(8,128)} %get-tuple-element.38), channel_id=1, source_target_pairs={{0,28},{4,0},{8,4},{12,8},{16,12},{20,16},{24,20},{28,24},{1,29},{... | collective-permute-start | bytes 2949128 | tf_op jit(solution)/shard_map/ppermute | solution.py:500

commit v3 on v2

--- a/solution.py
+++ b/solution.py
@@ -289,13 +289,13 @@
 
 def density_kernel(
     u_hbm, edge_hbm, below_ref, above_ref, sb_ref, sa_ref, order_ref, high_ref, low_ref, out_ref, wave_ref,
-    rho_out, mz_out, *rest,
+    rho_out, mz_out, *rest, begin,
 ):
     *parcel, d_ref, u_ref, b_ref, sem = rest
     half = u_hbm.shape[1]
     field = None
     if parcel:
-        field = pltpu.make_async_copy(u_hbm.at[4:7, half - b_ref.shape[1] :], b_ref, sem.at[3])
+        field = pltpu.make_async_copy(u_hbm.at[4:7, begin : begin + b_ref.shape[1]], b_ref, sem.at[3])
         field.start()
     fetch(u_hbm, edge_hbm, u_ref, sem, 0)
     rows = 2 * half
@@ -337,15 +337,19 @@
     if not parcel:
         return
     field.wait()
-    first = half - b_ref.shape[1]
-
-    def messages(n, _):
-        r = n * 4
-        state = lambda j: [u_ref[f, first + r + j + 2] for f in range(4)] + [b_ref[c, r + j] for c in range(3)]
-        write_messages(*parcel, n // 2, n % 2, state)
-        return 0
-
-    lax.fori_loop(0, b_ref.shape[1] // 4, messages, 0)
+    first = begin
+
+    row = 0
+    for up_ref, down_ref in zip(parcel[: len(parcel) // 2], parcel[len(parcel) // 2 :]):
+
+        def messages(n, _, up_ref=up_ref, down_ref=down_ref, row=row):
+            r = n * 4 + row
+            state = lambda j: [u_ref[f, first + r + j + 2] for f in range(4)] + [b_ref[c, r + j] for c in range(3)]
+            write_messages(up_ref, down_ref, n // 2, n % 2, state)
+            return 0
+
+        lax.fori_loop(0, up_ref.shape[0] * 2, messages, 0)
+        row += up_ref.shape[0] * 8
 
 
 def last_plane(below, above, j):
@@ -356,7 +360,12 @@
     return jnp.where(sub == 7, turn(above, 6 - 2 * j, 0), out)
 
 
-def main_kernel(u_hbm, edge_hbm, rho_ref, mz_ref, from_below, from_above, *rest, first):
+def main_kernel(u_hbm, edge_hbm, rho_ref, mz_ref, from_below, from_above, *rest, first, emit):
+    if emit:
+        *rest, later_ref, later_sem = rest
+        *rest, up_ref, down_ref, u_ref, f_ref, sem = rest
+        rest = [*rest, u_ref, f_ref, sem]
+        later = pltpu.make_async_copy(u_hbm.at[:7, u_hbm.shape[1] - later_ref.shape[1] :], later_ref, later_sem)
     mom_ref, mag_ref, u_ref, f_ref, sem = rest[-5:]
     chunk, total, half = rho_ref.shape[0], u_ref.shape[1], u_hbm.shape[1]
     step_id = pl.program_id(0)
@@ -380,6 +389,8 @@
         for i in range(total // chunk):
             for copy in copies(i):
                 copy.start()
+        if emit:
+            later.start()
 
     for i in range(total // chunk):
 
@@ -441,6 +452,19 @@
 
     lax.fori_loop(0, chunk // 4, body, 0)
 
+    if emit:
+
+        @pl.when(step_id == pl.num_programs(0) - 1)
+        def _():
+            later.wait()
+
+            def messages(n, _):
+                state = lambda j: [later_ref[f, n * 4 + j] for f in range(7)]
+                write_messages(up_ref, down_ref, n // 2, n % 2, state)
+                return 0
+
+            lax.fori_loop(0, later_ref.shape[1] // 4, messages, 0)
+
 
 def modes_kernel(w_ref, ch_ref, cl_ref, sh_ref, sl_ref, out_ref, x_ref, *, turned):
     dot = functools.partial(jnp.dot, preferred_element_type=jnp.float32)
@@ -515,7 +539,7 @@
     message = shape((2, half, planes, ny), f32)
     tile = shape((half, 8, ny), f32)
     steps = half // 8
-    counts = (steps * 5 // 8, steps - steps * 5 // 8) if steps >= 2 else (steps,)
+    counts = (steps - steps // 4 * 2, steps // 4, steps // 4) if steps >= 4 else (steps,)
 
     slots_here = sn_cells.shape[0]
     rho = density.reshape(2, half, planes, ny)
@@ -599,15 +623,15 @@
     band = ny // across
     turned = band % 128 != 0 or rows % 128 != 0
     hbm = pl.BlockSpec(memory_space=pl.ANY)
-    more = parcels[1:] * 2
+    more = parcels[1:2] * 2
     new_density, wave, rho_halo, mz_halo, *messages = pl.pallas_call(
-        density_kernel,
+        functools.partial(density_kernel, begin=counts[0] * 8),
         in_specs=[hbm, hbm] + [whole] * 7,
         out_specs=[whole] * (4 + len(more)),
         out_shape=[message, shape((across, 2, planes, rows, band), f32), tile, tile, *more],
         scratch_shapes=[
             pltpu.VMEM((8 * half, ny), f32), pltpu.VMEM((4, half + 4, 8, ny), f32),
-            pltpu.VMEM((3, counts[-1] * 8, 8, ny), f32), pltpu.SemaphoreType.DMA((4,)),
+            pltpu.VMEM((3, counts[min(1, len(counts) - 1)] * 8, 8, ny), f32), pltpu.SemaphoreType.DMA((4,)),
         ],
         compiler_params=params,
         cost_estimate=cost(*DENSITY_COST),
@@ -617,9 +641,9 @@
         np.stack([cos_high, -sin_high]), np.stack([cos_low, -sin_low]),
     )
 
-    if messages:
-        parcels_below.append(shift(messages[0], "gz", 1))
-        parcels_above.append(shift(messages[1], "gz", -1))
+    for up, down in zip(messages[: len(messages) // 2], messages[len(messages) // 2 :]):
+        parcels_below.append(shift(up, "gz", 1))
+        parcels_above.append(shift(down, "gz", -1))
     portion = lax.all_to_all(wave, "xy", split_axis=0, concat_axis=0, tiled=True)
     if turned:
         portion = portion.transpose(1, 2, 4, 0, 3).reshape(2, planes, band, NX)
@@ -636,26 +660,33 @@
     results = [shape((3, 2, half, planes, ny), f32)] * 2
     new = []
     for i, n in enumerate(counts):
+        emit = i == 0 and len(counts) == 3
+        sent = parcels[2:] * 2 if emit else []
+        if i == 2:
+            parcels_below.append(shift(messages[0], "gz", 1))
+            parcels_above.append(shift(messages[1], "gz", -1))
         chunk, first = 8, begins[i] * 8
         here = pl.BlockSpec((chunk, 8, ny), lambda k, o=begins[i]: (o + k, 0, 0))
         parcel = pl.BlockSpec((1, 20, 8, ny), lambda k: (k, 0, 0, 0))
         three = pl.BlockSpec((3, 2, chunk, planes, ny), lambda k, o=begins[i]: (0, 0, o + k, 0, 0))
         below, above = parcels_below[i], parcels_above[i]
         extra = [*new] + [modes] * (i > 0 and i == len(counts) - 1)
-        new = pl.pallas_call(
-            functools.partial(main_kernel, first=first),
+        *new, = pl.pallas_call(
+            functools.partial(main_kernel, first=first, emit=emit),
             grid=(n,),
             in_specs=[hbm, hbm] + [here] * 2 + [parcel] * 2 + [hbm] * len(extra),
-            out_specs=[three, three],
-            out_shape=results,
+            out_specs=[three, three] + [full(p.shape) for p in sent],
+            out_shape=results + sent,
             scratch_shapes=[
                 pltpu.VMEM((8, n * 8 + 4, 8, ny), f32), pltpu.VMEM((5, n * 8 + 4, 8, ny), f32), pltpu.SemaphoreType.DMA((n + 2,)),
-            ],
+            ] + ([pltpu.VMEM((7, counts[2] * 8, 8, ny), f32), pltpu.SemaphoreType.DMA] if emit else []),
             input_output_aliases={6: 0, 7: 1} if new else {},
             compiler_params=pltpu.CompilerParams(vmem_limit_bytes=62 * 1024 * 1024),
             cost_estimate=cost(*MAIN_COST),
             name=f"main{i}",
         )(state, edge, rho_halo, mz_halo, below, above, *extra)
+        if emit:
+            new, messages = new[:2], new[2:]
     new_mom, new_mag = new
 
     return (

time: 106 us -> 106 us (level)
  waiting for transfers between devices: 15.1 us -> 7.9 us
  starting transfers between devices: 24.6 us -> 28.9 us
  Pallas kernels: 63.5 us -> 66 us
    ppermute x8 -> x10, waiting for transfers between devices: 15.1 us -> 7.89 us  [shift(): return lax.ppermute(block, axis, [(i, (i + step) % n) for i in range(n)])]
    pallas_call x3 -> x4, Pallas kernels: 36.5 us -> 40.5 us  [the longest x3 26.9 us: on_device(): pl.pallas_call(functools.partial(main_kernel, first=first, emit=emit), gr...]
    ppermute x8 -> x10, starting transfers between devices: 14.6 us -> 18.4 us  [shift(): return lax.ppermute(block, axis, [(i, (i + step) % n) for i in range(n)])]
    pallas_call x1, Pallas kernels: 14.2 us -> 12.7 us  [on_device(): pl.pallas_call(functools.partial(state_kernel, depth=planes * layers, cou...]
  transfers between devices with their start and end apart: 10 -> 12, of which waited for: 3 -> 4; matrix products, arithmetic and copies ran while one was open for 0% -> 0% of each run, Pallas kernels for 50% -> 54%
where the time goes in v3:
time: 106 us; the launch traced here: 105 us
  Pallas kernels  66 us (62%)
  starting transfers between devices  28.9 us (27%)
  waiting for transfers between devices  7.9 us (7%)
  between operations  1.37 us (1%)
    pallas_call x3, Pallas kernels, on_device(): pl.pallas_call(functools.partial(main_kernel, first=first, emit=emit), gr...  26.9 us
    ppermute x10, starting transfers between devices, shift(): return lax.ppermute(block, axis, [(i, (i + step) % n) for i in range(n)])  18.4 us
    pallas_call x1, Pallas kernels, on_device(): pl.pallas_call(functools.partial(density_kernel, begin=counts[0] * 8), in...  13.7 us
    pallas_call x1, Pallas kernels, on_device(): pl.pallas_call(functools.partial(state_kernel, depth=planes * layers, cou...  12.7 us
    ppermute x10, waiting for transfers between devices, shift(): return lax.ppermute(block, axis, [(i, (i + step) % n) for i in range(n)])  7.89 us
    pallas_call x1, Pallas kernels, on_device(): pl.pallas_call(functools.partial(modes_kernel, turned=turned), in_specs=[...  6.93 us
    all_to_all x1, starting transfers between devices, on_device(): lax.all_to_all(mine, ('gz', 'xy'), split_axis=0, concat_axis=0, tiled=True)  5.43 us
    all_to_all x1, starting transfers between devices, on_device(): lax.all_to_all(wave, 'xy', split_axis=0, concat_axis=0, tiled=True)  5.02 us
  transfers between devices with their start and end apart: 12, of which 4 were waited for; matrix products, arithmetic and copies ran while one was open for 0% of the time, Pallas kernels for 54%

profile of v3, /device:TPU:0, one launch (start us, length us, event | category | flops | bytes accessed | tf_op | source)
XLA Modules:
  0.0 104.8 jit_solution(17952435538952274764)
XLA Ops:
  1.3 1.8 %first.1 = (s32[32,1,128]{2,1,0:T(1,128)}, f32[8,2,4,512]{3,2,1,0:T(4,128)}, f32[8,2,4,512]{3,2,1,0:T(4,128)}) custom-call(s32[1,3]{1,0:T(1,128)} %cell_ref.1, s32[1]{0:T(128)S(6)} %copy.25.count_ref, f32[2,64,4,512]{3,2,1,0:T(4,128)} %bitcast.18, f32[3,2,64,4,512]{4,3,2,1,0:T(4,128)} %bitcast.7, f32[3,2,64,4,512]{4,3,2,1,0:T(4,128)} %bitcast.13, ...), custom_call_target="tpu_custom_call" | custom-call | flops 1000000 | bytes 100000 | tf_op jit(solution)/shard_map/first/pallas_call | solution.py:553
  3.1 2.9 %collective-permute-start = (f32[8,2,4,512]{3,2,1,0:T(4,128)}, f32[8,2,4,512]{3,2,1,0:T(4,128)S(1)}, u32[]{:S(2)}, u32[]{:S(2)}) collective-permute-start(f32[8,2,4,512]{3,2,1,0:T(4,128)} %get-tuple-element.30), channel_id=1, source_target_pairs={{0,1},{1,2},{2,3},{3,0},{4,5},{5,6},{6,7},{7,4},{8,9},{9,10},{10,1... | collective-permute-start | bytes 393224 | tf_op jit(solution)/shard_map/ppermute | solution.py:524
  6.1 1.0 collective-permute-start.1
  7.0 5.4 %all-to-all-start = ((s32[32,1,128]{2,1,0:T(1,128)}), s32[32,1,128]{2,1,0:T(1,128)S(1)}, u32[]{:S(2)}, u32[]{:S(2)}) async-start(s32[32,1,128]{2,1,0:T(1,128)} %get-tuple-element.29.after_ref), calls=%async_computation | async-start | bytes 32768 | tf_op jit(solution)/shard_map/all_to_all | solution.py:572
  12.5 4.0 %pack.1 = (f32[16,3,8,512]{3,2,1,0:T(8,128)}, f32[16,3,8,512]{3,2,1,0:T(8,128)}) custom-call(f32[2,64,4,512]{3,2,1,0:T(4,128)} %bitcast.20, f32[3,2,64,4,512]{4,3,2,1,0:T(4,128)} %bitcast.9, s32[32,1,128]{2,1,0:T(1,128)} %get-tuple-element.29.after_ref), custom_call_target="tpu_custom_call" | custom-call | flops 1000000 | bytes 100000 | tf_op jit(solution)/shard_map/pack/pallas_call | solution.py:576
  16.5 0.3 collective-permute-start.2
  16.7 3.3 %collective-permute-start.3 = (f32[16,3,8,512]{3,2,1,0:T(8,128)}, f32[16,3,8,512]{3,2,1,0:T(8,128)}, u32[]{:S(2)}, u32[]{:S(2)}) collective-permute-start(f32[16,3,8,512]{3,2,1,0:T(8,128)} %get-tuple-element.35), channel_id=1, source_target_pairs={{0,28},{4,0},{8,4},{12,8},{16,12},{20,16},{24,20},{28,24},{1,29},{... | collective-permute-start | bytes 2359304 | tf_op jit(solution)/shard_map/ppermute | solution.py:524
  20.0 0.0 all-to-all-done.ev_ref
  20.0 0.0 collective-permute-done.before_ref
  20.1 0.0 collective-permute-done.1.after_ref
  20.1 0.6 copy-done
  20.6 0.1 copy-done.1
  20.7 0.0 copy-done.2
  20.7 12.7 %state.1 = (f32[8,64,8,512]{3,2,1,0:T(8,128)}, f32[8,4,8,512]{3,2,1,0:T(8,128)}, f32[64,8,512]{2,1,0:T(8,128)}, f32[64,8,512]{2,1,0:T(8,128)}, f32[4,20,8,512]{3,2,1,0:T(8,128)}, /*index=5*/f32[4,20,8,512]{3,2,1,0:T(8,128)}) custom-call(s32[32,1,128]{2,1,0:T(1,128)} %copy-done, f32[2,64,4,512]{3,2,1,0:T(4,128)} %bitcast.21, f32[3,2,64,4,512]{4,3,2,1,0:T(4,128)} %bitcast.10, ...), custom_call_target="tpu_custom_call" | custom-call | flops 999999995904 | bytes 4000000000 | tf_op jit(solution)/shard_map/state/pallas_call | solution.py:606
  33.4 0.1 collective-permute-start.4
  33.5 3.5 %collective-permute-start.5 = (f32[4,20,8,512]{3,2,1,0:T(8,128)}, f32[4,20,8,512]{3,2,1,0:T(8,128)}, u32[]{:S(2)}, u32[]{:S(2)}) collective-permute-start(f32[4,20,8,512]{3,2,1,0:T(8,128)} %get-tuple-element.42), channel_id=1, source_target_pairs={{0,28},{4,0},{8,4},{12,8},{16,12},{20,16},{24,20},{28,24},{1,29},{... | collective-permute-start | bytes 3932168 | tf_op jit(solution)/shard_map/ppermute | solution.py:524
  37.0 0.0 collective-permute-done.2.below_ref
  37.0 0.3 collective-permute-done.3.above_ref
  37.3 13.7 %density.1 = (f32[2,64,4,512]{3,2,1,0:T(4,128)}, f32[4,2,4,128,128]{4,3,2,1,0:T(8,128)}, f32[64,8,512]{2,1,0:T(8,128)}, f32[64,8,512]{2,1,0:T(8,128)}, f32[2,20,...) custom-call(f32[8,64,8,512]{3,2,1,0:T(8,128)} %get-tuple-element.32.u_hbm, f32[8,4,8,512]{3,2,1,0:T(8,128)} %get-tuple-element.33.edge_hbm, ...), custom_call_target="tpu_custom_call" | custom-call | flops 999999995904 | bytes 4000000000 | tf_op jit(solution)/shard_map/density/pallas_call | solution.py:627
  51.0 5.0 %all-to-all-start.1 = ((f32[4,2,4,128,128]{4,3,2,1,0:T(8,128)}), f32[4,2,4,128,128]{4,3,2,1,0:T(8,128)}, u32[]{:S(2)}, u32[]{:S(2)}) async-start(f32[4,2,4,128,128]{4,3,2,1,0:T(8,128)} %get-tuple-element.51), calls=%async_computation.1 | async-start | bytes 4194304 | tf_op jit(solution)/shard_map/all_to_all | solution.py:647
  56.0 0.5 collective-permute-start.8
  56.5 3.1 %collective-permute-start.9 = (f32[2,20,8,512]{3,2,1,0:T(8,128)}, f32[2,20,8,512]{3,2,1,0:T(8,128)}, u32[]{:S(2)}, u32[]{:S(2)}) collective-permute-start(f32[2,20,8,512]{3,2,1,0:T(8,128)} %get-tuple-element.46), channel_id=1, source_target_pairs={{0,28},{4,0},{8,4},{12,8},{16,12},{20,16},{24,20},{28,24},{1,29},{... | collective-permute-start | bytes 1966088 | tf_op jit(solution)/shard_map/ppermute | solution.py:524
  59.6 6.8 %collective-permute-done.4.from_below = f32[4,20,8,512]{3,2,1,0:T(8,128)} collective-permute-done((f32[4,20,8,512]{3,2,1,0:T(8,128)}, f32[4,20,8,512]{3,2,1,0:T(8,128)}, u32[]{:S(2)}, u32[]{:S(2)}) %collective-permute-start.4) | collective-permute-done | bytes 1310752 | tf_op jit(solution)/shard_map/ppermute | solution.py:524
  66.3 0.2 collective-permute-done.5.from_above
  66.6 12.1 %main0.1 = (f32[3,2,64,4,512]{4,3,2,1,0:T(4,128)}, f32[3,2,64,4,512]{4,3,2,1,0:T(4,128)}, f32[2,20,8,512]{3,2,1,0:T(8,128)}, f32[2,20,8,512]{3,2,1,0:T(8,128)}) custom-call(f32[8,64,8,512]{3,2,1,0:T(8,128)} %get-tuple-element.32.u_hbm, f32[8,4,8,512]{3,2,1,0:T(8,128)} %get-tuple-element.33.edge_hbm, f32[64,8,512]{2,1,0:T(8,128)} %get-tuple-element.39.rho_ref, ...), custom_call_target="tpu_custom_call" | custom-call | flops 999999995904 | bytes 4000000000 | tf_op jit(solution)/shard_map/main0/pallas_call | solution.py:674
  78.7 0.3 collective-permute-start.6
  79.0 3.5 %collective-permute-start.7 = (f32[2,20,8,512]{3,2,1,0:T(8,128)}, f32[2,20,8,512]{3,2,1,0:T(8,128)}, u32[]{:S(2)}, u32[]{:S(2)}) collective-permute-start(f32[2,20,8,512]{3,2,1,0:T(8,128)} %get-tuple-element.44), channel_id=1, source_target_pairs={{0,28},{4,0},{8,4},{12,8},{16,12},{20,16},{24,20},{28,24},{1,29},{... | collective-permute-start | bytes 1966088 | tf_op jit(solution)/shard_map/ppermute | solution.py:524
  82.5 7.4 %main1.1 = (f32[3,2,64,4,512]{4,3,2,1,0:T(4,128)}, f32[3,2,64,4,512]{4,3,2,1,0:T(4,128)}) custom-call(f32[8,64,8,512]{3,2,1,0:T(8,128)} %get-tuple-element.32.u_hbm, f32[8,4,8,512]{3,2,1,0:T(8,128)} %get-tuple-element.33.edge_hbm, f32[64,8,512]{2,1,0:T(8,128)} %get-tuple-element.39.rho_ref, ...), custom_call_target="tpu_custom_call", output_to_operand_aliasing={{0}: (6, {}), {1}: (7, {})} | custom-call | flops 999999995904 | bytes 4000000000 | tf_op jit(solution)/shard_map/main1/pallas_call | solution.py:674
  89.9 0.0 all-to-all-done.1.w_ref
  89.9 6.9 %modes.1.rest_2_ = f32[2,4,128,512]{3,2,1,0:T(8,128)} custom-call(f32[4,2,4,128,128]{4,3,2,1,0:T(8,128)} %all-to-all-done.1.w_ref, bf16[512,512]{1,0:T(8,128)(2,1)} %constant.17.clone.ch_ref, bf16[512,512]{1,0:T(8,128)(2,1)} %constant.18.clone.cl_ref, bf16[512,512]{1,0:T(8,128)(2,1)} %constant.19.clone.sh_ref, bf16[512,512]{1,0:T(8,128)(2,1)} %constant.20.clone.sl_ref), custom_call_target="tpu_custom_call" | custom-call | flops 1000000 | bytes 100000 | tf_op jit(solution)/shard_map/modes/pallas_call | solution.py:650
  96.9 0.6 collective-permute-done.6.from_below
  97.4 7.4 %main2.1 = (f32[3,2,64,4,512]{4,3,2,1,0:T(4,128)}, f32[3,2,64,4,512]{4,3,2,1,0:T(4,128)}) custom-call(f32[8,64,8,512]{3,2,1,0:T(8,128)} %get-tuple-element.32.u_hbm, f32[8,4,8,512]{3,2,1,0:T(8,128)} %get-tuple-element.33.edge_hbm, f32[64,8,512]{2,1,0:T(8,128)} %get-tuple-element.39.rho_ref, ...), custom_call_target="tpu_custom_call", output_to_operand_aliasing={{0}: (6, {}), {1}: (7, {})} | custom-call | flops 999999995904 | bytes 4000000000 | tf_op jit(solution)/shard_map/main2/pallas_call | solution.py:674
  (6 shorter events, 0.0 us)
Async XLA Ops:
  3.1 16.9 %collective-permute-start = (f32[8,2,4,512]{3,2,1,0:T(4,128)}, f32[8,2,4,512]{3,2,1,0:T(4,128)S(1)}, u32[]{:S(2)}, u32[]{:S(2)}) collective-permute-start(f32[8,2,4,512]{3,2,1,0:T(4,128)} %get-tuple-element.30), channel_id=1, source_target_pairs={{0,1},{1,2},{2,3},{3,0},{4,5},{5,6},{6,7},{7,4},{8,9},{9,10},{10,1... | collective-permute-start | bytes 393224 | tf_op jit(solution)/shard_map/ppermute | solution.py:524
  6.1 14.0 %collective-permute-start.1 = (f32[8,2,4,512]{3,2,1,0:T(4,128)}, f32[8,2,4,512]{3,2,1,0:T(4,128)S(1)}, u32[]{:S(2)}, u32[]{:S(2)}) collective-permute-start(f32[8,2,4,512]{3,2,1,0:T(4,128)} %get-tuple-element.31), channel_id=1, source_target_pairs={{0,3},{1,0},{2,1},{3,2},{4,7},{5,4},{6,5},{7,6},{8,11},{9,8},{10,9... | collective-permute-start | bytes 393224 | tf_op jit(solution)/shard_map/ppermute | solution.py:524
  7.0 13.0 %all-to-all-start = ((s32[32,1,128]{2,1,0:T(1,128)}), s32[32,1,128]{2,1,0:T(1,128)S(1)}, u32[]{:S(2)}, u32[]{:S(2)}) async-start(s32[32,1,128]{2,1,0:T(1,128)} %get-tuple-element.29.after_ref), calls=%async_computation | async-start | bytes 32768 | tf_op jit(solution)/shard_map/all_to_all | solution.py:572
  16.5 20.5 %collective-permute-start.2 = (f32[16,3,8,512]{3,2,1,0:T(8,128)}, f32[16,3,8,512]{3,2,1,0:T(8,128)}, u32[]{:S(2)}, u32[]{:S(2)}) collective-permute-start(f32[16,3,8,512]{3,2,1,0:T(8,128)} %get-tuple-element.34), channel_id=1, source_target_pairs={{0,4},{4,8},{8,12},{12,16},{16,20},{20,24},{24,28},{28,0},{1,5},{5... | collective-permute-start | bytes 2359304 | tf_op jit(solution)/shard_map/ppermute | solution.py:524
  16.7 20.6 %collective-permute-start.3 = (f32[16,3,8,512]{3,2,1,0:T(8,128)}, f32[16,3,8,512]{3,2,1,0:T(8,128)}, u32[]{:S(2)}, u32[]{:S(2)}) collective-permute-start(f32[16,3,8,512]{3,2,1,0:T(8,128)} %get-tuple-element.35), channel_id=1, source_target_pairs={{0,28},{4,0},{8,4},{12,8},{16,12},{20,16},{24,20},{28,24},{1,29},{... | collective-permute-start | bytes 2359304 | tf_op jit(solution)/shard_map/ppermute | solution.py:524
  20.0 0.6 copy-start
  20.0 0.7 copy-start.1
  20.1 0.7 copy-start.2
  33.4 32.9 %collective-permute-start.4 = (f32[4,20,8,512]{3,2,1,0:T(8,128)}, f32[4,20,8,512]{3,2,1,0:T(8,128)}, u32[]{:S(2)}, u32[]{:S(2)}) collective-permute-start(f32[4,20,8,512]{3,2,1,0:T(8,128)} %get-tuple-element.41), channel_id=1, source_target_pairs={{0,4},{4,8},{8,12},{12,16},{16,20},{20,24},{24,28},{28,0},{1,5},{5... | collective-permute-start | bytes 3932168 | tf_op jit(solution)/shard_map/ppermute | solution.py:524
  33.5 33.1 %collective-permute-start.5 = (f32[4,20,8,512]{3,2,1,0:T(8,128)}, f32[4,20,8,512]{3,2,1,0:T(8,128)}, u32[]{:S(2)}, u32[]{:S(2)}) collective-permute-start(f32[4,20,8,512]{3,2,1,0:T(8,128)} %get-tuple-element.42), channel_id=1, source_target_pairs={{0,28},{4,0},{8,4},{12,8},{16,12},{20,16},{24,20},{28,24},{1,29},{... | collective-permute-start | bytes 3932168 | tf_op jit(solution)/shard_map/ppermute | solution.py:524
  51.0 38.9 %all-to-all-start.1 = ((f32[4,2,4,128,128]{4,3,2,1,0:T(8,128)}), f32[4,2,4,128,128]{4,3,2,1,0:T(8,128)}, u32[]{:S(2)}, u32[]{:S(2)}) async-start(f32[4,2,4,128,128]{4,3,2,1,0:T(8,128)} %get-tuple-element.51), calls=%async_computation.1 | async-start | bytes 4194304 | tf_op jit(solution)/shard_map/all_to_all | solution.py:647
  56.0 26.5 %collective-permute-start.8 = (f32[2,20,8,512]{3,2,1,0:T(8,128)}, f32[2,20,8,512]{3,2,1,0:T(8,128)}, u32[]{:S(2)}, u32[]{:S(2)}) collective-permute-start(f32[2,20,8,512]{3,2,1,0:T(8,128)} %get-tuple-element.45), channel_id=1, source_target_pairs={{0,4},{4,8},{8,12},{12,16},{16,20},{20,24},{24,28},{28,0},{1,5},{5... | collective-permute-start | bytes 1966088 | tf_op jit(solution)/shard_map/ppermute | solution.py:524
  56.5 26.0 %collective-permute-start.9 = (f32[2,20,8,512]{3,2,1,0:T(8,128)}, f32[2,20,8,512]{3,2,1,0:T(8,128)}, u32[]{:S(2)}, u32[]{:S(2)}) collective-permute-start(f32[2,20,8,512]{3,2,1,0:T(8,128)} %get-tuple-element.46), channel_id=1, source_target_pairs={{0,28},{4,0},{8,4},{12,8},{16,12},{20,16},{24,20},{28,24},{1,29},{... | collective-permute-start | bytes 1966088 | tf_op jit(solution)/shard_map/ppermute | solution.py:524
  78.7 18.7 %collective-permute-start.6 = (f32[2,20,8,512]{3,2,1,0:T(8,128)}, f32[2,20,8,512]{3,2,1,0:T(8,128)}, u32[]{:S(2)}, u32[]{:S(2)}) collective-permute-start(f32[2,20,8,512]{3,2,1,0:T(8,128)} %get-tuple-element.43), channel_id=1, source_target_pairs={{0,4},{4,8},{8,12},{12,16},{16,20},{20,24},{24,28},{28,0},{1,5},{5... | collective-permute-start | bytes 1966088 | tf_op jit(solution)/shard_map/ppermute | solution.py:524
  79.0 18.4 %collective-permute-start.7 = (f32[2,20,8,512]{3,2,1,0:T(8,128)}, f32[2,20,8,512]{3,2,1,0:T(8,128)}, u32[]{:S(2)}, u32[]{:S(2)}) collective-permute-start(f32[2,20,8,512]{3,2,1,0:T(8,128)} %get-tuple-element.44), channel_id=1, source_target_pairs={{0,28},{4,0},{8,4},{12,8},{16,12},{20,16},{24,20},{28,24},{1,29},{... | collective-permute-start | bytes 1966088 | tf_op jit(solution)/shard_map/ppermute | solution.py:524

commit v4 on v2

--- a/solution.py
+++ b/solution.py
@@ -127,14 +127,14 @@
 def state_kernel(
     ev_ref, rho_ref, mom_ref, mag_ref, pot_ref, before_ref, after_ref, rho_l, mom_l, mag_l, pot_l,
     rho_h, mom_h, mag_h, pot_h, u_out, edge_out, sb_out, sa_out, up_ref, down_ref, s_ref, sb_ref, sa_ref, *,
-    depth, count, per_device,
+    depth, count, per_device, steps,
 ):
-    half, ny = s_ref.shape[1] - 4, s_ref.shape[3]
+    half, ny = 8 * steps, s_ref.shape[3]
     step_id = pl.program_id(0)
 
     @pl.when(step_id == 0)
     def _():
-        deposit(ev_ref, s_ref, sb_ref, sa_ref, depth, per_device)
+        deposit(ev_ref, s_ref, sb_ref, sa_ref, depth, per_device, half)
         pieces = lambda rho, mom, mag, pot, j: (
             [rho[0, j]] + [mom[c, 0, j] for c in range(3)] + [mag[c, 0, j] for c in range(3)]
             + [jnp.broadcast_to(pot, (4, ny))]
@@ -181,15 +181,15 @@
         lax.fori_loop(0, 2, lambda g, _: body(g, False), 0)
 
 
-def deposit(ev_ref, s_ref, sb_ref, sa_ref, depth, per_device):
-    half, ny = s_ref.shape[1] - 4, s_ref.shape[3]
+def deposit(ev_ref, s_ref, sb_ref, sa_ref, depth, per_device, half):
+    ny = s_ref.shape[3]
     rows, events = 2 * half, ev_ref.shape[0] * per_device
     row_start, plane_start = lax.axis_index("xy") * rows, lax.axis_index("gz") * 4
     s_ref[...] = jnp.zeros_like(s_ref)
     sb_ref[...] = jnp.zeros_like(sb_ref)
     sa_ref[...] = jnp.zeros_like(sa_ref)
 
-    shape = (4, 8, 128)
+    shape = (8, 8, 128)
     slot = slots(shape)
     sub = lax.broadcasted_iota(jnp.int32, shape, 1)
     step = lax.broadcasted_iota(jnp.int32, shape, 0)
@@ -222,12 +222,12 @@
                 dy2 = dy * dy
                 for h in range(2):
                     weight = jnp.where((sub >= 4) == (h == 1), count, 0).astype(jnp.float32)
-                    low = jnp.clip(rel - RADIUS + 1 - h * half + 2, 0, half + 4) // 4
-                    high = (jnp.clip(rel + RADIUS - 1 - h * half + 2, -1, half + 3) + 4) // 4
+                    low = jnp.clip(rel - RADIUS + 1 - h * half + 2, 0, s_ref.shape[1]) // 8
+                    high = (jnp.clip(rel + RADIUS - 1 - h * half + 2, -1, half + 3) + 8) // 8
 
                     def chunk(n, _):
-                        q = pl.ds(n * 4, 4)
-                        dx = (step + (n * 4 - 2 + h * half - rel)).astype(jnp.float32)
+                        q = pl.ds(n * 8, 8)
+                        dx = (step + (n * 8 - 2 + h * half - rel)).astype(jnp.float32)
                         flat = dx * dx + dy2
                         size = lambda d: jnp.maximum(1.0 - (flat + d * d) * (1.0 / (RADIUS * RADIUS)), 0.0) * weight
                         w = size(dz)
@@ -442,11 +442,11 @@
     lax.fori_loop(0, chunk // 4, body, 0)
 
 
-def modes_kernel(w_ref, ch_ref, cl_ref, sh_ref, sl_ref, out_ref, x_ref, *, turned):
+def modes_kernel(w_ref, ch_ref, cl_ref, mh_ref, ml_ref, ph_ref, pl_ref, out_ref, x_ref, *, turned):
     dot = functools.partial(jnp.dot, preferred_element_type=jnp.float32)
     planes, band, nx = out_ref.shape[1:]
 
-    def split(part):
+    def gathered(part):
         if turned:
             x = jnp.concatenate([w_ref[part, z] for z in range(planes)], axis=0)
         else:
@@ -455,18 +455,22 @@
                 for z in range(planes):
                     x_ref[z * band : (z + 1) * band, s * width : (s + 1) * width] = w_ref[s, part, z].T
             x = x_ref[...]
+        return x
+
+    def split(x):
         high = x.astype(jnp.bfloat16)
         return high, (x - high.astype(jnp.float32)).astype(jnp.bfloat16)
 
-    re, im = split(0), split(1)
+    re, im = gathered(0), gathered(1)
     times = lambda x, h, l: dot(x[0], h[...]) + dot(x[0], l[...]) + dot(x[1], h[...])
     scale = 1.0 / math.sqrt(NX * nx)
     shape = (band, nx)
     ky = lax.broadcasted_iota(jnp.int32, shape, 0) + lax.axis_index("xy") * band
     kx = lax.broadcasted_iota(jnp.int32, shape, 1)
     keep = jnp.where((ky == 0) & (kx == 0), 0.0, scale)
-    out_re = times(re, ch_ref, cl_ref) + times(im, sh_ref, sl_ref)
-    out_im = times(im, ch_ref, cl_ref) - times(re, sh_ref, sl_ref)
+    both = times(split(re + im), ch_ref, cl_ref)
+    out_re = both - times(split(im), mh_ref, ml_ref)
+    out_im = both - times(split(re), ph_ref, pl_ref)
     for z in range(planes):
         out_ref[0, z] = out_re[z * band : (z + 1) * band] * keep
         out_ref[1, z] = out_im[z * band : (z + 1) * band] * keep
@@ -478,8 +482,9 @@
 
 def tables(size):
     angle = (np.outer(np.arange(size), np.arange(size)) % size) * (2.0 * np.pi / size)
+    cosine, sine = np.cos(angle), np.sin(angle)
     result = []
-    for table in (np.cos(angle), np.sin(angle)):
+    for table in (cosine, sine, cosine - sine, cosine + sine):
         high = table.astype(np.float32).astype(ml_dtypes.bfloat16)
         low = (table - high.astype(np.float64)).astype(np.float32).astype(ml_dtypes.bfloat16)
         result += [high, low]
@@ -564,7 +569,7 @@
     below_a, above_a = shift(up, "gz", 1), shift(down, "gz", -1)
 
     parcels = [shape((n, 20, 8, ny), f32) for n in counts]
-    side = pltpu.VMEM((half + 4, 8, ny), f32)
+    side = pltpu.VMEM((half + 8, 8, ny), f32)
     begins = [sum(counts[:i]) for i in range(len(counts))]
     parcel = pl.BlockSpec((1, 20, 8, ny), lambda i: (jnp.minimum(i, counts[0] - 1), 0, 0, 0))
     eight = pl.BlockSpec((8, 8, ny), lambda i: (i, 0, 0))
@@ -580,7 +585,7 @@
     ]
     rows_of = lambda n: pl.BlockSpec((n, 2, 8, planes, ny), lambda i: (0, 0, i, 0, 0))
     state, edge, sb, sa, up_0, down_0 = pl.pallas_call(
-        functools.partial(state_kernel, depth=planes * layers, count=counts[0], per_device=slots_here),
+        functools.partial(state_kernel, depth=planes * layers, count=counts[0], per_device=slots_here, steps=steps),
         grid=(steps,),
         in_specs=[
             smem, pl.BlockSpec((2, 8, planes, ny), lambda i: (0, i, 0, 0)), rows_of(3), rows_of(3),
@@ -588,14 +593,15 @@
         ] + middle,
         out_specs=[pl.BlockSpec((8, 8, 8, ny), lambda i: (0, i, 0, 0)), full((8, 4, 8, ny)), eight, eight, parcel, parcel],
         out_shape=[shape((8, half, 8, ny), f32), shape((8, 4, 8, ny), f32), tile, tile, parcels[0], parcels[0]],
-        scratch_shapes=[pltpu.VMEM((4, half + 4, 8, ny), f32), side, side],
+        scratch_shapes=[pltpu.VMEM((4, half + 8, 8, ny), f32), side, side],
         compiler_params=params,
         cost_estimate=cost(*STATE_COST),
         name="state",
     )(events, rho, mom, mag, pot, before, after, *[rho, mom, mag, pot] * 2)
     parcels_below, parcels_above = [shift(up_0, "gz", 1)], [shift(down_0, "gz", -1)]
 
-    cos_high, cos_low, sin_high, sin_low = tables(ny)
+    cos_high, cos_low, sin_high, sin_low = tables(ny)[:4]
+    turns = tables(NX)
     band = ny // across
     turned = band % 128 != 0 or rows % 128 != 0
     hbm = pl.BlockSpec(memory_space=pl.ANY)
@@ -625,14 +631,14 @@
         portion = portion.transpose(1, 2, 4, 0, 3).reshape(2, planes, band, NX)
     modes = pl.pallas_call(
         functools.partial(modes_kernel, turned=turned),
-        in_specs=[whole] * 5,
+        in_specs=[whole] * 7,
         out_specs=whole,
         out_shape=shape((2, planes, band, NX), f32),
         scratch_shapes=[pltpu.VMEM((planes * band, NX), f32)],
         compiler_params=params,
         cost_estimate=cost(*MODES_COST),
         name="modes",
-    )(portion, *tables(NX))
+    )(portion, *turns[:2], *turns[4:])
     results = [shape((3, 2, half, planes, ny), f32)] * 2
     new = []
     for i, n in enumerate(counts):

time: 106 us -> 105 us (level)
  transfers between devices with their start and end apart: 10 -> 10, of which waited for: 3 -> 3; matrix products, arithmetic and copies ran while one was open for 0% -> 0% of each run, Pallas kernels for 50% -> 49%
where the time goes in v4:
time: 105 us
  Pallas kernels  62.8 us (60%)
  starting transfers between devices  25.1 us (24%)
  waiting for transfers between devices  14.7 us (14%)
  between operations  1.36 us (1%)
    pallas_call x2, Pallas kernels, on_device(): pl.pallas_call(functools.partial(main_kernel, first=first), grid=(n,), in...  22.2 us
    ppermute x8, waiting for transfers between devices, shift(): return lax.ppermute(block, axis, [(i, (i + step) % n) for i in range(n)])  14.7 us
    ppermute x8, starting transfers between devices, shift(): return lax.ppermute(block, axis, [(i, (i + step) % n) for i in range(n)])  14.6 us
    pallas_call x1, Pallas kernels, on_device(): pl.pallas_call(density_kernel, in_specs=[hbm, hbm] + [whole] * 7, out_spe...  14.3 us
    pallas_call x1, Pallas kernels, on_device(): pl.pallas_call(functools.partial(state_kernel, depth=planes * layers, cou...  13.5 us
    pallas_call x1, Pallas kernels, on_device(): pl.pallas_call(functools.partial(modes_kernel, turned=turned), in_specs=[...  6.87 us
    all_to_all x1, starting transfers between devices, on_device(): lax.all_to_all(mine, ('gz', 'xy'), split_axis=0, concat_axis=0, tiled=True)  5.43 us
    all_to_all x1, starting transfers between devices, on_device(): lax.all_to_all(wave, 'xy', split_axis=0, concat_axis=0, tiled=True)  5.06 us
  transfers between devices with their start and end apart: 10, of which 3 were waited for; matrix products, arithmetic and copies ran while one was open for 0% of the time, Pallas kernels for 49%

profile of v4, /device:TPU:0, one launch (start us, length us, event | category | flops | bytes accessed | tf_op | source)
XLA Modules:
  0.0 104.6 jit_solution(11813626883511649218)
XLA Ops:
  1.3 1.8 %first.1 = (s32[32,1,128]{2,1,0:T(1,128)}, f32[8,2,4,512]{3,2,1,0:T(4,128)}, f32[8,2,4,512]{3,2,1,0:T(4,128)}) custom-call(s32[1,3]{1,0:T(1,128)} %cell_ref.1, s32[1]{0:T(128)S(6)} %copy.23.count_ref, f32[2,64,4,512]{3,2,1,0:T(4,128)} %bitcast.18, f32[3,2,64,4,512]{4,3,2,1,0:T(4,128)} %bitcast.7, f32[3,2,64,4,512]{4,3,2,1,0:T(4,128)} %bitcast.13, ...), custom_call_target="tpu_custom_call" | custom-call | flops 1000000 | bytes 100000 | tf_op jit(solution)/shard_map/first/pallas_call | solution.py:534
  3.1 2.9 %collective-permute-start = (f32[8,2,4,512]{3,2,1,0:T(4,128)}, f32[8,2,4,512]{3,2,1,0:T(4,128)S(1)}, u32[]{:S(2)}, u32[]{:S(2)}) collective-permute-start(f32[8,2,4,512]{3,2,1,0:T(4,128)} %get-tuple-element.26), channel_id=1, source_target_pairs={{0,1},{1,2},{2,3},{3,0},{4,5},{5,6},{6,7},{7,4},{8,9},{9,10},{10,1... | collective-permute-start | bytes 393224 | tf_op jit(solution)/shard_map/ppermute | solution.py:505
  6.1 1.0 collective-permute-start.1
  7.0 5.4 %all-to-all-start = ((s32[32,1,128]{2,1,0:T(1,128)}), s32[32,1,128]{2,1,0:T(1,128)S(1)}, u32[]{:S(2)}, u32[]{:S(2)}) async-start(s32[32,1,128]{2,1,0:T(1,128)} %get-tuple-element.25.after_ref), calls=%async_computation | async-start | bytes 32768 | tf_op jit(solution)/shard_map/all_to_all | solution.py:553
  12.5 4.0 %pack.1 = (f32[16,3,8,512]{3,2,1,0:T(8,128)}, f32[16,3,8,512]{3,2,1,0:T(8,128)}) custom-call(f32[2,64,4,512]{3,2,1,0:T(4,128)} %bitcast.20, f32[3,2,64,4,512]{4,3,2,1,0:T(4,128)} %bitcast.9, s32[32,1,128]{2,1,0:T(1,128)} %get-tuple-element.25.after_ref), custom_call_target="tpu_custom_call" | custom-call | flops 1000000 | bytes 100000 | tf_op jit(solution)/shard_map/pack/pallas_call | solution.py:557
  16.5 0.3 collective-permute-start.2
  16.7 3.3 %collective-permute-start.3 = (f32[16,3,8,512]{3,2,1,0:T(8,128)}, f32[16,3,8,512]{3,2,1,0:T(8,128)}, u32[]{:S(2)}, u32[]{:S(2)}) collective-permute-start(f32[16,3,8,512]{3,2,1,0:T(8,128)} %get-tuple-element.31), channel_id=1, source_target_pairs={{0,28},{4,0},{8,4},{12,8},{16,12},{20,16},{24,20},{28,24},{1,29},{... | collective-permute-start | bytes 2359304 | tf_op jit(solution)/shard_map/ppermute | solution.py:505
  20.0 0.0 all-to-all-done.ev_ref
  20.0 0.0 collective-permute-done.before_ref
  20.0 0.0 copy-start.1
  20.1 0.0 collective-permute-done.1.after_ref
  20.1 0.0 copy-start.2
  20.1 0.6 copy-done
  20.6 0.1 copy-done.1
  20.7 0.1 copy-done.2
  20.8 13.5 %state.1 = (f32[8,64,8,512]{3,2,1,0:T(8,128)}, f32[8,4,8,512]{3,2,1,0:T(8,128)}, f32[64,8,512]{2,1,0:T(8,128)}, f32[64,8,512]{2,1,0:T(8,128)}, f32[5,20,8,512]{3,2,1,0:T(8,128)}, /*index=5*/f32[5,20,8,512]{3,2,1,0:T(8,128)}) custom-call(s32[32,1,128]{2,1,0:T(1,128)} %copy-done, f32[2,64,4,512]{3,2,1,0:T(4,128)} %bitcast.21, f32[3,2,64,4,512]{4,3,2,1,0:T(4,128)} %bitcast.10, ...), custom_call_target="tpu_custom_call" | custom-call | flops 999999995904 | bytes 4000000000 | tf_op jit(solution)/shard_map/state/pallas_call | solution.py:587
  34.3 0.1 collective-permute-start.6
  34.4 3.5 %collective-permute-start.7 = (f32[5,20,8,512]{3,2,1,0:T(8,128)}, f32[5,20,8,512]{3,2,1,0:T(8,128)}, u32[]{:S(2)}, u32[]{:S(2)}) collective-permute-start(f32[5,20,8,512]{3,2,1,0:T(8,128)} %get-tuple-element.40), channel_id=1, source_target_pairs={{0,28},{4,0},{8,4},{12,8},{16,12},{20,16},{24,20},{28,24},{1,29},{... | collective-permute-start | bytes 4915208 | tf_op jit(solution)/shard_map/ppermute | solution.py:505
  37.9 0.0 collective-permute-done.2.below_ref
  37.9 0.0 collective-permute-done.3.above_ref
  37.9 14.3 %density.1 = (f32[2,64,4,512]{3,2,1,0:T(4,128)}, f32[4,2,4,128,128]{4,3,2,1,0:T(8,128)}, f32[64,8,512]{2,1,0:T(8,128)}, f32[64,8,512]{2,1,0:T(8,128)}, f32[3,20,...) custom-call(f32[8,64,8,512]{3,2,1,0:T(8,128)} %get-tuple-element.28.u_hbm, f32[8,4,8,512]{3,2,1,0:T(8,128)} %get-tuple-element.29.edge_hbm, ...), custom_call_target="tpu_custom_call" | custom-call | flops 999999995904 | bytes 4000000000 | tf_op jit(solution)/shard_map/density/pallas_call | solution.py:609
  52.2 5.1 %all-to-all-start.1 = ((f32[4,2,4,128,128]{4,3,2,1,0:T(8,128)}), f32[4,2,4,128,128]{4,3,2,1,0:T(8,128)}, u32[]{:S(2)}, u32[]{:S(2)}) async-start(f32[4,2,4,128,128]{4,3,2,1,0:T(8,128)} %get-tuple-element.43), calls=%async_computation.1 | async-start | bytes 4194304 | tf_op jit(solution)/shard_map/all_to_all | solution.py:629
  57.3 0.0 collective-permute-start.4
  57.3 3.5 %collective-permute-start.5 = (f32[3,20,8,512]{3,2,1,0:T(8,128)}, f32[3,20,8,512]{3,2,1,0:T(8,128)}, u32[]{:S(2)}, u32[]{:S(2)}) collective-permute-start(f32[3,20,8,512]{3,2,1,0:T(8,128)} %get-tuple-element.38), channel_id=1, source_target_pairs={{0,28},{4,0},{8,4},{12,8},{16,12},{20,16},{24,20},{28,24},{1,29},{... | collective-permute-start | bytes 2949128 | tf_op jit(solution)/shard_map/ppermute | solution.py:505
  60.8 13.4 %collective-permute-done.6.from_below = f32[5,20,8,512]{3,2,1,0:T(8,128)} collective-permute-done((f32[5,20,8,512]{3,2,1,0:T(8,128)}, f32[5,20,8,512]{3,2,1,0:T(8,128)}, u32[]{:S(2)}, u32[]{:S(2)}) %collective-permute-start.6) | collective-permute-done | bytes 1638432 | tf_op jit(solution)/shard_map/ppermute | solution.py:505
  74.3 0.2 collective-permute-done.7.from_above
  74.5 13.0 %main0.1 = (f32[3,2,64,4,512]{4,3,2,1,0:T(4,128)}, f32[3,2,64,4,512]{4,3,2,1,0:T(4,128)}) custom-call(f32[8,64,8,512]{3,2,1,0:T(8,128)} %get-tuple-element.28.u_hbm, f32[8,4,8,512]{3,2,1,0:T(8,128)} %get-tuple-element.29.edge_hbm, f32[64,8,512]{2,1,0:T(8,128)} %get-tuple-element.35.rho_ref, f32[64,8,512]{2,1,0:T(8,128)} %get-tuple-element.36.mz_ref, ...), custom_call_target="tpu_custom_call" | custom-call | flops 999999995904 | bytes 4000000000 | tf_op jit(solution)/shard_map/main0/pallas_call | solution.py:651
  87.4 0.0 all-to-all-done.1.w_ref
  87.5 6.9 %modes.1.rest_2_ = f32[2,4,128,512]{3,2,1,0:T(8,128)} custom-call(f32[4,2,4,128,128]{4,3,2,1,0:T(8,128)} %all-to-all-done.1.w_ref, bf16[512,512]{1,0:T(8,128)(2,1)} %constant.21.clone.ch_ref, bf16[512,512]{1,0:T(8,128)(2,1)} %constant.22.clone.cl_ref, bf16[512,512]{1,0:T(8,128)(2,1)} %constant.23.clone.mh_ref, bf16[512,512]{1,0:T(8,128)(2,1)} %constant.24.clone.ml_ref, ...), custom_call_target="tpu_custom_call" | custom-call | flops 1000000 | bytes 100000 | tf_op jit(solution)/shard_map/modes/pallas_call | solution.py:632
  94.3 1.0 collective-permute-done.4.from_below
  95.3 0.0 collective-permute-done.5.from_above
  95.3 9.3 %main1.1 = (f32[3,2,64,4,512]{4,3,2,1,0:T(4,128)}, f32[3,2,64,4,512]{4,3,2,1,0:T(4,128)}) custom-call(f32[8,64,8,512]{3,2,1,0:T(8,128)} %get-tuple-element.28.u_hbm, f32[8,4,8,512]{3,2,1,0:T(8,128)} %get-tuple-element.29.edge_hbm, f32[64,8,512]{2,1,0:T(8,128)} %get-tuple-element.35.rho_ref, ...), custom_call_target="tpu_custom_call", output_to_operand_aliasing={{0}: (6, {}), {1}: (7, {})} | custom-call | flops 999999995904 | bytes 4000000000 | tf_op jit(solution)/shard_map/main1/pallas_call | solution.py:651
  (1 shorter events, 0.0 us)
Async XLA Ops:
  3.1 16.9 %collective-permute-start = (f32[8,2,4,512]{3,2,1,0:T(4,128)}, f32[8,2,4,512]{3,2,1,0:T(4,128)S(1)}, u32[]{:S(2)}, u32[]{:S(2)}) collective-permute-start(f32[8,2,4,512]{3,2,1,0:T(4,128)} %get-tuple-element.26), channel_id=1, source_target_pairs={{0,1},{1,2},{2,3},{3,0},{4,5},{5,6},{6,7},{7,4},{8,9},{9,10},{10,1... | collective-permute-start | bytes 393224 | tf_op jit(solution)/shard_map/ppermute | solution.py:505
  6.1 14.0 %collective-permute-start.1 = (f32[8,2,4,512]{3,2,1,0:T(4,128)}, f32[8,2,4,512]{3,2,1,0:T(4,128)S(1)}, u32[]{:S(2)}, u32[]{:S(2)}) collective-permute-start(f32[8,2,4,512]{3,2,1,0:T(4,128)} %get-tuple-element.27), channel_id=1, source_target_pairs={{0,3},{1,0},{2,1},{3,2},{4,7},{5,4},{6,5},{7,6},{8,11},{9,8},{10,9... | collective-permute-start | bytes 393224 | tf_op jit(solution)/shard_map/ppermute | solution.py:505
  7.0 13.0 %all-to-all-start = ((s32[32,1,128]{2,1,0:T(1,128)}), s32[32,1,128]{2,1,0:T(1,128)S(1)}, u32[]{:S(2)}, u32[]{:S(2)}) async-start(s32[32,1,128]{2,1,0:T(1,128)} %get-tuple-element.25.after_ref), calls=%async_computation | async-start | bytes 32768 | tf_op jit(solution)/shard_map/all_to_all | solution.py:553
  16.5 21.4 %collective-permute-start.2 = (f32[16,3,8,512]{3,2,1,0:T(8,128)}, f32[16,3,8,512]{3,2,1,0:T(8,128)}, u32[]{:S(2)}, u32[]{:S(2)}) collective-permute-start(f32[16,3,8,512]{3,2,1,0:T(8,128)} %get-tuple-element.30), channel_id=1, source_target_pairs={{0,4},{4,8},{8,12},{12,16},{16,20},{20,24},{24,28},{28,0},{1,5},{5... | collective-permute-start | bytes 2359304 | tf_op jit(solution)/shard_map/ppermute | solution.py:505
  16.7 21.2 %collective-permute-start.3 = (f32[16,3,8,512]{3,2,1,0:T(8,128)}, f32[16,3,8,512]{3,2,1,0:T(8,128)}, u32[]{:S(2)}, u32[]{:S(2)}) collective-permute-start(f32[16,3,8,512]{3,2,1,0:T(8,128)} %get-tuple-element.31), channel_id=1, source_target_pairs={{0,28},{4,0},{8,4},{12,8},{16,12},{20,16},{24,20},{28,24},{1,29},{... | collective-permute-start | bytes 2359304 | tf_op jit(solution)/shard_map/ppermute | solution.py:505
  20.0 0.6 copy-start
  20.0 0.7 copy-start.1
  20.1 0.7 copy-start.2
  34.3 39.9 %collective-permute-start.6 = (f32[5,20,8,512]{3,2,1,0:T(8,128)}, f32[5,20,8,512]{3,2,1,0:T(8,128)}, u32[]{:S(2)}, u32[]{:S(2)}) collective-permute-start(f32[5,20,8,512]{3,2,1,0:T(8,128)} %get-tuple-element.39), channel_id=1, source_target_pairs={{0,4},{4,8},{8,12},{12,16},{16,20},{20,24},{24,28},{28,0},{1,5},{5... | collective-permute-start | bytes 4915208 | tf_op jit(solution)/shard_map/ppermute | solution.py:505
  34.4 40.1 %collective-permute-start.7 = (f32[5,20,8,512]{3,2,1,0:T(8,128)}, f32[5,20,8,512]{3,2,1,0:T(8,128)}, u32[]{:S(2)}, u32[]{:S(2)}) collective-permute-start(f32[5,20,8,512]{3,2,1,0:T(8,128)} %get-tuple-element.40), channel_id=1, source_target_pairs={{0,28},{4,0},{8,4},{12,8},{16,12},{20,16},{24,20},{28,24},{1,29},{... | collective-permute-start | bytes 4915208 | tf_op jit(solution)/shard_map/ppermute | solution.py:505
  52.2 35.2 %all-to-all-start.1 = ((f32[4,2,4,128,128]{4,3,2,1,0:T(8,128)}), f32[4,2,4,128,128]{4,3,2,1,0:T(8,128)}, u32[]{:S(2)}, u32[]{:S(2)}) async-start(f32[4,2,4,128,128]{4,3,2,1,0:T(8,128)} %get-tuple-element.43), calls=%async_computation.1 | async-start | bytes 4194304 | tf_op jit(solution)/shard_map/all_to_all | solution.py:629
  57.3 38.0 %collective-permute-start.4 = (f32[3,20,8,512]{3,2,1,0:T(8,128)}, f32[3,20,8,512]{3,2,1,0:T(8,128)}, u32[]{:S(2)}, u32[]{:S(2)}) collective-permute-start(f32[3,20,8,512]{3,2,1,0:T(8,128)} %get-tuple-element.37), channel_id=1, source_target_pairs={{0,4},{4,8},{8,12},{12,16},{16,20},{20,24},{24,28},{28,0},{1,5},{5... | collective-permute-start | bytes 2949128 | tf_op jit(solution)/shard_map/ppermute | solution.py:505
  57.3 38.0 %collective-permute-start.5 = (f32[3,20,8,512]{3,2,1,0:T(8,128)}, f32[3,20,8,512]{3,2,1,0:T(8,128)}, u32[]{:S(2)}, u32[]{:S(2)}) collective-permute-start(f32[3,20,8,512]{3,2,1,0:T(8,128)} %get-tuple-element.38), channel_id=1, source_target_pairs={{0,28},{4,0},{8,4},{12,8},{16,12},{20,16},{24,20},{28,24},{1,29},{... | collective-permute-start | bytes 2949128 | tf_op jit(solution)/shard_map/ppermute | solution.py:505

commit v5 on v4

--- a/solution.py
+++ b/solution.py
@@ -356,9 +356,47 @@
     return jnp.where(sub == 7, turn(above, 6 - 2 * j, 0), out)
 
 
-def main_kernel(u_hbm, edge_hbm, rho_ref, mz_ref, from_below, from_above, *rest, first):
+def halo_planes(rho_ref, mz_ref, from_below, from_above, r, g, j):
+    bn, an, bf, af = from_below[0, r], from_above[0, r], from_below[0, 8 + r], from_above[0, 8 + r]
+    hm = [ends(bn, an, 0), ends(bn, an, 1), mz_ref[r]]
+    hb = [last_plane(from_below[0, 18 + g], from_above[0, 18 + g], j), ends(bn, an, 2), ends(bn, an, 3)]
+    fh = fluxes(*shared(rho_ref[r], hm, hb), hm, hb, 2)
+    halo = hm + hb
+    far = [ends(bf, af, c) for c in range(4)] + [last_plane(from_below[0, 16 + g], from_above[0, 16 + g], j), None]
+    return fh, halo, far
+
+
+def halo_kernel(rho_ref, mz_ref, from_below, from_above, mom_in, mag_in, *rest):
+    mom_ref, mag_ref = rest[-2:]
+
+    def row(r, g, j):
+        fh, halo, far = halo_planes(rho_ref, mz_ref, from_below, from_above, r, g, j)
+        slot = slots(halo[0].shape)
+        first, last = slot == 0, slot == 3
+        for c in range(6):
+            add = DIFFUSION * halo[c]
+            if fh[c] is not None:
+                add += jnp.where(first, NEAR, -NEAR) * fh[c]
+            add = jnp.where(first | last, add, 0.0)
+            if fh[c] is not None:
+                beyond = jnp.where(slot == 1, turn(fh[c], 1, 0), jnp.where(slot == 2, turn(fh[c], -1, 0), far[c]))
+                add += jnp.where(slot >= 2, FAR, -FAR) * beyond
+            if c < 3:
+                unpair(mom_ref, pair(mom_in, c, r) + add, c, r)
+            else:
+                unpair(mag_ref, pair(mag_in, c - 3, r) + add, c - 3, r)
+
+    def body(g, _):
+        for j in range(4):
+            row(4 * g + j, g, j)
+        return 0
+
+    lax.fori_loop(0, 2, body, 0)
+
+
+def main_kernel(u_hbm, edge_hbm, rho_ref, mz_ref, from_below, from_above, *rest, first, inner):
     mom_ref, mag_ref, u_ref, f_ref, sem = rest[-5:]
-    chunk, total, half = rho_ref.shape[0], u_ref.shape[1], u_hbm.shape[1]
+    chunk, total, half = 8, u_ref.shape[1], u_hbm.shape[1]
     step_id = pl.program_id(0)
     start = step_id * chunk
     kept = (0, 1, 2, 4, 5)
@@ -403,12 +441,12 @@
         v, pressure = shared(u[0], u[1:4], u[4:7])
         fy = fluxes(v, pressure, u[1:4], u[4:7], 1)
         fz = fluxes(v, pressure, u[1:4], u[4:7], 2)
-        bn, an, bf, af = from_below[0, r], from_above[0, r], from_below[0, 8 + r], from_above[0, 8 + r]
-        hm = [ends(bn, an, 0), ends(bn, an, 1), mz_ref[r]]
-        hb = [last_plane(from_below[0, 18 + g], from_above[0, 18 + g], j), ends(bn, an, 2), ends(bn, an, 3)]
-        fh = fluxes(*shared(rho_ref[r], hm, hb), hm, hb, 2)
-        halo = hm + hb
-        far = [ends(bf, af, c) for c in range(4)] + [last_plane(from_below[0, 16 + g], from_above[0, 16 + g], j), None]
+        if inner:
+            zero = jnp.zeros_like(u[0])
+            fh = halo = far = [zero] * 5 + [None]
+            halo = [zero] * 6
+        else:
+            fh, halo, far = halo_planes(rho_ref, mz_ref, from_below, from_above, r, g, j)
         for c in range(6):
             field = u[c + 1]
             new = field * (1.0 - 6.0 * DIFFUSION)
@@ -640,28 +678,47 @@
         name="modes",
     )(portion, *turns[:2], *turns[4:])
     results = [shape((3, 2, half, planes, ny), f32)] * 2
-    new = []
-    for i, n in enumerate(counts):
-        chunk, first = 8, begins[i] * 8
-        here = pl.BlockSpec((chunk, 8, ny), lambda k, o=begins[i]: (o + k, 0, 0))
-        parcel = pl.BlockSpec((1, 20, 8, ny), lambda k: (k, 0, 0, 0))
-        three = pl.BlockSpec((3, 2, chunk, planes, ny), lambda k, o=begins[i]: (0, 0, o + k, 0, 0))
-        below, above = parcels_below[i], parcels_above[i]
-        extra = [*new] + [modes] * (i > 0 and i == len(counts) - 1)
-        new = pl.pallas_call(
-            functools.partial(main_kernel, first=first),
+    three = lambda b: pl.BlockSpec((3, 2, 8, planes, ny), lambda k: (0, 0, b + k, 0, 0))
+    here = lambda b: pl.BlockSpec((8, 8, ny), lambda k: (b + k, 0, 0))
+    parcel = pl.BlockSpec((1, 20, 8, ny), lambda k: (k, 0, 0, 0))
+    wide = pltpu.CompilerParams(vmem_limit_bytes=62 * 1024 * 1024)
+
+    def main(i, inner, name, *new):
+        n, b = counts[i], begins[i]
+        halos = [hbm] * 4 if inner else [here(b)] * 2 + [parcel] * 2
+        parts = (rho_halo, mz_halo) if inner else (parcels_below[i], parcels_above[i])
+        return pl.pallas_call(
+            functools.partial(main_kernel, first=b * 8, inner=inner),
             grid=(n,),
-            in_specs=[hbm, hbm] + [here] * 2 + [parcel] * 2 + [hbm] * len(extra),
-            out_specs=[three, three],
+            in_specs=[hbm, hbm] + halos + [hbm] * len(new),
+            out_specs=[three(b), three(b)],
             out_shape=results,
             scratch_shapes=[
-                pltpu.VMEM((8, n * 8 + 4, 8, ny), f32), pltpu.VMEM((5, n * 8 + 4, 8, ny), f32), pltpu.SemaphoreType.DMA((n + 2,)),
+                pltpu.VMEM((8, n * 8 + 4, 8, ny), f32), pltpu.VMEM((5, n * 8 + 4, 8, ny), f32),
+                pltpu.SemaphoreType.DMA((n + 2,)),
             ],
             input_output_aliases={6: 0, 7: 1} if new else {},
-            compiler_params=pltpu.CompilerParams(vmem_limit_bytes=62 * 1024 * 1024),
+            compiler_params=wide,
             cost_estimate=cost(*MAIN_COST),
-            name=f"main{i}",
-        )(state, edge, rho_halo, mz_halo, below, above, *extra)
+            name=name,
+        )(state, edge, rho_halo, mz_halo, *parts, *new)
+
+    if len(counts) == 1:
+        new = main(0, False, "main0")
+    else:
+        new = main(0, False, "main0", *main(1, True, "inner1"))
+        n, b = counts[1], begins[1]
+        new = pl.pallas_call(
+            halo_kernel,
+            grid=(n,),
+            in_specs=[here(b)] * 2 + [parcel] * 2 + [three(b)] * 2 + [hbm],
+            out_specs=[three(b)] * 2,
+            out_shape=results,
+            input_output_aliases={4: 0, 5: 1},
+            compiler_params=wide,
+            cost_estimate=cost(*MAIN_COST),
+            name="halo1",
+        )(rho_halo, mz_halo, parcels_below[1], parcels_above[1], *new, modes)
     new_mom, new_mag = new
 
     return (

time: 105 us -> 103 us (0.981)
  waiting for transfers between devices: 14.7 us -> 8.28 us
  Pallas kernels: 62.8 us -> 67.4 us
    ppermute x8, waiting for transfers between devices: 14.7 us -> 8.28 us  [shift(): return lax.ppermute(block, axis, [(i, (i + step) % n) for i in range(n)])]
    pallas_call x2 -> x3, Pallas kernels: 22.2 us -> 25.3 us  [the longest x2 19.8 us: main(): pl.pallas_call(functools.partial(main_kernel, first=b * 8, inner=inner),...]
    pallas_call x1, Pallas kernels: 13.5 us -> 15 us  [on_device(): pl.pallas_call(functools.partial(state_kernel, depth=planes * layers, cou...]
  transfers between devices with their start and end apart: 10 -> 10, of which waited for: 3 -> 3; matrix products, arithmetic and copies ran while one was open for 0% -> 0% of each run, Pallas kernels for 49% -> 59%
where the time goes in v5:
time: 103 us; the launch traced here: 102 us
  Pallas kernels  67.4 us (65%)
  starting transfers between devices  24.6 us (24%)
  waiting for transfers between devices  8.28 us (8%)
  between operations  1.38 us (1%)
    pallas_call x2, Pallas kernels, main(): pl.pallas_call(functools.partial(main_kernel, first=b * 8, inner=inner),...  19.8 us
    pallas_call x1, Pallas kernels, on_device(): pl.pallas_call(functools.partial(state_kernel, depth=planes * layers, cou...  15 us
    ppermute x8, starting transfers between devices, shift(): return lax.ppermute(block, axis, [(i, (i + step) % n) for i in range(n)])  14.6 us
    pallas_call x1, Pallas kernels, on_device(): pl.pallas_call(density_kernel, in_specs=[hbm, hbm] + [whole] * 7, out_spe...  14.3 us
    ppermute x8, waiting for transfers between devices, shift(): return lax.ppermute(block, axis, [(i, (i + step) % n) for i in range(n)])  8.28 us
    pallas_call x1, Pallas kernels, on_device(): pl.pallas_call(functools.partial(modes_kernel, turned=turned), in_specs=[...  6.85 us
    pallas_call x1, Pallas kernels, on_device(): pl.pallas_call(halo_kernel, grid=(n,), in_specs=[here(b)] * 2 + [parcel]...  5.54 us
    all_to_all x1, starting transfers between devices, on_device(): lax.all_to_all(mine, ('gz', 'xy'), split_axis=0, concat_axis=0, tiled=True)  5.43 us
  transfers between devices with their start and end apart: 10, of which 3 were waited for; matrix products, arithmetic and copies ran while one was open for 0% of the time, Pallas kernels for 59%

profile of v5, /device:TPU:0, one launch (start us, length us, event | category | flops | bytes accessed | tf_op | source)
XLA Modules:
  0.0 102.3 jit_solution(12057863272597684119)
XLA Ops:
  1.3 1.8 %first.1 = (s32[32,1,128]{2,1,0:T(1,128)}, f32[8,2,4,512]{3,2,1,0:T(4,128)}, f32[8,2,4,512]{3,2,1,0:T(4,128)}) custom-call(s32[1,3]{1,0:T(1,128)} %cell_ref.1, s32[1]{0:T(128)S(6)} %copy.27.count_ref, f32[2,64,4,512]{3,2,1,0:T(4,128)} %bitcast.18, f32[3,2,64,4,512]{4,3,2,1,0:T(4,128)} %bitcast.7, f32[3,2,64,4,512]{4,3,2,1,0:T(4,128)} %bitcast.13, ...), custom_call_target="tpu_custom_call" | custom-call | flops 1000000 | bytes 100000 | tf_op jit(solution)/shard_map/first/pallas_call | solution.py:572
  3.1 2.9 %collective-permute-start = (f32[8,2,4,512]{3,2,1,0:T(4,128)}, f32[8,2,4,512]{3,2,1,0:T(4,128)S(1)}, u32[]{:S(2)}, u32[]{:S(2)}) collective-permute-start(f32[8,2,4,512]{3,2,1,0:T(4,128)} %get-tuple-element.28), channel_id=1, source_target_pairs={{0,1},{1,2},{2,3},{3,0},{4,5},{5,6},{6,7},{7,4},{8,9},{9,10},{10,1... | collective-permute-start | bytes 393224 | tf_op jit(solution)/shard_map/ppermute | solution.py:543
  6.1 1.0 collective-permute-start.1
  7.0 5.4 %all-to-all-start = ((s32[32,1,128]{2,1,0:T(1,128)}), s32[32,1,128]{2,1,0:T(1,128)S(1)}, u32[]{:S(2)}, u32[]{:S(2)}) async-start(s32[32,1,128]{2,1,0:T(1,128)} %get-tuple-element.27.after_ref), calls=%async_computation | async-start | bytes 32768 | tf_op jit(solution)/shard_map/all_to_all | solution.py:591
  12.5 4.0 %pack.1 = (f32[16,3,8,512]{3,2,1,0:T(8,128)}, f32[16,3,8,512]{3,2,1,0:T(8,128)}) custom-call(f32[2,64,4,512]{3,2,1,0:T(4,128)} %bitcast.20, f32[3,2,64,4,512]{4,3,2,1,0:T(4,128)} %bitcast.9, s32[32,1,128]{2,1,0:T(1,128)} %get-tuple-element.27.after_ref), custom_call_target="tpu_custom_call" | custom-call | flops 1000000 | bytes 100000 | tf_op jit(solution)/shard_map/pack/pallas_call | solution.py:595
  16.5 0.3 collective-permute-start.2
  16.7 3.3 %collective-permute-start.3 = (f32[16,3,8,512]{3,2,1,0:T(8,128)}, f32[16,3,8,512]{3,2,1,0:T(8,128)}, u32[]{:S(2)}, u32[]{:S(2)}) collective-permute-start(f32[16,3,8,512]{3,2,1,0:T(8,128)} %get-tuple-element.33), channel_id=1, source_target_pairs={{0,28},{4,0},{8,4},{12,8},{16,12},{20,16},{24,20},{28,24},{1,29},{... | collective-permute-start | bytes 2359304 | tf_op jit(solution)/shard_map/ppermute | solution.py:543
  20.0 0.0 all-to-all-done.ev_ref
  20.0 0.0 collective-permute-done.before_ref
  20.0 0.0 copy-start.1
  20.1 0.0 collective-permute-done.1.after_ref
  20.1 0.6 copy-done
  20.6 0.1 copy-done.1
  20.7 0.0 copy-done.2
  20.7 15.0 %state.1 = (f32[8,64,8,512]{3,2,1,0:T(8,128)}, f32[8,4,8,512]{3,2,1,0:T(8,128)}, f32[64,8,512]{2,1,0:T(8,128)}, f32[64,8,512]{2,1,0:T(8,128)}, f32[5,20,8,512]{3,2,1,0:T(8,128)}, /*index=5*/f32[5,20,8,512]{3,2,1,0:T(8,128)}) custom-call(s32[32,1,128]{2,1,0:T(1,128)} %copy-done, f32[2,64,4,512]{3,2,1,0:T(4,128)} %bitcast.21, f32[3,2,64,4,512]{4,3,2,1,0:T(4,128)} %bitcast.10, ...), custom_call_target="tpu_custom_call" | custom-call | flops 999999995904 | bytes 4000000000 | tf_op jit(solution)/shard_map/state/pallas_call | solution.py:625
  35.7 0.1 collective-permute-start.6
  35.8 3.5 %collective-permute-start.7 = (f32[5,20,8,512]{3,2,1,0:T(8,128)}, f32[5,20,8,512]{3,2,1,0:T(8,128)}, u32[]{:S(2)}, u32[]{:S(2)}) collective-permute-start(f32[5,20,8,512]{3,2,1,0:T(8,128)} %get-tuple-element.42), channel_id=1, source_target_pairs={{0,28},{4,0},{8,4},{12,8},{16,12},{20,16},{24,20},{28,24},{1,29},{... | collective-permute-start | bytes 4915208 | tf_op jit(solution)/shard_map/ppermute | solution.py:543
  39.3 0.0 collective-permute-done.2.below_ref
  39.3 0.0 collective-permute-done.3.above_ref
  39.3 14.3 %density.1 = (f32[2,64,4,512]{3,2,1,0:T(4,128)}, f32[4,2,4,128,128]{4,3,2,1,0:T(8,128)}, f32[64,8,512]{2,1,0:T(8,128)}, f32[64,8,512]{2,1,0:T(8,128)}, f32[3,20,...) custom-call(f32[8,64,8,512]{3,2,1,0:T(8,128)} %get-tuple-element.30.u_hbm, f32[8,4,8,512]{3,2,1,0:T(8,128)} %get-tuple-element.31.edge_hbm, ...), custom_call_target="tpu_custom_call" | custom-call | flops 999999995904 | bytes 4000000000 | tf_op jit(solution)/shard_map/density/pallas_call | solution.py:647
  53.7 4.5 %all-to-all-start.1 = ((f32[4,2,4,128,128]{4,3,2,1,0:T(8,128)}), f32[4,2,4,128,128]{4,3,2,1,0:T(8,128)}, u32[]{:S(2)}, u32[]{:S(2)}) async-start(f32[4,2,4,128,128]{4,3,2,1,0:T(8,128)} %get-tuple-element.47), calls=%async_computation.1 | async-start | bytes 4194304 | tf_op jit(solution)/shard_map/all_to_all | solution.py:667
  58.2 0.1 collective-permute-start.4
  58.3 3.5 %collective-permute-start.5 = (f32[3,20,8,512]{3,2,1,0:T(8,128)}, f32[3,20,8,512]{3,2,1,0:T(8,128)}, u32[]{:S(2)}, u32[]{:S(2)}) collective-permute-start(f32[3,20,8,512]{3,2,1,0:T(8,128)} %get-tuple-element.40), channel_id=1, source_target_pairs={{0,28},{4,0},{8,4},{12,8},{16,12},{20,16},{24,20},{28,24},{1,29},{... | collective-permute-start | bytes 2949128 | tf_op jit(solution)/shard_map/ppermute | solution.py:543
  61.8 6.9 %inner1.1 = (f32[3,2,64,4,512]{4,3,2,1,0:T(4,128)}, f32[3,2,64,4,512]{4,3,2,1,0:T(4,128)}) custom-call(f32[8,64,8,512]{3,2,1,0:T(8,128)} %get-tuple-element.30.u_hbm, f32[8,4,8,512]{3,2,1,0:T(8,128)} %get-tuple-element.31.edge_hbm, f32[64,8,512]{2,1,0:T(8,128)} %get-tuple-element.37.rho_ref.from_below, f32[64,8,512]{2,1,0:T(8,128)} %get-tuple-element.38.mz_ref.from_above, ...), custom_call_target="tpu_custom_call" | custom-call | flops 999999995904 | bytes 4000000000 | tf_op jit(solution)/shard_map/inner1/pallas_call | solution.py:690
  68.7 7.0 %collective-permute-done.6.from_below = f32[5,20,8,512]{3,2,1,0:T(8,128)} collective-permute-done((f32[5,20,8,512]{3,2,1,0:T(8,128)}, f32[5,20,8,512]{3,2,1,0:T(8,128)}, u32[]{:S(2)}, u32[]{:S(2)}) %collective-permute-start.6) | collective-permute-done | bytes 1638432 | tf_op jit(solution)/shard_map/ppermute | solution.py:543
  75.7 0.2 collective-permute-done.7.from_above
  75.9 13.0 %main0.1 = (f32[3,2,64,4,512]{4,3,2,1,0:T(4,128)}, f32[3,2,64,4,512]{4,3,2,1,0:T(4,128)}) custom-call(f32[8,64,8,512]{3,2,1,0:T(8,128)} %get-tuple-element.30.u_hbm, f32[8,4,8,512]{3,2,1,0:T(8,128)} %get-tuple-element.31.edge_hbm, f32[64,8,512]{2,1,0:T(8,128)} %get-tuple-element.37.rho_ref.from_below, ...), custom_call_target="tpu_custom_call", output_to_operand_aliasing={{0}: (6, {}), {1}: (7, {})} | custom-call | flops 999999995904 | bytes 4000000000 | tf_op jit(solution)/shard_map/main0/pallas_call | solution.py:690
  88.9 0.0 all-to-all-done.1.w_ref
  88.9 6.8 %modes.1.rest_0_ = f32[2,4,128,512]{3,2,1,0:T(8,128)} custom-call(f32[4,2,4,128,128]{4,3,2,1,0:T(8,128)} %all-to-all-done.1.w_ref, bf16[512,512]{1,0:T(8,128)(2,1)} %constant.21.clone.ch_ref, bf16[512,512]{1,0:T(8,128)(2,1)} %constant.22.clone.cl_ref, bf16[512,512]{1,0:T(8,128)(2,1)} %constant.23.clone.mh_ref, bf16[512,512]{1,0:T(8,128)(2,1)} %constant.24.clone.ml_ref, ...), custom_call_target="tpu_custom_call" | custom-call | flops 1000000 | bytes 100000 | tf_op jit(solution)/shard_map/modes/pallas_call | solution.py:670
  95.7 1.0 collective-permute-done.4.from_below
  96.8 0.0 collective-permute-done.5.from_above
  96.8 5.5 %halo1.1 = (f32[3,2,64,4,512]{4,3,2,1,0:T(4,128)}, f32[3,2,64,4,512]{4,3,2,1,0:T(4,128)}) custom-call(f32[64,8,512]{2,1,0:T(8,128)} %get-tuple-element.37.rho_ref.from_below, f32[64,8,512]{2,1,0:T(8,128)} %get-tuple-element.38.mz_ref.from_above, f32[3,20,8,512]{3,2,1,0:T(8,128)} %collective-permute-done.4.from_below, ...), custom_call_target="tpu_custom_call", output_to_operand_aliasing={{0}: (4, {}), {1}: (5, {})} | custom-call | flops 999999995904 | bytes 4000000000 | tf_op jit(solution)/shard_map/halo1/pallas_call | solution.py:711
  (2 shorter events, 0.0 us)
Async XLA Ops:
  3.1 16.9 %collective-permute-start = (f32[8,2,4,512]{3,2,1,0:T(4,128)}, f32[8,2,4,512]{3,2,1,0:T(4,128)S(1)}, u32[]{:S(2)}, u32[]{:S(2)}) collective-permute-start(f32[8,2,4,512]{3,2,1,0:T(4,128)} %get-tuple-element.28), channel_id=1, source_target_pairs={{0,1},{1,2},{2,3},{3,0},{4,5},{5,6},{6,7},{7,4},{8,9},{9,10},{10,1... | collective-permute-start | bytes 393224 | tf_op jit(solution)/shard_map/ppermute | solution.py:543
  6.1 14.0 %collective-permute-start.1 = (f32[8,2,4,512]{3,2,1,0:T(4,128)}, f32[8,2,4,512]{3,2,1,0:T(4,128)S(1)}, u32[]{:S(2)}, u32[]{:S(2)}) collective-permute-start(f32[8,2,4,512]{3,2,1,0:T(4,128)} %get-tuple-element.29), channel_id=1, source_target_pairs={{0,3},{1,0},{2,1},{3,2},{4,7},{5,4},{6,5},{7,6},{8,11},{9,8},{10,9... | collective-permute-start | bytes 393224 | tf_op jit(solution)/shard_map/ppermute | solution.py:543
  7.0 13.0 %all-to-all-start = ((s32[32,1,128]{2,1,0:T(1,128)}), s32[32,1,128]{2,1,0:T(1,128)S(1)}, u32[]{:S(2)}, u32[]{:S(2)}) async-start(s32[32,1,128]{2,1,0:T(1,128)} %get-tuple-element.27.after_ref), calls=%async_computation | async-start | bytes 32768 | tf_op jit(solution)/shard_map/all_to_all | solution.py:591
  16.5 22.9 %collective-permute-start.2 = (f32[16,3,8,512]{3,2,1,0:T(8,128)}, f32[16,3,8,512]{3,2,1,0:T(8,128)}, u32[]{:S(2)}, u32[]{:S(2)}) collective-permute-start(f32[16,3,8,512]{3,2,1,0:T(8,128)} %get-tuple-element.32), channel_id=1, source_target_pairs={{0,4},{4,8},{8,12},{12,16},{16,20},{20,24},{24,28},{28,0},{1,5},{5... | collective-permute-start | bytes 2359304 | tf_op jit(solution)/shard_map/ppermute | solution.py:543
  16.7 22.6 %collective-permute-start.3 = (f32[16,3,8,512]{3,2,1,0:T(8,128)}, f32[16,3,8,512]{3,2,1,0:T(8,128)}, u32[]{:S(2)}, u32[]{:S(2)}) collective-permute-start(f32[16,3,8,512]{3,2,1,0:T(8,128)} %get-tuple-element.33), channel_id=1, source_target_pairs={{0,28},{4,0},{8,4},{12,8},{16,12},{20,16},{24,20},{28,24},{1,29},{... | collective-permute-start | bytes 2359304 | tf_op jit(solution)/shard_map/ppermute | solution.py:543
  20.0 0.6 copy-start
  20.0 0.7 copy-start.1
  20.1 0.7 copy-start.2
  35.7 39.9 %collective-permute-start.6 = (f32[5,20,8,512]{3,2,1,0:T(8,128)}, f32[5,20,8,512]{3,2,1,0:T(8,128)}, u32[]{:S(2)}, u32[]{:S(2)}) collective-permute-start(f32[5,20,8,512]{3,2,1,0:T(8,128)} %get-tuple-element.41), channel_id=1, source_target_pairs={{0,4},{4,8},{8,12},{12,16},{16,20},{20,24},{24,28},{28,0},{1,5},{5... | collective-permute-start | bytes 4915208 | tf_op jit(solution)/shard_map/ppermute | solution.py:543
  35.8 40.1 %collective-permute-start.7 = (f32[5,20,8,512]{3,2,1,0:T(8,128)}, f32[5,20,8,512]{3,2,1,0:T(8,128)}, u32[]{:S(2)}, u32[]{:S(2)}) collective-permute-start(f32[5,20,8,512]{3,2,1,0:T(8,128)} %get-tuple-element.42), channel_id=1, source_target_pairs={{0,28},{4,0},{8,4},{12,8},{16,12},{20,16},{24,20},{28,24},{1,29},{... | collective-permute-start | bytes 4915208 | tf_op jit(solution)/shard_map/ppermute | solution.py:543
  53.7 35.2 %all-to-all-start.1 = ((f32[4,2,4,128,128]{4,3,2,1,0:T(8,128)}), f32[4,2,4,128,128]{4,3,2,1,0:T(8,128)}, u32[]{:S(2)}, u32[]{:S(2)}) async-start(f32[4,2,4,128,128]{4,3,2,1,0:T(8,128)} %get-tuple-element.47), calls=%async_computation.1 | async-start | bytes 4194304 | tf_op jit(solution)/shard_map/all_to_all | solution.py:667
  58.2 38.5 %collective-permute-start.4 = (f32[3,20,8,512]{3,2,1,0:T(8,128)}, f32[3,20,8,512]{3,2,1,0:T(8,128)}, u32[]{:S(2)}, u32[]{:S(2)}) collective-permute-start(f32[3,20,8,512]{3,2,1,0:T(8,128)} %get-tuple-element.39), channel_id=1, source_target_pairs={{0,4},{4,8},{8,12},{12,16},{16,20},{20,24},{24,28},{28,0},{1,5},{5... | collective-permute-start | bytes 2949128 | tf_op jit(solution)/shard_map/ppermute | solution.py:543
  58.3 38.5 %collective-permute-start.5 = (f32[3,20,8,512]{3,2,1,0:T(8,128)}, f32[3,20,8,512]{3,2,1,0:T(8,128)}, u32[]{:S(2)}, u32[]{:S(2)}) collective-permute-start(f32[3,20,8,512]{3,2,1,0:T(8,128)} %get-tuple-element.40), channel_id=1, source_target_pairs={{0,28},{4,0},{8,4},{12,8},{16,12},{20,16},{24,20},{28,24},{1,29},{... | collective-permute-start | bytes 2949128 | tf_op jit(solution)/shard_map/ppermute | solution.py:543

commit v6 on v5

--- a/solution.py
+++ b/solution.py
@@ -558,7 +558,7 @@
     message = shape((2, half, planes, ny), f32)
     tile = shape((half, 8, ny), f32)
     steps = half // 8
-    counts = (steps * 5 // 8, steps - steps * 5 // 8) if steps >= 2 else (steps,)
+    counts = (steps - steps // 2, steps // 2) if steps >= 2 else (steps,)
 
     slots_here = sn_cells.shape[0]
     rho = density.reshape(2, half, planes, ny)

time: 103 us -> 102 us (level)
    ppermute x8, waiting for transfers between devices: 8.28 us -> 5.11 us  [shift(): return lax.ppermute(block, axis, [(i, (i + step) % n) for i in range(n)])]
    all_to_all x1, waiting for transfers between devices: 0.01 us -> 2.49 us  [on_device(): lax.all_to_all(wave, 'xy', split_axis=0, concat_axis=0, tiled=True)]
    pallas_call x1, Pallas kernels: 15 us -> 13.3 us  [on_device(): pl.pallas_call(functools.partial(state_kernel, depth=planes * layers, cou...]
  transfers between devices with their start and end apart: 10 -> 10, of which waited for: 3 -> 2; matrix products, arithmetic and copies ran while one was open for 0% -> 0% of each run, Pallas kernels for 59% -> 58%
where the time goes in v6:
time: 102 us; the launch traced here: 101 us
  Pallas kernels  66.7 us (65%)
  starting transfers between devices  25 us (25%)
  waiting for transfers between devices  7.6 us (7%)
  between operations  1.37 us (1%)
    pallas_call x2, Pallas kernels, main(): pl.pallas_call(functools.partial(main_kernel, first=b * 8, inner=inner),...  19.5 us
    pallas_call x1, Pallas kernels, on_device(): pl.pallas_call(density_kernel, in_specs=[hbm, hbm] + [whole] * 7, out_spe...  15 us
    ppermute x8, starting transfers between devices, shift(): return lax.ppermute(block, axis, [(i, (i + step) % n) for i in range(n)])  14.6 us
    pallas_call x1, Pallas kernels, on_device(): pl.pallas_call(functools.partial(state_kernel, depth=planes * layers, cou...  13.3 us
    pallas_call x1, Pallas kernels, on_device(): pl.pallas_call(functools.partial(modes_kernel, turned=turned), in_specs=[...  6.84 us
    pallas_call x1, Pallas kernels, on_device(): pl.pallas_call(halo_kernel, grid=(n,), in_specs=[here(b)] * 2 + [parcel]...  6.18 us
    all_to_all x1, starting transfers between devices, on_device(): lax.all_to_all(mine, ('gz', 'xy'), split_axis=0, concat_axis=0, tiled=True)  5.43 us
    ppermute x8, waiting for transfers between devices, shift(): return lax.ppermute(block, axis, [(i, (i + step) % n) for i in range(n)])  5.11 us
  transfers between devices with their start and end apart: 10, of which 2 were waited for; matrix products, arithmetic and copies ran while one was open for 0% of the time, Pallas kernels for 58%

profile of v6, /device:TPU:0, one launch (start us, length us, event | category | flops | bytes accessed | tf_op | source)
XLA Modules:
  0.0 101.3 jit_solution(13808139603482729274)
XLA Ops:
  1.3 1.8 %first.1 = (s32[32,1,128]{2,1,0:T(1,128)}, f32[8,2,4,512]{3,2,1,0:T(4,128)}, f32[8,2,4,512]{3,2,1,0:T(4,128)}) custom-call(s32[1,3]{1,0:T(1,128)} %cell_ref.1, s32[1]{0:T(128)S(6)} %copy.27.count_ref, f32[2,64,4,512]{3,2,1,0:T(4,128)} %bitcast.18, f32[3,2,64,4,512]{4,3,2,1,0:T(4,128)} %bitcast.7, f32[3,2,64,4,512]{4,3,2,1,0:T(4,128)} %bitcast.13, ...), custom_call_target="tpu_custom_call" | custom-call | flops 1000000 | bytes 100000 | tf_op jit(solution)/shard_map/first/pallas_call | solution.py:572
  3.1 2.9 %collective-permute-start = (f32[8,2,4,512]{3,2,1,0:T(4,128)}, f32[8,2,4,512]{3,2,1,0:T(4,128)S(1)}, u32[]{:S(2)}, u32[]{:S(2)}) collective-permute-start(f32[8,2,4,512]{3,2,1,0:T(4,128)} %get-tuple-element.28), channel_id=1, source_target_pairs={{0,1},{1,2},{2,3},{3,0},{4,5},{5,6},{6,7},{7,4},{8,9},{9,10},{10,1... | collective-permute-start | bytes 393224 | tf_op jit(solution)/shard_map/ppermute | solution.py:543
  6.1 1.0 collective-permute-start.1
  7.0 5.4 %all-to-all-start = ((s32[32,1,128]{2,1,0:T(1,128)}), s32[32,1,128]{2,1,0:T(1,128)S(1)}, u32[]{:S(2)}, u32[]{:S(2)}) async-start(s32[32,1,128]{2,1,0:T(1,128)} %get-tuple-element.27.after_ref), calls=%async_computation | async-start | bytes 32768 | tf_op jit(solution)/shard_map/all_to_all | solution.py:591
  12.5 4.0 %pack.1 = (f32[16,3,8,512]{3,2,1,0:T(8,128)}, f32[16,3,8,512]{3,2,1,0:T(8,128)}) custom-call(f32[2,64,4,512]{3,2,1,0:T(4,128)} %bitcast.20, f32[3,2,64,4,512]{4,3,2,1,0:T(4,128)} %bitcast.9, s32[32,1,128]{2,1,0:T(1,128)} %get-tuple-element.27.after_ref), custom_call_target="tpu_custom_call" | custom-call | flops 1000000 | bytes 100000 | tf_op jit(solution)/shard_map/pack/pallas_call | solution.py:595
  16.5 0.3 collective-permute-start.2
  16.7 3.3 %collective-permute-start.3 = (f32[16,3,8,512]{3,2,1,0:T(8,128)}, f32[16,3,8,512]{3,2,1,0:T(8,128)}, u32[]{:S(2)}, u32[]{:S(2)}) collective-permute-start(f32[16,3,8,512]{3,2,1,0:T(8,128)} %get-tuple-element.33), channel_id=1, source_target_pairs={{0,28},{4,0},{8,4},{12,8},{16,12},{20,16},{24,20},{28,24},{1,29},{... | collective-permute-start | bytes 2359304 | tf_op jit(solution)/shard_map/ppermute | solution.py:543
  20.0 0.0 all-to-all-done.ev_ref
  20.0 0.0 collective-permute-done.before_ref
  20.1 0.0 collective-permute-done.1.after_ref
  20.1 0.0 copy-start.2
  20.1 0.6 copy-done
  20.6 0.1 copy-done.1
  20.7 0.0 copy-done.2
  20.7 13.3 %state.1 = (f32[8,64,8,512]{3,2,1,0:T(8,128)}, f32[8,4,8,512]{3,2,1,0:T(8,128)}, f32[64,8,512]{2,1,0:T(8,128)}, f32[64,8,512]{2,1,0:T(8,128)}, f32[4,20,8,512]{3,2,1,0:T(8,128)}, /*index=5*/f32[4,20,8,512]{3,2,1,0:T(8,128)}) custom-call(s32[32,1,128]{2,1,0:T(1,128)} %copy-done, f32[2,64,4,512]{3,2,1,0:T(4,128)} %bitcast.21, f32[3,2,64,4,512]{4,3,2,1,0:T(4,128)} %bitcast.10, ...), custom_call_target="tpu_custom_call" | custom-call | flops 999999995904 | bytes 4000000000 | tf_op jit(solution)/shard_map/state/pallas_call | solution.py:625
  34.1 0.1 collective-permute-start.6
  34.1 3.5 %collective-permute-start.7 = (f32[4,20,8,512]{3,2,1,0:T(8,128)}, f32[4,20,8,512]{3,2,1,0:T(8,128)}, u32[]{:S(2)}, u32[]{:S(2)}) collective-permute-start(f32[4,20,8,512]{3,2,1,0:T(8,128)} %get-tuple-element.42), channel_id=1, source_target_pairs={{0,28},{4,0},{8,4},{12,8},{16,12},{20,16},{24,20},{28,24},{1,29},{... | collective-permute-start | bytes 3932168 | tf_op jit(solution)/shard_map/ppermute | solution.py:543
  37.7 0.0 collective-permute-done.2.below_ref
  37.7 0.0 collective-permute-done.3.above_ref
  37.7 15.0 %density.1 = (f32[2,64,4,512]{3,2,1,0:T(4,128)}, f32[4,2,4,128,128]{4,3,2,1,0:T(8,128)}, f32[64,8,512]{2,1,0:T(8,128)}, f32[64,8,512]{2,1,0:T(8,128)}, f32[4,20,...) custom-call(f32[8,64,8,512]{3,2,1,0:T(8,128)} %get-tuple-element.30.u_hbm, f32[8,4,8,512]{3,2,1,0:T(8,128)} %get-tuple-element.31.edge_hbm, ...), custom_call_target="tpu_custom_call" | custom-call | flops 999999995904 | bytes 4000000000 | tf_op jit(solution)/shard_map/density/pallas_call | solution.py:647
  52.7 5.0 %all-to-all-start.1 = ((f32[4,2,4,128,128]{4,3,2,1,0:T(8,128)}), f32[4,2,4,128,128]{4,3,2,1,0:T(8,128)}, u32[]{:S(2)}, u32[]{:S(2)}) async-start(f32[4,2,4,128,128]{4,3,2,1,0:T(8,128)} %get-tuple-element.47), calls=%async_computation.1 | async-start | bytes 4194304 | tf_op jit(solution)/shard_map/all_to_all | solution.py:667
  57.6 0.2 collective-permute-start.4
  57.8 3.3 %collective-permute-start.5 = (f32[4,20,8,512]{3,2,1,0:T(8,128)}, f32[4,20,8,512]{3,2,1,0:T(8,128)}, u32[]{:S(2)}, u32[]{:S(2)}) collective-permute-start(f32[4,20,8,512]{3,2,1,0:T(8,128)} %get-tuple-element.40), channel_id=1, source_target_pairs={{0,28},{4,0},{8,4},{12,8},{16,12},{20,16},{24,20},{28,24},{1,29},{... | collective-permute-start | bytes 3932168 | tf_op jit(solution)/shard_map/ppermute | solution.py:543
  61.2 8.4 %inner1.1 = (f32[3,2,64,4,512]{4,3,2,1,0:T(4,128)}, f32[3,2,64,4,512]{4,3,2,1,0:T(4,128)}) custom-call(f32[8,64,8,512]{3,2,1,0:T(8,128)} %get-tuple-element.30.u_hbm, f32[8,4,8,512]{3,2,1,0:T(8,128)} %get-tuple-element.31.edge_hbm, f32[64,8,512]{2,1,0:T(8,128)} %get-tuple-element.37.rho_ref.from_below, f32[64,8,512]{2,1,0:T(8,128)} %get-tuple-element.38.mz_ref.from_above, ...), custom_call_target="tpu_custom_call" | custom-call | flops 999999995904 | bytes 4000000000 | tf_op jit(solution)/shard_map/inner1/pallas_call | solution.py:690
  69.5 0.0 collective-permute-done.6.from_below
  69.6 0.0 collective-permute-done.7.from_above
  69.6 11.1 %main0.1 = (f32[3,2,64,4,512]{4,3,2,1,0:T(4,128)}, f32[3,2,64,4,512]{4,3,2,1,0:T(4,128)}) custom-call(f32[8,64,8,512]{3,2,1,0:T(8,128)} %get-tuple-element.30.u_hbm, f32[8,4,8,512]{3,2,1,0:T(8,128)} %get-tuple-element.31.edge_hbm, f32[64,8,512]{2,1,0:T(8,128)} %get-tuple-element.37.rho_ref.from_below, ...), custom_call_target="tpu_custom_call", output_to_operand_aliasing={{0}: (6, {}), {1}: (7, {})} | custom-call | flops 999999995904 | bytes 4000000000 | tf_op jit(solution)/shard_map/main0/pallas_call | solution.py:690
  80.7 2.5 %all-to-all-done.1.w_ref = f32[4,2,4,128,128]{4,3,2,1,0:T(8,128)} async-done(((f32[4,2,4,128,128]{4,3,2,1,0:T(8,128)}), f32[4,2,4,128,128]{4,3,2,1,0:T(8,128)}, u32[]{:S(2)}, u32[]{:S(2)}) %all-to-all-start.1) | async-done | bytes 2097184 | tf_op jit(solution)/shard_map/all_to_all | solution.py:667
  83.1 6.8 %modes.1.rest_0_ = f32[2,4,128,512]{3,2,1,0:T(8,128)} custom-call(f32[4,2,4,128,128]{4,3,2,1,0:T(8,128)} %all-to-all-done.1.w_ref, bf16[512,512]{1,0:T(8,128)(2,1)} %constant.21.clone.ch_ref, bf16[512,512]{1,0:T(8,128)(2,1)} %constant.22.clone.cl_ref, bf16[512,512]{1,0:T(8,128)(2,1)} %constant.23.clone.mh_ref, bf16[512,512]{1,0:T(8,128)(2,1)} %constant.24.clone.ml_ref, ...), custom_call_target="tpu_custom_call" | custom-call | flops 1000000 | bytes 100000 | tf_op jit(solution)/shard_map/modes/pallas_call | solution.py:670
  90.0 5.1 %collective-permute-done.4.from_below = f32[4,20,8,512]{3,2,1,0:T(8,128)} collective-permute-done((f32[4,20,8,512]{3,2,1,0:T(8,128)}, f32[4,20,8,512]{3,2,1,0:T(8,128)}, u32[]{:S(2)}, u32[]{:S(2)}) %collective-permute-start.4) | collective-permute-done | bytes 1310752 | tf_op jit(solution)/shard_map/ppermute | solution.py:543
  95.1 0.0 collective-permute-done.5.from_above
  95.1 6.2 %halo1.1 = (f32[3,2,64,4,512]{4,3,2,1,0:T(4,128)}, f32[3,2,64,4,512]{4,3,2,1,0:T(4,128)}) custom-call(f32[64,8,512]{2,1,0:T(8,128)} %get-tuple-element.37.rho_ref.from_below, f32[64,8,512]{2,1,0:T(8,128)} %get-tuple-element.38.mz_ref.from_above, f32[4,20,8,512]{3,2,1,0:T(8,128)} %collective-permute-done.4.from_below, ...), custom_call_target="tpu_custom_call", output_to_operand_aliasing={{0}: (4, {}), {1}: (5, {})} | custom-call | flops 999999995904 | bytes 4000000000 | tf_op jit(solution)/shard_map/halo1/pallas_call | solution.py:711
  (2 shorter events, 0.0 us)
Async XLA Ops:
  3.1 16.9 %collective-permute-start = (f32[8,2,4,512]{3,2,1,0:T(4,128)}, f32[8,2,4,512]{3,2,1,0:T(4,128)S(1)}, u32[]{:S(2)}, u32[]{:S(2)}) collective-permute-start(f32[8,2,4,512]{3,2,1,0:T(4,128)} %get-tuple-element.28), channel_id=1, source_target_pairs={{0,1},{1,2},{2,3},{3,0},{4,5},{5,6},{6,7},{7,4},{8,9},{9,10},{10,1... | collective-permute-start | bytes 393224 | tf_op jit(solution)/shard_map/ppermute | solution.py:543
  6.1 14.0 %collective-permute-start.1 = (f32[8,2,4,512]{3,2,1,0:T(4,128)}, f32[8,2,4,512]{3,2,1,0:T(4,128)S(1)}, u32[]{:S(2)}, u32[]{:S(2)}) collective-permute-start(f32[8,2,4,512]{3,2,1,0:T(4,128)} %get-tuple-element.29), channel_id=1, source_target_pairs={{0,3},{1,0},{2,1},{3,2},{4,7},{5,4},{6,5},{7,6},{8,11},{9,8},{10,9... | collective-permute-start | bytes 393224 | tf_op jit(solution)/shard_map/ppermute | solution.py:543
  7.0 13.0 %all-to-all-start = ((s32[32,1,128]{2,1,0:T(1,128)}), s32[32,1,128]{2,1,0:T(1,128)S(1)}, u32[]{:S(2)}, u32[]{:S(2)}) async-start(s32[32,1,128]{2,1,0:T(1,128)} %get-tuple-element.27.after_ref), calls=%async_computation | async-start | bytes 32768 | tf_op jit(solution)/shard_map/all_to_all | solution.py:591
  16.5 21.2 %collective-permute-start.2 = (f32[16,3,8,512]{3,2,1,0:T(8,128)}, f32[16,3,8,512]{3,2,1,0:T(8,128)}, u32[]{:S(2)}, u32[]{:S(2)}) collective-permute-start(f32[16,3,8,512]{3,2,1,0:T(8,128)} %get-tuple-element.32), channel_id=1, source_target_pairs={{0,4},{4,8},{8,12},{12,16},{16,20},{20,24},{24,28},{28,0},{1,5},{5... | collective-permute-start | bytes 2359304 | tf_op jit(solution)/shard_map/ppermute | solution.py:543
  16.7 20.9 %collective-permute-start.3 = (f32[16,3,8,512]{3,2,1,0:T(8,128)}, f32[16,3,8,512]{3,2,1,0:T(8,128)}, u32[]{:S(2)}, u32[]{:S(2)}) collective-permute-start(f32[16,3,8,512]{3,2,1,0:T(8,128)} %get-tuple-element.33), channel_id=1, source_target_pairs={{0,28},{4,0},{8,4},{12,8},{16,12},{20,16},{24,20},{28,24},{1,29},{... | collective-permute-start | bytes 2359304 | tf_op jit(solution)/shard_map/ppermute | solution.py:543
  20.0 0.6 copy-start
  20.0 0.7 copy-start.1
  20.1 0.7 copy-start.2
  34.1 35.5 %collective-permute-start.6 = (f32[4,20,8,512]{3,2,1,0:T(8,128)}, f32[4,20,8,512]{3,2,1,0:T(8,128)}, u32[]{:S(2)}, u32[]{:S(2)}) collective-permute-start(f32[4,20,8,512]{3,2,1,0:T(8,128)} %get-tuple-element.41), channel_id=1, source_target_pairs={{0,4},{4,8},{8,12},{12,16},{16,20},{20,24},{24,28},{28,0},{1,5},{5... | collective-permute-start | bytes 3932168 | tf_op jit(solution)/shard_map/ppermute | solution.py:543
  34.1 35.4 %collective-permute-start.7 = (f32[4,20,8,512]{3,2,1,0:T(8,128)}, f32[4,20,8,512]{3,2,1,0:T(8,128)}, u32[]{:S(2)}, u32[]{:S(2)}) collective-permute-start(f32[4,20,8,512]{3,2,1,0:T(8,128)} %get-tuple-element.42), channel_id=1, source_target_pairs={{0,28},{4,0},{8,4},{12,8},{16,12},{20,16},{24,20},{28,24},{1,29},{... | collective-permute-start | bytes 3932168 | tf_op jit(solution)/shard_map/ppermute | solution.py:543
  52.7 30.5 %all-to-all-start.1 = ((f32[4,2,4,128,128]{4,3,2,1,0:T(8,128)}), f32[4,2,4,128,128]{4,3,2,1,0:T(8,128)}, u32[]{:S(2)}, u32[]{:S(2)}) async-start(f32[4,2,4,128,128]{4,3,2,1,0:T(8,128)} %get-tuple-element.47), calls=%async_computation.1 | async-start | bytes 4194304 | tf_op jit(solution)/shard_map/all_to_all | solution.py:667
  57.6 37.5 %collective-permute-start.4 = (f32[4,20,8,512]{3,2,1,0:T(8,128)}, f32[4,20,8,512]{3,2,1,0:T(8,128)}, u32[]{:S(2)}, u32[]{:S(2)}) collective-permute-start(f32[4,20,8,512]{3,2,1,0:T(8,128)} %get-tuple-element.39), channel_id=1, source_target_pairs={{0,4},{4,8},{8,12},{12,16},{16,20},{20,24},{24,28},{28,0},{1,5},{5... | collective-permute-start | bytes 3932168 | tf_op jit(solution)/shard_map/ppermute | solution.py:543
  57.8 37.3 %collective-permute-start.5 = (f32[4,20,8,512]{3,2,1,0:T(8,128)}, f32[4,20,8,512]{3,2,1,0:T(8,128)}, u32[]{:S(2)}, u32[]{:S(2)}) collective-permute-start(f32[4,20,8,512]{3,2,1,0:T(8,128)} %get-tuple-element.40), channel_id=1, source_target_pairs={{0,28},{4,0},{8,4},{12,8},{16,12},{20,16},{24,20},{28,24},{1,29},{... | collective-permute-start | bytes 3932168 | tf_op jit(solution)/shard_map/ppermute | solution.py:543

commit v7 on v5

--- a/solution.py
+++ b/solution.py
@@ -17,7 +17,7 @@
 DIFFUSION = 0.05
 NEAR = 8.0 * TIME_STEP / 12.0
 FAR = TIME_STEP / 12.0
-VMEM = 56 * 1024 * 1024
+VMEM = 62 * 1024 * 1024
 PACK_COST = MODES_COST = (1e6, 1e5)
 STATE_COST = DENSITY_COST = (1e12, 4e9)
 MAIN_COST = (1e12, 4e9)
@@ -591,7 +591,7 @@
     events = lax.all_to_all(mine, ("gz", "xy"), split_axis=0, concat_axis=0, tiled=True)
     before, after = shift(last_rows, "xy", 1), shift(first_rows, "xy", -1)
 
-    some = math.gcd(half, 16)
+    some = math.gcd(half, 32)
     up, down = pl.pallas_call(
         pack_kernel,
         grid=(half // some,),

time: 103 us -> 102 us (level)
  Pallas kernels: 67.4 us -> 66.2 us
    pallas_call x1, Pallas kernels: 4.03 us -> 2.99 us  [on_device(): pl.pallas_call(pack_kernel, grid=(half // some,), in_specs=[pl.BlockSpec(...]
  transfers between devices with their start and end apart: 10 -> 10, of which waited for: 3 -> 3; matrix products, arithmetic and copies ran while one was open for 0% -> 0% of each run, Pallas kernels for 59% -> 58%
where the time goes in v7:
time: 102 us
  Pallas kernels  66.2 us (65%)
  starting transfers between devices  24.6 us (24%)
  waiting for transfers between devices  8.92 us (9%)
  between operations  1.37 us (1%)
    pallas_call x2, Pallas kernels, main(): pl.pallas_call(functools.partial(main_kernel, first=b * 8, inner=inner),...  19.8 us
    pallas_call x1, Pallas kernels, on_device(): pl.pallas_call(functools.partial(state_kernel, depth=planes * layers, cou...  14.8 us
    ppermute x8, starting transfers between devices, shift(): return lax.ppermute(block, axis, [(i, (i + step) % n) for i in range(n)])  14.6 us
    pallas_call x1, Pallas kernels, on_device(): pl.pallas_call(density_kernel, in_specs=[hbm, hbm] + [whole] * 7, out_spe...  14.3 us
    ppermute x8, waiting for transfers between devices, shift(): return lax.ppermute(block, axis, [(i, (i + step) % n) for i in range(n)])  8.27 us
    pallas_call x1, Pallas kernels, on_device(): pl.pallas_call(functools.partial(modes_kernel, turned=turned), in_specs=[...  6.84 us
    pallas_call x1, Pallas kernels, on_device(): pl.pallas_call(halo_kernel, grid=(n,), in_specs=[here(b)] * 2 + [parcel]...  5.54 us
    all_to_all x1, starting transfers between devices, on_device(): lax.all_to_all(mine, ('gz', 'xy'), split_axis=0, concat_axis=0, tiled=True)  5.43 us
  transfers between devices with their start and end apart: 10, of which 3 were waited for; matrix products, arithmetic and copies ran while one was open for 0% of the time, Pallas kernels for 58%

profile of v7, /device:TPU:0, one launch (start us, length us, event | category | flops | bytes accessed | tf_op | source)
XLA Modules:
  0.0 101.7 jit_solution(1705826198683622672)
XLA Ops:
  1.3 1.8 %first.1 = (s32[32,1,128]{2,1,0:T(1,128)}, f32[8,2,4,512]{3,2,1,0:T(4,128)}, f32[8,2,4,512]{3,2,1,0:T(4,128)}) custom-call(s32[1,3]{1,0:T(1,128)} %cell_ref.1, s32[1]{0:T(128)S(6)} %copy.27.count_ref, f32[2,64,4,512]{3,2,1,0:T(4,128)} %bitcast.18, f32[3,2,64,4,512]{4,3,2,1,0:T(4,128)} %bitcast.7, f32[3,2,64,4,512]{4,3,2,1,0:T(4,128)} %bitcast.13, ...), custom_call_target="tpu_custom_call" | custom-call | flops 1000000 | bytes 100000 | tf_op jit(solution)/shard_map/first/pallas_call | solution.py:572
  3.1 2.9 %collective-permute-start = (f32[8,2,4,512]{3,2,1,0:T(4,128)}, f32[8,2,4,512]{3,2,1,0:T(4,128)S(1)}, u32[]{:S(2)}, u32[]{:S(2)}) collective-permute-start(f32[8,2,4,512]{3,2,1,0:T(4,128)} %get-tuple-element.28), channel_id=1, source_target_pairs={{0,1},{1,2},{2,3},{3,0},{4,5},{5,6},{6,7},{7,4},{8,9},{9,10},{10,1... | collective-permute-start | bytes 393224 | tf_op jit(solution)/shard_map/ppermute | solution.py:543
  6.1 1.0 collective-permute-start.1
  7.0 5.4 %all-to-all-start = ((s32[32,1,128]{2,1,0:T(1,128)}), s32[32,1,128]{2,1,0:T(1,128)S(1)}, u32[]{:S(2)}, u32[]{:S(2)}) async-start(s32[32,1,128]{2,1,0:T(1,128)} %get-tuple-element.27.after_ref), calls=%async_computation | async-start | bytes 32768 | tf_op jit(solution)/shard_map/all_to_all | solution.py:591
  12.5 3.0 %pack.1 = (f32[16,3,8,512]{3,2,1,0:T(8,128)}, f32[16,3,8,512]{3,2,1,0:T(8,128)}) custom-call(f32[2,64,4,512]{3,2,1,0:T(4,128)} %bitcast.20, f32[3,2,64,4,512]{4,3,2,1,0:T(4,128)} %bitcast.9, s32[32,1,128]{2,1,0:T(1,128)} %get-tuple-element.27.after_ref), custom_call_target="tpu_custom_call" | custom-call | flops 1000000 | bytes 100000 | tf_op jit(solution)/shard_map/pack/pallas_call | solution.py:595
  15.4 0.3 collective-permute-start.2
  15.7 3.3 %collective-permute-start.3 = (f32[16,3,8,512]{3,2,1,0:T(8,128)}, f32[16,3,8,512]{3,2,1,0:T(8,128)}, u32[]{:S(2)}, u32[]{:S(2)}) collective-permute-start(f32[16,3,8,512]{3,2,1,0:T(8,128)} %get-tuple-element.33), channel_id=1, source_target_pairs={{0,28},{4,0},{8,4},{12,8},{16,12},{20,16},{24,20},{28,24},{1,29},{... | collective-permute-start | bytes 2359304 | tf_op jit(solution)/shard_map/ppermute | solution.py:543
  19.0 0.6 all-to-all-done.ev_ref
  19.6 0.0 collective-permute-done.before_ref
  19.6 0.0 collective-permute-done.1.after_ref
  19.6 0.0 copy-start.2
  19.7 0.6 copy-done
  20.2 0.1 copy-done.1
  20.3 0.0 copy-done.2
  20.3 14.8 %state.1 = (f32[8,64,8,512]{3,2,1,0:T(8,128)}, f32[8,4,8,512]{3,2,1,0:T(8,128)}, f32[64,8,512]{2,1,0:T(8,128)}, f32[64,8,512]{2,1,0:T(8,128)}, f32[5,20,8,512]{3,2,1,0:T(8,128)}, /*index=5*/f32[5,20,8,512]{3,2,1,0:T(8,128)}) custom-call(s32[32,1,128]{2,1,0:T(1,128)} %copy-done, f32[2,64,4,512]{3,2,1,0:T(4,128)} %bitcast.21, f32[3,2,64,4,512]{4,3,2,1,0:T(4,128)} %bitcast.10, ...), custom_call_target="tpu_custom_call" | custom-call | flops 999999995904 | bytes 4000000000 | tf_op jit(solution)/shard_map/state/pallas_call | solution.py:625
  35.2 0.1 collective-permute-start.6
  35.2 3.5 %collective-permute-start.7 = (f32[5,20,8,512]{3,2,1,0:T(8,128)}, f32[5,20,8,512]{3,2,1,0:T(8,128)}, u32[]{:S(2)}, u32[]{:S(2)}) collective-permute-start(f32[5,20,8,512]{3,2,1,0:T(8,128)} %get-tuple-element.42), channel_id=1, source_target_pairs={{0,28},{4,0},{8,4},{12,8},{16,12},{20,16},{24,20},{28,24},{1,29},{... | collective-permute-start | bytes 4915208 | tf_op jit(solution)/shard_map/ppermute | solution.py:543
  38.8 0.0 collective-permute-done.2.below_ref
  38.8 0.0 collective-permute-done.3.above_ref
  38.8 14.3 %density.1 = (f32[2,64,4,512]{3,2,1,0:T(4,128)}, f32[4,2,4,128,128]{4,3,2,1,0:T(8,128)}, f32[64,8,512]{2,1,0:T(8,128)}, f32[64,8,512]{2,1,0:T(8,128)}, f32[3,20,...) custom-call(f32[8,64,8,512]{3,2,1,0:T(8,128)} %get-tuple-element.30.u_hbm, f32[8,4,8,512]{3,2,1,0:T(8,128)} %get-tuple-element.31.edge_hbm, ...), custom_call_target="tpu_custom_call" | custom-call | flops 999999995904 | bytes 4000000000 | tf_op jit(solution)/shard_map/density/pallas_call | solution.py:647
  53.1 4.5 %all-to-all-start.1 = ((f32[4,2,4,128,128]{4,3,2,1,0:T(8,128)}), f32[4,2,4,128,128]{4,3,2,1,0:T(8,128)}, u32[]{:S(2)}, u32[]{:S(2)}) async-start(f32[4,2,4,128,128]{4,3,2,1,0:T(8,128)} %get-tuple-element.47), calls=%async_computation.1 | async-start | bytes 4194304 | tf_op jit(solution)/shard_map/all_to_all | solution.py:667
  57.6 0.1 collective-permute-start.4
  57.7 3.5 %collective-permute-start.5 = (f32[3,20,8,512]{3,2,1,0:T(8,128)}, f32[3,20,8,512]{3,2,1,0:T(8,128)}, u32[]{:S(2)}, u32[]{:S(2)}) collective-permute-start(f32[3,20,8,512]{3,2,1,0:T(8,128)} %get-tuple-element.40), channel_id=1, source_target_pairs={{0,28},{4,0},{8,4},{12,8},{16,12},{20,16},{24,20},{28,24},{1,29},{... | collective-permute-start | bytes 2949128 | tf_op jit(solution)/shard_map/ppermute | solution.py:543
  61.2 6.9 %inner1.1 = (f32[3,2,64,4,512]{4,3,2,1,0:T(4,128)}, f32[3,2,64,4,512]{4,3,2,1,0:T(4,128)}) custom-call(f32[8,64,8,512]{3,2,1,0:T(8,128)} %get-tuple-element.30.u_hbm, f32[8,4,8,512]{3,2,1,0:T(8,128)} %get-tuple-element.31.edge_hbm, f32[64,8,512]{2,1,0:T(8,128)} %get-tuple-element.37.rho_ref.from_below, f32[64,8,512]{2,1,0:T(8,128)} %get-tuple-element.38.mz_ref.from_above, ...), custom_call_target="tpu_custom_call" | custom-call | flops 999999995904 | bytes 4000000000 | tf_op jit(solution)/shard_map/inner1/pallas_call | solution.py:690
  68.1 7.3 %collective-permute-done.6.from_below = f32[5,20,8,512]{3,2,1,0:T(8,128)} collective-permute-done((f32[5,20,8,512]{3,2,1,0:T(8,128)}, f32[5,20,8,512]{3,2,1,0:T(8,128)}, u32[]{:S(2)}, u32[]{:S(2)}) %collective-permute-start.6) | collective-permute-done | bytes 1638432 | tf_op jit(solution)/shard_map/ppermute | solution.py:543
  75.4 0.0 collective-permute-done.7.from_above
  75.4 13.0 %main0.1 = (f32[3,2,64,4,512]{4,3,2,1,0:T(4,128)}, f32[3,2,64,4,512]{4,3,2,1,0:T(4,128)}) custom-call(f32[8,64,8,512]{3,2,1,0:T(8,128)} %get-tuple-element.30.u_hbm, f32[8,4,8,512]{3,2,1,0:T(8,128)} %get-tuple-element.31.edge_hbm, f32[64,8,512]{2,1,0:T(8,128)} %get-tuple-element.37.rho_ref.from_below, ...), custom_call_target="tpu_custom_call", output_to_operand_aliasing={{0}: (6, {}), {1}: (7, {})} | custom-call | flops 999999995904 | bytes 4000000000 | tf_op jit(solution)/shard_map/main0/pallas_call | solution.py:690
  88.4 0.0 all-to-all-done.1.w_ref
  88.4 6.8 %modes.1.rest_0_ = f32[2,4,128,512]{3,2,1,0:T(8,128)} custom-call(f32[4,2,4,128,128]{4,3,2,1,0:T(8,128)} %all-to-all-done.1.w_ref, bf16[512,512]{1,0:T(8,128)(2,1)} %constant.21.clone.ch_ref, bf16[512,512]{1,0:T(8,128)(2,1)} %constant.22.clone.cl_ref, bf16[512,512]{1,0:T(8,128)(2,1)} %constant.23.clone.mh_ref, bf16[512,512]{1,0:T(8,128)(2,1)} %constant.24.clone.ml_ref, ...), custom_call_target="tpu_custom_call" | custom-call | flops 1000000 | bytes 100000 | tf_op jit(solution)/shard_map/modes/pallas_call | solution.py:670
  95.3 0.9 collective-permute-done.4.from_below
  96.2 0.0 collective-permute-done.5.from_above
  96.2 5.5 %halo1.1 = (f32[3,2,64,4,512]{4,3,2,1,0:T(4,128)}, f32[3,2,64,4,512]{4,3,2,1,0:T(4,128)}) custom-call(f32[64,8,512]{2,1,0:T(8,128)} %get-tuple-element.37.rho_ref.from_below, f32[64,8,512]{2,1,0:T(8,128)} %get-tuple-element.38.mz_ref.from_above, f32[3,20,8,512]{3,2,1,0:T(8,128)} %collective-permute-done.4.from_below, ...), custom_call_target="tpu_custom_call", output_to_operand_aliasing={{0}: (4, {}), {1}: (5, {})} | custom-call | flops 999999995904 | bytes 4000000000 | tf_op jit(solution)/shard_map/halo1/pallas_call | solution.py:711
  (2 shorter events, 0.0 us)
Async XLA Ops:
  3.1 16.5 %collective-permute-start = (f32[8,2,4,512]{3,2,1,0:T(4,128)}, f32[8,2,4,512]{3,2,1,0:T(4,128)S(1)}, u32[]{:S(2)}, u32[]{:S(2)}) collective-permute-start(f32[8,2,4,512]{3,2,1,0:T(4,128)} %get-tuple-element.28), channel_id=1, source_target_pairs={{0,1},{1,2},{2,3},{3,0},{4,5},{5,6},{6,7},{7,4},{8,9},{9,10},{10,1... | collective-permute-start | bytes 393224 | tf_op jit(solution)/shard_map/ppermute | solution.py:543
  6.1 13.6 %collective-permute-start.1 = (f32[8,2,4,512]{3,2,1,0:T(4,128)}, f32[8,2,4,512]{3,2,1,0:T(4,128)S(1)}, u32[]{:S(2)}, u32[]{:S(2)}) collective-permute-start(f32[8,2,4,512]{3,2,1,0:T(4,128)} %get-tuple-element.29), channel_id=1, source_target_pairs={{0,3},{1,0},{2,1},{3,2},{4,7},{5,4},{6,5},{7,6},{8,11},{9,8},{10,9... | collective-permute-start | bytes 393224 | tf_op jit(solution)/shard_map/ppermute | solution.py:543
  7.0 12.6 %all-to-all-start = ((s32[32,1,128]{2,1,0:T(1,128)}), s32[32,1,128]{2,1,0:T(1,128)S(1)}, u32[]{:S(2)}, u32[]{:S(2)}) async-start(s32[32,1,128]{2,1,0:T(1,128)} %get-tuple-element.27.after_ref), calls=%async_computation | async-start | bytes 32768 | tf_op jit(solution)/shard_map/all_to_all | solution.py:591
  15.4 23.3 %collective-permute-start.2 = (f32[16,3,8,512]{3,2,1,0:T(8,128)}, f32[16,3,8,512]{3,2,1,0:T(8,128)}, u32[]{:S(2)}, u32[]{:S(2)}) collective-permute-start(f32[16,3,8,512]{3,2,1,0:T(8,128)} %get-tuple-element.32), channel_id=1, source_target_pairs={{0,4},{4,8},{8,12},{12,16},{16,20},{20,24},{24,28},{28,0},{1,5},{5... | collective-permute-start | bytes 2359304 | tf_op jit(solution)/shard_map/ppermute | solution.py:543
  15.7 23.1 %collective-permute-start.3 = (f32[16,3,8,512]{3,2,1,0:T(8,128)}, f32[16,3,8,512]{3,2,1,0:T(8,128)}, u32[]{:S(2)}, u32[]{:S(2)}) collective-permute-start(f32[16,3,8,512]{3,2,1,0:T(8,128)} %get-tuple-element.33), channel_id=1, source_target_pairs={{0,28},{4,0},{8,4},{12,8},{16,12},{20,16},{24,20},{28,24},{1,29},{... | collective-permute-start | bytes 2359304 | tf_op jit(solution)/shard_map/ppermute | solution.py:543
  19.6 0.6 copy-start
  19.6 0.7 copy-start.1
  19.6 0.7 copy-start.2
  35.2 40.3 %collective-permute-start.6 = (f32[5,20,8,512]{3,2,1,0:T(8,128)}, f32[5,20,8,512]{3,2,1,0:T(8,128)}, u32[]{:S(2)}, u32[]{:S(2)}) collective-permute-start(f32[5,20,8,512]{3,2,1,0:T(8,128)} %get-tuple-element.41), channel_id=1, source_target_pairs={{0,4},{4,8},{8,12},{12,16},{16,20},{20,24},{24,28},{28,0},{1,5},{5... | collective-permute-start | bytes 4915208 | tf_op jit(solution)/shard_map/ppermute | solution.py:543
  35.2 40.2 %collective-permute-start.7 = (f32[5,20,8,512]{3,2,1,0:T(8,128)}, f32[5,20,8,512]{3,2,1,0:T(8,128)}, u32[]{:S(2)}, u32[]{:S(2)}) collective-permute-start(f32[5,20,8,512]{3,2,1,0:T(8,128)} %get-tuple-element.42), channel_id=1, source_target_pairs={{0,28},{4,0},{8,4},{12,8},{16,12},{20,16},{24,20},{28,24},{1,29},{... | collective-permute-start | bytes 4915208 | tf_op jit(solution)/shard_map/ppermute | solution.py:543
  53.1 35.3 %all-to-all-start.1 = ((f32[4,2,4,128,128]{4,3,2,1,0:T(8,128)}), f32[4,2,4,128,128]{4,3,2,1,0:T(8,128)}, u32[]{:S(2)}, u32[]{:S(2)}) async-start(f32[4,2,4,128,128]{4,3,2,1,0:T(8,128)} %get-tuple-element.47), calls=%async_computation.1 | async-start | bytes 4194304 | tf_op jit(solution)/shard_map/all_to_all | solution.py:667
  57.6 38.5 %collective-permute-start.4 = (f32[3,20,8,512]{3,2,1,0:T(8,128)}, f32[3,20,8,512]{3,2,1,0:T(8,128)}, u32[]{:S(2)}, u32[]{:S(2)}) collective-permute-start(f32[3,20,8,512]{3,2,1,0:T(8,128)} %get-tuple-element.39), channel_id=1, source_target_pairs={{0,4},{4,8},{8,12},{12,16},{16,20},{20,24},{24,28},{28,0},{1,5},{5... | collective-permute-start | bytes 2949128 | tf_op jit(solution)/shard_map/ppermute | solution.py:543
  57.7 38.5 %collective-permute-start.5 = (f32[3,20,8,512]{3,2,1,0:T(8,128)}, f32[3,20,8,512]{3,2,1,0:T(8,128)}, u32[]{:S(2)}, u32[]{:S(2)}) collective-permute-start(f32[3,20,8,512]{3,2,1,0:T(8,128)} %get-tuple-element.40), channel_id=1, source_target_pairs={{0,28},{4,0},{8,4},{12,8},{16,12},{20,16},{24,20},{28,24},{1,29},{... | collective-permute-start | bytes 2949128 | tf_op jit(solution)/shard_map/ppermute | solution.py:543
